TPU v7x, 32 devices: a whole 2x2x4 slice. The times are simulated.
32 devices in a mesh: dp: 8 (over y, x, core), tensor: 4 (over z).
Axes of the slice: x: 2, y: 2, z: 4, core: 2. Of those that a mesh axis runs over, the one named last changes fastest.
Arguments:
- tokens_in: bfloat16 [16, 1028, 1024], P('dp', 'tensor'), may hold values from -6 to 6
- cotangent: bfloat16 [16, 1028, 1024], P('dp', 'tensor'), may hold values from -6 to 6
- image_flag: int32 [16], P('dp'), may hold values from 0 to 1, as said below
- key_mask: int32 [16, 1028], P('dp'), may hold values from 0 to 1, as said below
- column_mask: int32 [2736], P('tensor'), may hold values from 0 to 1, as said below
- attention_norm_gain: float32 [1024], replicated, may hold values from 0.5 to 1.5
- attention_norm_bias: float32 [1024], replicated, may hold values from -2 to 2
- w_query: bfloat16 [1024, 1024], P('dp', 'tensor'), may hold values from -0.1875 to 0.1875
- w_key: bfloat16 [1024, 1024], P('dp', 'tensor'), may hold values from -0.1875 to 0.1875
- w_value: bfloat16 [1024, 1024], P('dp', 'tensor'), may hold values from -0.1875 to 0.1875
- query_bias: float32 [1024], P('tensor'), may hold values from -2 to 2
- value_bias: float32 [1024], P('tensor'), may hold values from -2 to 2
- w_out: bfloat16 [1024, 1024], P('tensor', 'dp'), may hold values from -3 to 3
- out_bias: float32 [1024], replicated, may hold values from -2 to 2
- feedforward_norm_gain: float32 [1024], replicated, may hold values from 0.5 to 1.5
- feedforward_norm_bias: float32 [1024], replicated, may hold values from -2 to 2
- w_gate: bfloat16 [1024, 2736], P('dp', 'tensor'), may hold values from -0.1875 to 0.1875
- gate_bias: float32 [2736], P('tensor'), may hold values from -2 to 2
- w_up: bfloat16 [1024, 2736], P('dp', 'tensor'), may hold values from -0.1875 to 0.1875
- up_bias: float32 [2736], P('tensor'), may hold values from -2 to 2
- inner_gain: float32 [2736], P('tensor'), may hold values from 0.5 to 1.5
- inner_shift: float32 [2736], P('tensor'), may hold values from -2 to 2
- w_down: bfloat16 [2736, 1024], P('tensor', 'dp'), may hold values from -0.109375 to 0.109375
- down_bias: float32 [1024], replicated, may hold values from -2 to 2
Outputs:
- output: bfloat16 [16, 1028, 1024], P('dp', 'tensor')
- input_grad: float32 [16, 1028, 1024], P('dp', 'tensor')
- attn_gain_grad: float32 [1024], replicated
- attn_shift_grad: float32 [1024], replicated
- w_query_grad: float32 [1024, 1024], P('dp', 'tensor')
- w_key_grad: float32 [1024, 1024], P('dp', 'tensor')
- w_value_grad: float32 [1024, 1024], P('dp', 'tensor')
- query_bias_grad: float32 [1024], P('tensor')
- value_bias_grad: float32 [1024], P('tensor')
- w_out_grad: float32 [1024, 1024], P('tensor', 'dp')
- out_bias_grad: float32 [1024], replicated
- mlp_gain_grad: float32 [1024], replicated
- mlp_shift_grad: float32 [1024], replicated
- w_gate_grad: float32 [1024, 2736], P('dp', 'tensor')
- gate_bias_grad: float32 [2736], P('tensor')
- w_up_grad: float32 [1024, 2736], P('dp', 'tensor')
- up_bias_grad: float32 [2736], P('tensor')
- inner_gain_grad: float32 [2736], P('tensor')
- inner_shift_grad: float32 [2736], P('tensor')
- w_down_grad: float32 [2736, 1024], P('tensor', 'dp')
- down_bias_grad: float32 [1024], replicated
Inputs may be any that keep to these rules, and one draw needn't show every extreme that they name: `image_flag`: exactly one image has flag 0. `key_mask`: each image has exactly 3 zeros. `column_mask`: exactly 6 zeros.
All inputs are finite; a program needn't handle non-finite values.
Results may differ from a plain program's by a relative error of at most 0.03.
Values may be sent and summed in bfloat16 or wider, within the bound.
A program may use at most 256 MiB of HBM per device.

v0:
```python
import jax
import jax.numpy as jnp
from jax import lax
from jax.sharding import PartitionSpec as P

HEAD = 64
FF = 2736
PADCOLS = 6
GRID = 32


EPS = 1e-06
ROPE_BASE = 10000.0


def rotary_tables(length, head):
    quarter = head // 4
    place = jnp.arange(length, dtype=jnp.int32)
    inside = (place >= 1) & (place <= GRID * GRID)
    cell = jnp.maximum(place - 1, 0)
    row_pos = jnp.where(inside, cell // GRID, 0).astype(jnp.float32)
    col_pos = jnp.where(inside, cell % GRID, 0).astype(jnp.float32)
    freq = ROPE_BASE ** (-jnp.arange(quarter, dtype=jnp.float32) / quarter)
    angle = jnp.concatenate(
        [row_pos[:, None] * freq[None, :], col_pos[:, None] * freq[None, :]], axis=1
    )
    return (jnp.cos(angle)[:, None, :], jnp.sin(angle)[:, None, :])


def rotate(values, cosv, sinv):
    quarter = values.shape[-1] // 4
    first = jnp.concatenate(
        [values[..., :quarter], values[..., 2 * quarter : 3 * quarter]], axis=-1
    )
    second = jnp.concatenate(
        [values[..., quarter : 2 * quarter], values[..., 3 * quarter :]], axis=-1
    )
    new_first = first * cosv - second * sinv
    new_second = second * cosv + first * sinv
    return jnp.concatenate(
        [
            new_first[..., :quarter],
            new_second[..., :quarter],
            new_first[..., quarter:],
            new_second[..., quarter:],
        ],
        axis=-1,
    )


def norm_pieces(values):
    row_mean = jnp.mean(values, axis=-1, keepdims=True)
    var = jnp.mean(jnp.square(values - row_mean), axis=-1, keepdims=True)
    inverse_scale = lax.rsqrt(var + EPS)
    return ((values - row_mean) * inverse_scale, inverse_scale)


def norm_backward(incoming_gradient, centered_normalized, inverse_scale, norm_gain):
    inner_activation = incoming_gradient * norm_gain
    return inverse_scale * (
        inner_activation
        - jnp.mean(inner_activation, axis=-1, keepdims=True)
        - centered_normalized
        * jnp.mean(inner_activation * centered_normalized, axis=-1, keepdims=True)
    )


def matmul(left, right):
    return jnp.dot(left, right, preferred_element_type=jnp.float32)


def matmul_right_t(left, right):
    return lax.dot_general(
        left, right, (((1,), (1,)), ((), ())), preferred_element_type=jnp.float32
    )


def matmul_left_t(left, right):
    return lax.dot_general(
        left, right, (((0,), (0,)), ((), ())), preferred_element_type=jnp.float32
    )


def fetch_weights(w_query, w_key, w_value, w_out, w_gate, w_up, w_down):
    return (
        lax.all_gather(w_query, "dp", axis=0, tiled=True),
        lax.all_gather(w_key, "dp", axis=0, tiled=True),
        lax.all_gather(w_value, "dp", axis=0, tiled=True),
        lax.all_gather(w_out, "dp", axis=1, tiled=True),
        lax.all_gather(w_gate, "dp", axis=0, tiled=True),
        lax.all_gather(w_up, "dp", axis=0, tiled=True),
        lax.all_gather(w_down, "dp", axis=1, tiled=True),
    )


def shards(
    tokens_in,
    cotangent,
    image_flag,
    key_mask,
    column_mask,
    attention_norm_gain,
    attention_norm_bias,
    w_query,
    w_key,
    w_value,
    query_bias,
    value_bias,
    w_out,
    out_bias,
    feedforward_norm_gain,
    feedforward_norm_bias,
    w_gate,
    gate_bias,
    w_up,
    up_bias,
    inner_gain,
    inner_shift,
    w_down,
    down_bias,
):
    micro = tokens_in.shape[0]
    rows = tokens_in.shape[1]
    ntensor = lax.axis_size("tensor")
    length = rows * ntensor
    heads = w_query.shape[1] // HEAD
    columns = column_mask.astype(jnp.float32)
    count_live = float(FF - PADCOLS)
    cosv, sinv = rotary_tables(length, HEAD)
    scale_qk = HEAD ** (-0.5)
    outputs = []
    input_gradients = []
    totals = None
    for step in range(micro):
        weights = fetch_weights(w_query, w_key, w_value, w_out, w_gate, w_up, w_down)
        full_q, full_k, full_v, full_o, full_g, full_u, full_d = weights
        token_rows = tokens_in[step].astype(jnp.float32)
        live = key_mask[step] > 0
        first_normalized, first_inverse_scale = norm_pieces(token_rows)
        normed_rows = (first_normalized * attention_norm_gain + attention_norm_bias).astype(
            jnp.bfloat16
        )
        normed_all = lax.all_gather(normed_rows, "tensor", axis=0, tiled=True)
        query = rotate(
            (matmul(normed_all, full_q) + query_bias).reshape(length, heads, HEAD), cosv, sinv
        ).astype(jnp.bfloat16)
        key = rotate(matmul(normed_all, full_k).reshape(length, heads, HEAD), cosv, sinv).astype(
            jnp.bfloat16
        )
        value = (
            (matmul(normed_all, full_v) + value_bias)
            .reshape(length, heads, HEAD)
            .astype(jnp.bfloat16)
        )
        scores = (
            jnp.einsum("qhd,khd->hqk", query, key, preferred_element_type=jnp.float32) * scale_qk
        )
        scores = jnp.where(live[None, None, :], scores, -1e30)
        top = jnp.max(scores, axis=-1, keepdims=True)
        expo = jnp.exp(scores - top)
        denom = jnp.sum(expo, axis=-1, keepdims=True)
        logsum = top + jnp.log(denom)
        probs = (expo / denom).astype(jnp.bfloat16)
        mixed = (
            jnp.einsum("hqk,khd->qhd", probs, value, preferred_element_type=jnp.float32)
            .reshape(length, heads * HEAD)
            .astype(jnp.bfloat16)
        )
        attn_out = lax.psum_scatter(
            matmul(mixed, full_o).astype(jnp.bfloat16), "tensor", scatter_dimension=0, tiled=True
        ).astype(jnp.float32)
        middle_activation = token_rows + attn_out + out_bias
        second_normalized, second_inverse_scale = norm_pieces(middle_activation)
        normed_second_rows = (
            second_normalized * feedforward_norm_gain + feedforward_norm_bias
        ).astype(jnp.bfloat16)
        normed2_all = lax.all_gather(normed_second_rows, "tensor", axis=0, tiled=True)
        gate = matmul(normed2_all, full_g) + gate_bias
        up_part = matmul(normed2_all, full_u) + up_bias
        sigma = jax.nn.sigmoid(gate)
        act = gate * sigma * up_part
        sums = lax.psum(
            (jnp.sum(act * columns, axis=-1), jnp.sum(act * act * columns, axis=-1)), "tensor"
        )
        row_mean = sums[0][:, None] / count_live
        var = sums[1][:, None] / count_live - row_mean * row_mean
        inner_scale = lax.rsqrt(var + EPS)
        nhat = (act - row_mean) * inner_scale
        hidden = (columns * (nhat * inner_gain + inner_shift)).astype(jnp.bfloat16)
        mlp_out = lax.psum_scatter(
            matmul(hidden, full_d).astype(jnp.bfloat16), "tensor", scatter_dimension=0, tiled=True
        ).astype(jnp.float32)
        outputs.append((middle_activation + mlp_out + down_bias).astype(jnp.bfloat16))
        full_q, full_k, full_v, full_o, full_g, full_u, full_d = fetch_weights(
            w_query, w_key, w_value, w_out, w_gate, w_up, w_down
        )
        output_gradient = cotangent[step].astype(jnp.float32) * image_flag[step].astype(jnp.float32)
        grad_all = lax.all_gather(
            output_gradient.astype(jnp.bfloat16), "tensor", axis=0, tiled=True
        )
        grad_down = matmul_left_t(hidden, grad_all)
        d_hidden = matmul_right_t(grad_all, full_d) * columns
        grad_inner_gain = jnp.sum(d_hidden * nhat, axis=0)
        grad_inner_shift = jnp.sum(d_hidden, axis=0)
        d_nhat = d_hidden * inner_gain
        back_sums = lax.psum((jnp.sum(d_nhat, axis=-1), jnp.sum(d_nhat * nhat, axis=-1)), "tensor")
        d_act = inner_scale * (
            d_nhat - columns * (back_sums[0][:, None] + nhat * back_sums[1][:, None]) / count_live
        )
        d_gate = d_act * up_part * sigma * (1.0 + gate * (1.0 - sigma))
        d_up = d_act * gate * sigma
        grad_gate_bias = jnp.sum(d_gate, axis=0)
        grad_up_bias = jnp.sum(d_up, axis=0)
        gate_low = d_gate.astype(jnp.bfloat16)
        up_low = d_up.astype(jnp.bfloat16)
        grad_gate = matmul_left_t(normed2_all, gate_low)
        grad_up = matmul_left_t(normed2_all, up_low)
        normed_second_gradient = lax.psum_scatter(
            (matmul_right_t(gate_low, full_g) + matmul_right_t(up_low, full_u)).astype(
                jnp.bfloat16
            ),
            "tensor",
            scatter_dimension=0,
            tiled=True,
        ).astype(jnp.float32)
        feedforward_gain_gradient = jnp.sum(normed_second_gradient * second_normalized, axis=0)
        grad_mlp_shift = jnp.sum(normed_second_gradient, axis=0)
        middle_gradient = output_gradient + norm_backward(
            normed_second_gradient, second_normalized, second_inverse_scale, feedforward_norm_gain
        )
        grad_out_bias = jnp.sum(middle_gradient, axis=0)
        grad_down_bias = jnp.sum(output_gradient, axis=0)
        mid_all = lax.all_gather(middle_gradient.astype(jnp.bfloat16), "tensor", axis=0, tiled=True)
        grad_out_weight = matmul_left_t(mixed, mid_all)
        d_mixed = matmul_right_t(mid_all, full_o).astype(jnp.bfloat16).reshape(length, heads, HEAD)
        scores = (
            jnp.einsum("qhd,khd->hqk", query, key, preferred_element_type=jnp.float32) * scale_qk
        )
        scores = jnp.where(live[None, None, :], scores, -1e30)
        probs_full = jnp.exp(scores - logsum)
        d_probs = jnp.einsum("qhd,khd->hqk", d_mixed, value, preferred_element_type=jnp.float32)
        d_value = jnp.einsum(
            "hqk,qhd->khd",
            probs_full.astype(jnp.bfloat16),
            d_mixed,
            preferred_element_type=jnp.float32,
        ).reshape(length, heads * HEAD)
        d_scores = (
            probs_full * (d_probs - jnp.sum(d_probs * probs_full, axis=-1, keepdims=True))
        ).astype(jnp.bfloat16)
        d_query = rotate(
            jnp.einsum("hqk,khd->qhd", d_scores, key, preferred_element_type=jnp.float32)
            * scale_qk,
            cosv,
            -sinv,
        ).reshape(length, heads * HEAD)
        d_key = rotate(
            jnp.einsum("hqk,qhd->khd", d_scores, query, preferred_element_type=jnp.float32)
            * scale_qk,
            cosv,
            -sinv,
        ).reshape(length, heads * HEAD)
        grad_query_bias = jnp.sum(d_query, axis=0)
        grad_value_bias = jnp.sum(d_value, axis=0)
        query_low = d_query.astype(jnp.bfloat16)
        key_low = d_key.astype(jnp.bfloat16)
        value_low = d_value.astype(jnp.bfloat16)
        grad_query = matmul_left_t(normed_all, query_low)
        grad_key = matmul_left_t(normed_all, key_low)
        grad_value = matmul_left_t(normed_all, value_low)
        normed_gradient = lax.psum_scatter(
            (
                matmul_right_t(query_low, full_q)
                + matmul_right_t(key_low, full_k)
                + matmul_right_t(value_low, full_v)
            ).astype(jnp.bfloat16),
            "tensor",
            scatter_dimension=0,
            tiled=True,
        ).astype(jnp.float32)
        attention_gain_gradient = jnp.sum(normed_gradient * first_normalized, axis=0)
        grad_attn_shift = jnp.sum(normed_gradient, axis=0)
        input_gradients.append(
            middle_gradient
            + norm_backward(
                normed_gradient, first_normalized, first_inverse_scale, attention_norm_gain
            )
        )
        fresh = (
            grad_query,
            grad_key,
            grad_value,
            grad_out_weight,
            grad_gate,
            grad_up,
            grad_down,
            attention_gain_gradient,
            grad_attn_shift,
            grad_out_bias,
            feedforward_gain_gradient,
            grad_mlp_shift,
            grad_down_bias,
            grad_query_bias,
            grad_value_bias,
            grad_gate_bias,
            grad_up_bias,
            grad_inner_gain,
            grad_inner_shift,
        )
        totals = (
            fresh if totals is None else tuple((left + right for left, right in zip(totals, fresh)))
        )
    weight_sums = (
        lax.psum_scatter(totals[0], "dp", scatter_dimension=0, tiled=True),
        lax.psum_scatter(totals[1], "dp", scatter_dimension=0, tiled=True),
        lax.psum_scatter(totals[2], "dp", scatter_dimension=0, tiled=True),
        lax.psum_scatter(totals[3], "dp", scatter_dimension=1, tiled=True),
        lax.psum_scatter(totals[4], "dp", scatter_dimension=0, tiled=True),
        lax.psum_scatter(totals[5], "dp", scatter_dimension=0, tiled=True),
        lax.psum_scatter(totals[6], "dp", scatter_dimension=1, tiled=True),
    )
    place = lax.axis_index("tensor")

    def spread(piece):
        whole = jnp.zeros((piece.shape[0] * ntensor,), jnp.float32)
        return lax.dynamic_update_slice(whole, piece, (place * piece.shape[0],))

    vector_sums = lax.psum(
        (
            totals[7],
            totals[8],
            totals[9],
            totals[10],
            totals[11],
            totals[12],
            spread(totals[13]),
            spread(totals[14]),
            spread(totals[15]),
            spread(totals[16]),
            spread(totals[17]),
            spread(totals[18]),
        ),
        ("dp", "tensor"),
    )

    def own(whole, size):
        return lax.dynamic_slice_in_dim(whole, place * size, size, 0)

    head_width = totals[13].shape[0]
    hidden_width = totals[15].shape[0]
    return (
        jnp.stack(outputs),
        jnp.stack(input_gradients),
        vector_sums[0],
        vector_sums[1],
        weight_sums[0],
        weight_sums[1],
        weight_sums[2],
        own(vector_sums[6], head_width),
        own(vector_sums[7], head_width),
        weight_sums[3],
        vector_sums[2],
        vector_sums[3],
        vector_sums[4],
        weight_sums[4],
        own(vector_sums[8], hidden_width),
        weight_sums[5],
        own(vector_sums[9], hidden_width),
        own(vector_sums[10], hidden_width),
        own(vector_sums[11], hidden_width),
        weight_sums[6],
        vector_sums[5],
    )


def solution(mesh):
    in_specs = (
        P("dp", "tensor", None),
        P("dp", "tensor", None),
        P("dp"),
        P("dp", None),
        P("tensor"),
        P(),
        P(),
        P("dp", "tensor"),
        P("dp", "tensor"),
        P("dp", "tensor"),
        P("tensor"),
        P("tensor"),
        P("tensor", "dp"),
        P(),
        P(),
        P(),
        P("dp", "tensor"),
        P("tensor"),
        P("dp", "tensor"),
        P("tensor"),
        P("tensor"),
        P("tensor"),
        P("tensor", "dp"),
        P(),
    )
    out_specs = (
        P("dp", "tensor", None),
        P("dp", "tensor", None),
        P(),
        P(),
        P("dp", "tensor"),
        P("dp", "tensor"),
        P("dp", "tensor"),
        P("tensor"),
        P("tensor"),
        P("tensor", "dp"),
        P(),
        P(),
        P(),
        P("dp", "tensor"),
        P("tensor"),
        P("dp", "tensor"),
        P("tensor"),
        P("tensor"),
        P("tensor"),
        P("tensor", "dp"),
        P(),
    )
    return jax.shard_map(shards, mesh=mesh, in_specs=in_specs, out_specs=out_specs, check_vma=False)
```

profile of v0, /device:TPU:0, one launch (start us, length us, event | category | flops | bytes accessed | tf_op | source)
XLA Modules:
  0.0 1425.9 jit_solution(5293965656040145266)
XLA Ops:
  73.7 37.5 %all-gather.30.cloned.1.call-done = bf16[4,257,1024]{2,1,0:T(8,128)(2,1)} async-done(((bf16[1,257,1024]{2,1,0:T(8,128)(2,1)}), bf16[4,257,1024]{2,1,0:T(8,128)(2,1)}) %all-gather.30.cloned.1.call-update) | async-done | bytes 2105360 | tf_op jit(solution)/shard_map/all_gather | solution.py:143
  201.9 77.9 %fusion.148 = (bf16[264,1024]{1,0:T(8,128)(2,1)}, bf16[264,1024]{1,0:T(8,128)(2,1)}) fusion(bf16[1028,1024]{1,0:T(8,128)(2,1)} %convolution_convert_fusion.3, bf16[1028,1024]{1,0:T(8,128)(2,1)S(1)} %convolution_convert_fusion.1), kind=kCustom, calls=%all-reduce-scatter.10 | all-reduce-scatter fusion | flops 2162689 | bytes 5292544
  309.2 30.3 %all-gather.32.cloned.1.call-done = bf16[4,257,1024]{2,1,0:T(8,128)(2,1)} async-done(((bf16[1,257,1024]{2,1,0:T(8,128)(2,1)}), bf16[4,257,1024]{2,1,0:T(8,128)(2,1)}) %all-gather.32.cloned.1.call-update) | async-done | bytes 2105360 | tf_op jit(solution)/shard_map/all_gather | solution.py:177
  343.0 44.0 %all-gather.28.cloned.1.call-done = bf16[4,257,1024]{2,1,0:T(8,128)(2,1)} async-done(((bf16[1,257,1024]{2,1,0:T(8,128)(2,1)}), bf16[4,257,1024]{2,1,0:T(8,128)(2,1)}) %all-gather.28.cloned.1.call-update) | async-done | bytes 2105360 | tf_op jit(solution)/shard_map/all_gather | solution.py:177
  390.5 22.3 %all-gather.20.cloned.1.call-done = bf16[1024,684]{0,1:T(8,128)(2,1)} async-done(((bf16[128,684]{0,1:T(8,128)(2,1)}), bf16[1024,684]{0,1:T(8,128)(2,1)}) %all-gather.20.cloned.1.call-update) | async-done | bytes 1400848 | tf_op jit(solution)/shard_map/all_gather | solution.py:90
  422.0 17.9 %all-gather.22.cloned.1.call-done = bf16[1024,684]{0,1:T(8,128)(2,1)} async-done(((bf16[128,684]{0,1:T(8,128)(2,1)}), bf16[1024,684]{0,1:T(8,128)(2,1)}) %all-gather.22.cloned.1.call-update) | async-done | bytes 1400848 | tf_op jit(solution)/shard_map/all_gather | solution.py:91
  451.4 19.3 %all-reduce.18 = (f32[1028]{0:T(1024)S(1)}, f32[1028]{0:T(1024)S(1)}, f32[1028]{0:T(1024)S(1)}, f32[1028]{0:T(1024)S(1)}) all-reduce(f32[1028]{0:T(1024)S(1)} %get-tuple-element.118, f32[1028]{0:T(1024)S(1)} %get-tuple-element.119, f32[1028]{0:T(1024)S(1)} %get-tuple-element.91, ...), channel_id=1, replica_groups=mesh['dp'=8,'tensor'=4] {'tensor'}, use_global_device_ids=true, to_apply=%region_22.23 | all-reduce | flops 4112 | bytes 32896 | tf_op jit(solution)/shard_map/psum | solution.py:182
  480.3 15.8 %all-reduce.17 = (f32[1028]{0:T(1024)S(1)}, f32[1028]{0:T(1024)S(1)}, f32[1028]{0:T(1024)S(1)}, f32[1028]{0:T(1024)S(1)}) all-reduce(f32[1028]{0:T(1024)S(1)} %get-tuple-element.307, f32[1028]{0:T(1024)S(1)} %get-tuple-element.306, f32[1028]{0:T(1024)S(1)} %get-tuple-element.85, ...), channel_id=1, replica_groups=mesh['dp'=8,'tensor'=4] {'tensor'}, use_global_device_ids=true, to_apply=%region_27.28 | all-reduce | flops 4112 | bytes 32896 | tf_op jit(solution)/shard_map/psum | solution.py:206
  517.3 71.1 %fusion.147 = (bf16[264,1024]{1,0:T(8,128)(2,1)S(1)}, bf16[264,1024]{1,0:T(8,128)(2,1)}) fusion(bf16[1028,1024]{1,0:T(8,128)(2,1)} %fusion.24, bf16[1028,1024]{1,0:T(8,128)(2,1)} %fusion.25), kind=kCustom, calls=%all-reduce-scatter.9 | all-reduce-scatter fusion | flops 2162689 | bytes 5292544
  628.5 24.6 %all-gather.40.cloned.1.call-done = bf16[4,257,1024]{2,1,0:T(8,128)(2,1)} async-done(((bf16[1,257,1024]{2,1,0:T(8,128)(2,1)}), bf16[4,257,1024]{2,1,0:T(8,128)(2,1)}) %all-gather.40.cloned.1.call-update) | async-done | bytes 2105360 | tf_op jit(solution)/shard_map/all_gather | solution.py:233
  669.5 12.3 multiply_reduce_fusion
  681.8 19.5 %all-gather.36.cloned.1.call-done = bf16[4,257,1024]{2,1,0:T(8,128)(2,1)} async-done(((bf16[1,257,1024]{2,1,0:T(8,128)(2,1)}), bf16[4,257,1024]{2,1,0:T(8,128)(2,1)}) %all-gather.36.cloned.1.call-update) | async-done | bytes 2105360 | tf_op jit(solution)/shard_map/all_gather | solution.py:233
  719.7 11.8 multiply_reduce_fusion.1
  731.6 14.0 multiply_convert_fusion
  761.1 13.4 multiply_convert_fusion.1
  800.7 148.2 %fusion.146 = (bf16[264,1024]{1,0:T(8,128)(2,1)}, bf16[264,1024]{1,0:T(8,128)(2,1)S(1)}, bf16[264,1024]{1,0:T(8,128)(2,1)}, bf16[264,1024]{1,0:T(8,128)(2,1)}) fusion(bf16[1028,1024]{1,0:T(8,128)(2,1)} %convolution_convert_fusion, bf16[1028,1024]{1,0:T(8,128)(2,1)} %convolution_convert_fusion.2, bf16[1028,1024]{1,0:T(8,128)(2,1)} %fusion.23, ...), kind=kCustom, calls=%all-reduce-scatter.8 | all-reduce-scatter fusion | flops 4325377 | bytes 10584576
  1033.9 66.8 %all-reduce.24.cloned.1.call-done = (f32[1024]{0:T(1024)}, f32[1024]{0:T(1024)}, f32[1024]{0:T(1024)}, f32[1024]{0:T(1024)}, f32[1024]{0:T(1024)}, /*index=5*/f3...) async-done(((f32[1024]{0:T(1024)}, f32[1024]{0:T(1024)}, f32[1024]{0:T(1024)}, ...) | async-done | bytes 76560 | tf_op jit(solution)/shard_map/psum | solution.py:328
  1108.8 43.2 %reduce-scatter.36.cloned.1.call-done = f32[684,128]{1,0:T(8,128)} async-done(((f32[684,1024]{1,0:T(8,128)}), f32[684,128]{1,0:T(8,128)}) %reduce-scatter.36.cloned.1.call-update) | async-done | bytes 350224 | tf_op jit(solution)/shard_map/reduce_scatter | solution.py:320
  1152.0 49.7 %reduce-scatter.34.cloned.1.call-done = f32[128,684]{0,1:T(8,128)} async-done(((f32[1024,684]{0,1:T(8,128)}), f32[128,684]{0,1:T(8,128)}) %reduce-scatter.34.cloned.1.call-update) | async-done | bytes 350224 | tf_op jit(solution)/shard_map/reduce_scatter | solution.py:319
  1201.7 49.7 %reduce-scatter.32.cloned.1.call-done = f32[128,684]{0,1:T(8,128)} async-done(((f32[1024,684]{0,1:T(8,128)}), f32[128,684]{0,1:T(8,128)}) %reduce-scatter.32.cloned.1.call-update) | async-done | bytes 350224 | tf_op jit(solution)/shard_map/reduce_scatter | solution.py:318
  1251.4 40.0 %reduce-scatter.30.cloned.1.call-done = f32[256,128]{1,0:T(8,128)} async-done(((f32[256,1024]{1,0:T(8,128)}), f32[256,128]{1,0:T(8,128)}) %reduce-scatter.30.cloned.1.call-update) | async-done | bytes 131088 | tf_op jit(solution)/shard_map/reduce_scatter | solution.py:317
  1291.4 40.0 %reduce-scatter.28.cloned.1.call-done = f32[128,256]{1,0:T(8,128)} async-done(((f32[1024,256]{1,0:T(8,128)}), f32[128,256]{1,0:T(8,128)}) %reduce-scatter.28.cloned.1.call-update) | async-done | bytes 131088 | tf_op jit(solution)/shard_map/reduce_scatter | solution.py:316
  1331.4 40.0 %reduce-scatter.26.cloned.1.call-done = f32[128,256]{1,0:T(8,128)} async-done(((f32[1024,256]{1,0:T(8,128)}), f32[128,256]{1,0:T(8,128)}) %reduce-scatter.26.cloned.1.call-update) | async-done | bytes 131088 | tf_op jit(solution)/shard_map/reduce_scatter | solution.py:315
  1371.4 40.1 %reduce-scatter.24.cloned.1.call-done = f32[128,256]{1,0:T(8,128)} async-done(((f32[1024,256]{1,0:T(8,128)}), f32[128,256]{1,0:T(8,128)}) %reduce-scatter.24.cloned.1.call-update) | async-done | bytes 131088 | tf_op jit(solution)/shard_map/reduce_scatter | solution.py:314
  (597 shorter events, 457.8 us)
Async XLA Ops:
  7.2 59.5 %all-gather.26.cloned.1.call-start = ((), (), s32[]{:S(2)}) async-start(), calls=%async_computation.17 | async-start | bytes 2703360 | tf_op jit(solution)/shard_map/all_gather | solution.py:143
  13.0 98.2 %all-gather.30.cloned.1.call-start = ((), (), s32[]{:S(2)}) async-start(), calls=%async_computation.19 | async-start | bytes 2703360 | tf_op jit(solution)/shard_map/all_gather | solution.py:143
  13.8 282.8 %all-gather.34.cloned.1.call-start = ((), (), s32[]{:S(2)}) async-start(), calls=%async_computation.21 | async-start | bytes 2703360 | tf_op jit(solution)/shard_map/all_gather | solution.py:198
  19.2 280.8 %all-gather.38.cloned.1.call-start = ((), (), s32[]{:S(2)}) async-start(), calls=%async_computation.23 | async-start | bytes 2703360 | tf_op jit(solution)/shard_map/all_gather | solution.py:198
  21.6 282.1 %all-gather.24.cloned.1.call-start = ((), (), s32[]{:S(2)}) async-start(), calls=%async_computation.9 | async-start | bytes 1585152 | tf_op jit(solution)/shard_map/all_gather | solution.py:92
  22.2 317.3 %all-gather.32.cloned.1.call-start = ((), (), s32[]{:S(2)}) async-start(), calls=%async_computation.20 | async-start | bytes 2703360 | tf_op jit(solution)/shard_map/all_gather | solution.py:177
  282.8 6.4 collective-permute-start
  293.4 93.6 %all-gather.28.cloned.1.call-start = ((), (), s32[]{:S(2)}) async-start(), calls=%async_computation.18 | async-start | bytes 2703360 | tf_op jit(solution)/shard_map/all_gather | solution.py:177
  294.1 118.6 %all-gather.20.cloned.1.call-start = ((), (), s32[]{:S(2)}) async-start(), calls=%async_computation.7 | async-start | bytes 1585152 | tf_op jit(solution)/shard_map/all_gather | solution.py:90
  294.9 144.9 %all-gather.22.cloned.1.call-start = ((), (), s32[]{:S(2)}) async-start(), calls=%async_computation.8 | async-start | bytes 1585152 | tf_op jit(solution)/shard_map/all_gather | solution.py:91
  295.6 357.5 %all-gather.40.cloned.1.call-start = ((), (), s32[]{:S(2)}) async-start(), calls=%async_computation.24 | async-start | bytes 2703360 | tf_op jit(solution)/shard_map/all_gather | solution.py:233
  591.8 6.3 collective-permute-start.4
  607.0 94.3 %all-gather.36.cloned.1.call-start = ((), (), s32[]{:S(2)}) async-start(), calls=%async_computation.22 | async-start | bytes 2703360 | tf_op jit(solution)/shard_map/all_gather | solution.py:233
  619.8 480.9 %all-reduce.24.cloned.1.call-start = ((), (), s32[]{:S(2)}) async-start(), calls=%async_computation.25 | async-start | bytes 163840 | tf_op jit(solution)/shard_map/psum | solution.py:328
  949.9 8.2 collective-permute-start.5
  952.2 9.7 collective-permute-start.7
  955.0 10.0 collective-permute-start.1
  974.8 177.3 %reduce-scatter.36.cloned.1.call-start = ((), (), s32[]{:S(2)}) async-start(), calls=%async_computation.16 | async-start | bytes 3170304 | tf_op jit(solution)/shard_map/reduce_scatter | solution.py:320
  982.2 219.5 %reduce-scatter.34.cloned.1.call-start = ((), (), s32[]{:S(2)}) async-start(), calls=%async_computation.15 | async-start | bytes 3170304 | tf_op jit(solution)/shard_map/reduce_scatter | solution.py:319
  990.2 261.2 %reduce-scatter.32.cloned.1.call-start = ((), (), s32[]{:S(2)}) async-start(), calls=%async_computation.14 | async-start | bytes 3170304 | tf_op jit(solution)/shard_map/reduce_scatter | solution.py:318
  998.4 293.1 %reduce-scatter.30.cloned.1.call-start = ((), (), s32[]{:S(2)}) async-start(), calls=%async_computation.13 | async-start | bytes 1179648 | tf_op jit(solution)/shard_map/reduce_scatter | solution.py:317
  1003.1 328.3 %reduce-scatter.28.cloned.1.call-start = ((), (), s32[]{:S(2)}) async-start(), calls=%async_computation.12 | async-start | bytes 1179648 | tf_op jit(solution)/shard_map/reduce_scatter | solution.py:316
  1007.9 363.5 %reduce-scatter.26.cloned.1.call-start = ((), (), s32[]{:S(2)}) async-start(), calls=%async_computation.11 | async-start | bytes 1179648 | tf_op jit(solution)/shard_map/reduce_scatter | solution.py:315
  1012.6 398.9 %reduce-scatter.24.cloned.1.call-start = ((), (), s32[]{:S(2)}) async-start(), calls=%async_computation.10 | async-start | bytes 1179648 | tf_op jit(solution)/shard_map/reduce_scatter | solution.py:314
  (168 other events, 2716.1 us)
Sparse Core Ops, SparseCore 0:
  13.1 49.9 all-gather.25
  65.2 45.9 all-gather.29
  112.8 45.9 all-gather.33
  160.2 45.8 all-gather.37
  207.9 23.9 all-gather.23
  293.5 45.8 all-gather.31
  341.0 45.9 all-gather.27
  388.9 23.8 all-gather.19
  414.7 25.1 all-gather.21
  607.1 45.9 all-gather.39
  655.3 45.9 all-gather.35
  974.9 125.7 all-reduce.23
  1105.2 46.7 reduce-scatter.35
  1156.3 45.3 reduce-scatter.33
  1206.0 45.3 reduce-scatter.31
  1255.4 36.0 reduce-scatter.29
  1295.3 35.9 reduce-scatter.27
  1335.3 36.0 reduce-scatter.25
  1375.5 36.0 reduce-scatter.23
where the time goes:
time: 1430 us
  waiting for transfers between devices  571 us (40%)
  blocking collectives  375 us (26%)
  matrix products  236 us (17%)
  local copies, waits for them, and re-layouts  118 us (8%)
  other arithmetic  89.2 us (6%)
  between operations  18.7 us (1%)
  starting transfers between devices  17.7 us (1%)
    unnamed x3, blocking collectives  297 us
    unnamed x363, local copies, waits for them, and re-layouts  86.2 us
    all_gather x2, waiting for transfers between devices, shards(): lax.all_gather(normed_second_rows, 'tensor', axis=0, tiled=True)  74.3 us
    psum x1, waiting for transfers between devices, shards(): lax.psum((totals[7], totals[8], totals[9], totals[10], totals[11], totals...  66.8 us
    reduce_scatter x1, waiting for transfers between devices, shards(): lax.psum_scatter(totals[5], 'dp', scatter_dimension=0, tiled=True)  49.7 us
    reduce_scatter x1, waiting for transfers between devices, shards(): lax.psum_scatter(totals[4], 'dp', scatter_dimension=0, tiled=True)  49.7 us
    dot_general x14, matrix products, matmul_left_t(): lax.dot_general(left, right, (((0,), (0,)), ((), ())), preferred_element_...  48.2 us
    dot_general x14, matrix products, matmul(): return jnp.dot(left, right, preferred_element_type=jnp.float32)  45.8 us
  transfers between devices with their start and end apart: 27, of which 16 were waited for; matrix products, arithmetic and copies ran while one was open for 24% of the time, Pallas kernels for 0%

commit v1 on v0

v1 whole, which is shorter than its diff:
```python
import functools
import math

import jax
import jax.numpy as jnp
from jax import lax
from jax.experimental import pallas as pl
from jax.experimental.pallas import tpu as pltpu
from jax.sharding import PartitionSpec as P

HEAD = 64
FF = 2736
PADCOLS = 6
GRID = 32
EPS = 1e-06
ROPE_BASE = 10000.0
LANES = 128
MESH = pl.DeviceIdType.MESH
LOG2E = math.log2(math.e)
LN2 = math.log(2.0)
SCALE = HEAD ** (-0.5)
F32 = jnp.float32
BF16 = jnp.bfloat16


def up_to(size, unit):
    return -(-size // unit) * unit


def rotary_tables(length, head):
    quarter = head // 4
    place = jnp.arange(length, dtype=jnp.int32)
    inside = (place >= 1) & (place <= GRID * GRID)
    cell = jnp.maximum(place - 1, 0)
    row_pos = jnp.where(inside, cell // GRID, 0).astype(F32)
    col_pos = jnp.where(inside, cell % GRID, 0).astype(F32)
    freq = ROPE_BASE ** (-jnp.arange(quarter, dtype=F32) / quarter)
    angle = jnp.concatenate(
        [row_pos[:, None] * freq[None, :], col_pos[:, None] * freq[None, :]], axis=1
    )
    return jnp.cos(angle), jnp.sin(angle)


def lane_tables(length, quarter, block, rows_padded):
    cosv, sinv = rotary_tables(length, HEAD)

    def lay(first, second):
        one = jnp.concatenate(
            [first[:, :quarter], second[:, :quarter], first[:, quarter:], second[:, quarter:]], axis=1
        )
        two = jnp.concatenate([one, one], axis=1)
        cut = two.reshape(length // block, block, 2 * HEAD)
        return jnp.pad(cut, ((0, 0), (0, rows_padded - block), (0, 0))).reshape(-1, 2 * HEAD)

    zero = jnp.zeros_like(sinv)
    return lay(cosv, cosv), lay(-sinv, zero), lay(zero, sinv)


def norm_pieces(values):
    row_mean = jnp.mean(values, axis=-1, keepdims=True)
    var = jnp.mean(jnp.square(values - row_mean), axis=-1, keepdims=True)
    inverse_scale = lax.rsqrt(var + EPS)
    return ((values - row_mean) * inverse_scale, inverse_scale)


def norm_backward(incoming_gradient, centered_normalized, inverse_scale, norm_gain):
    inner = incoming_gradient * norm_gain
    return inverse_scale * (
        inner
        - jnp.mean(inner, axis=-1, keepdims=True)
        - centered_normalized * jnp.mean(inner * centered_normalized, axis=-1, keepdims=True)
    )


def matmul(left, right):
    return jnp.dot(left, right, preferred_element_type=F32)


def matmul_right_t(left, right):
    return lax.dot_general(left, right, (((1,), (1,)), ((), ())), preferred_element_type=F32)


def matmul_left_t(left, right):
    return lax.dot_general(left, right, (((0,), (0,)), ((), ())), preferred_element_type=F32)


class Kind:
    def __init__(self, by_rows, shard, n_dp):
        self.given = shard
        self.n_dp = n_dp
        self.turn = not by_rows and shard[1] % LANES != 0
        if self.turn:
            shard = (shard[1], up_to(shard[0], LANES))
        self.by_rows = by_rows or self.turn
        self.shard = shard
        a, b = shard
        if self.by_rows:
            self.whole, self.two = (n_dp * a, 2 * b), (2 * a, b)
        else:
            self.whole, self.two = (2 * a, n_dp * b), (a, 2 * b)

    def piece(self, ref, slot, chip):
        a, b = self.shard
        if self.by_rows:
            return ref.at[pl.ds(_mult(chip, 2 * a), 2 * a), pl.ds(_mult(slot, b), b)]
        return ref.at[pl.ds(_mult(slot, a), a), pl.ds(_mult(chip, 2 * b), 2 * b)]

    def half(self, two, core):
        a, b = self.shard
        if self.by_rows:
            return two.at[pl.ds(_mult(core, a), a)]
        return two.at[:, pl.ds(_mult(core, b), b)]

    def one(self, ref, slot, chip, core):
        a, b = self.shard
        if self.by_rows:
            return ref.at[pl.ds(_mult(chip * 2 + core, a), a), pl.ds(_mult(slot, b), b)]
        return ref.at[pl.ds(_mult(slot, a), a), pl.ds(_mult(chip * 2 + core, b), b)]

    def enter(self, shard):
        if not self.turn:
            return shard
        return jnp.pad(shard.T, ((0, 0), (0, self.shard[1] - self.given[0])))

    def leave(self, shard):
        return shard[:, : self.given[0]].T if self.turn else shard

    def join(self, whole):
        if not self.turn:
            return whole
        a, b = self.shard
        whole = whole.reshape(self.n_dp * a, 2, b)[:, :, : self.given[0]]
        return whole.transpose(1, 2, 0).reshape(2 * self.given[0], self.n_dp * a)

    def cut(self, whole):
        if not self.turn:
            return whole
        a, b = self.shard
        whole = whole.reshape(2, self.given[0], self.n_dp * a).transpose(2, 0, 1)
        return jnp.pad(whole, ((0, 0), (0, 0), (0, b - self.given[0]))).reshape(self.whole)


def _mult(index, size):
    return index * size if isinstance(index, int) else pl.multiple_of(index * size, size)


class Place:
    def __init__(self, n_dp, n_tensor):
        self.dp = lax.axis_index("dp")
        self.z = lax.axis_index("tensor")
        self.core = lax.rem(self.dp, 2)
        self.chip = lax.div(self.dp, 2)
        self.nz = n_tensor
        self.chips = n_dp // 2
        self.bits = self.chips.bit_length() - 1
        self.home = self.core == lax.div(self.z, n_tensor // 2)
        self.slot = lax.rem(self.z, n_tensor // 2)

    def flip(self, bit):
        low = lax.rem(lax.div(self.chip, 1 << bit), 2)
        return self.chip + (1 - 2 * low) * (1 << bit)

    def across(self):
        return (self.dp + 1 - 2 * self.core, self.z)

    def beside(self, bit):
        return (self.flip(bit) * 2 + self.core, self.z)

    def shifted(self, by):
        return (self.dp, lax.rem(self.z + by, self.nz))

    def barrier(self):
        everyone = [self.across()]
        everyone += [self.shifted(s) for s in range(1, self.nz)]
        everyone += [self.beside(b) for b in range(self.bits)]
        bar = pltpu.get_barrier_semaphore()
        for one in everyone:
            pl.semaphore_signal(bar, inc=1, device_id=one, device_id_type=MESH)
        pl.semaphore_wait(bar, len(everyone))


def remote(src, dst, send, recv, to):
    return pltpu.make_async_remote_copy(
        src_ref=src, dst_ref=dst, send_sem=send, recv_sem=recv, device_id=to, device_id_type=MESH
    )


def flipped(chip, value):
    return lax.bitwise_xor(chip, value)


def gather_kernel(kinds, n_acts, n_packs, n_pairs, sizes, *refs):
    n_dp, n_tensor = sizes
    n_w = len(kinds)
    me = Place(n_dp, n_tensor)
    at = 0
    groups = []
    for count in (n_acts, n_packs, n_pairs, n_w) * 2:
        groups.append(refs[at : at + count])
        at += count
    act_in, pack_in, pair_in, w_in, act_out, pack_out, pair_out, w_out = groups
    (a_send, a_recv, a_fwd, a_back, k_send, k_recv, q_send, q_recv, s_send, s_recv, z_send, z_recv, b_send, b_recv, loc) = refs[at:]
    half_z = n_tensor // 2
    me.barrier()

    def local(src, dst, n):
        return pltpu.make_async_copy(src, dst, loc.at[n])

    for j, kind in enumerate(kinds):
        mine = kind.one(w_out[j], me.slot, me.chip, me.core)

        @pl.when(me.home)
        def _(j=j, mine=mine):
            local(w_in[j], mine, j).start()

        @pl.when(jnp.logical_not(me.home))
        def _(j=j, mine=mine):
            remote(w_in[j], mine, s_send.at[j], s_recv.at[j], me.across()).start()

    def act_copy(n, i):
        target = half_z * me.core + i
        return target, remote(
            act_in[n].at[i], act_out[n].at[me.z], a_send.at[n, i], a_recv.at[n, me.z], (me.dp, target)
        )

    def start_acts(n):
        for i in range(half_z):
            target, copy = act_copy(n, i)
            pl.when(target != me.z)(copy.start)

            @pl.when(target == me.z)
            def _(n=n, i=i):
                local(act_in[n].at[i], act_out[n].at[me.z], n_w + n).start()

    def pass_acts(n):
        @pl.when(me.home)
        def _():
            for s in range(n_tensor):
                src = lax.rem(me.z + s, n_tensor)
                slab = act_out[n].at[src]
                if s == 0:
                    local(slab, slab, n_w + n).wait()
                else:
                    remote(slab, slab, a_send.at[n, 0], a_recv.at[n, src], me.across()).wait_recv()
                remote(slab, slab, a_fwd.at[n, src], a_back.at[n, src], me.across()).start()

    def end_acts(n):
        for i in range(half_z):
            target, copy = act_copy(n, i)
            pl.when(target != me.z)(copy.wait_send)
        for src in range(n_tensor):
            slab = act_out[n].at[src]
            copy = remote(slab, slab, a_fwd.at[n, src], a_back.at[n, src], me.across())

            pl.when(me.home)(copy.wait_send)
            pl.when(jnp.logical_not(me.home))(copy.wait_recv)

    def pack_copy(n, s):
        return remote(
            pack_in[n], pack_out[n].at[me.slot], k_send.at[n, s - 1], k_recv.at[n, me.slot], me.shifted(s)
        )

    for n in range(n_packs):

        @pl.when(me.home)
        def _(n=n):
            local(pack_in[n], pack_out[n].at[me.slot], n_w + n_acts + n).start()
            for s in range(1, n_tensor):
                pack_copy(n, s).start()

    for n in range(n_pairs):
        there = remote(pair_in[n], pair_out[n], q_send.at[n], q_recv.at[n], me.across())

        @pl.when(me.home)
        def _(n=n, there=there):
            local(pair_in[n], pair_out[n], n_w + n_acts + n_packs + n).start()
            there.start()

    if n_acts and n_packs:
        for n in range(n_acts):
            start_acts(n)

    def start_z(j):
        kind = kinds[j]
        mine = kind.one(w_out[j], me.slot, me.chip, me.core)

        @pl.when(me.home)
        def _():
            local(w_in[j], mine, j).wait()
            remote(w_in[j], mine, s_send.at[j], s_recv.at[j], me.across()).wait_recv()
            src = kind.piece(w_out[j], me.slot, me.chip)
            for s in range(1, n_tensor):
                remote(src, src, z_send.at[j, s - 1], z_recv.at[j, me.slot], me.shifted(s)).start()

    def wait_z(j):
        for slot in range(2):
            src = kinds[j].piece(w_out[j], slot, me.chip)
            copy = remote(src, src, z_send.at[j, 0], z_recv.at[j, slot], me.across())
            pl.when(me.core * half_z + slot != me.z)(copy.wait_recv)

    def bit_copies(j, step, slot):
        bit = step if slot == 0 else me.bits - 1 - step
        low = 1 if slot == 0 else 1 << (me.bits - step)

        def held(m):
            return flipped(me.chip, m * low)

        def send(m):
            src = kinds[j].piece(w_out[j], slot, held(m))
            return remote(src, src, b_send.at[j, step, slot, m], b_recv.at[j, step, slot, m], me.beside(bit))

        return send

    def start_bits(j, step):
        for slot in range(2):
            send = bit_copies(j, step, slot)
            _each(1 << step, lambda m: send(m).start())

    def wait_bits(j, step):
        for slot in range(2):
            send = bit_copies(j, step, slot)
            _each(1 << step, lambda m: send(m).wait_recv())

    lag = me.bits + 1
    if n_w:
        start_z(0)
    for tick in range(n_w + lag):
        if tick < n_w:
            wait_z(tick)
            if tick + 1 < n_w:
                start_z(tick + 1)
            elif not n_packs:
                for n in range(n_acts):
                    start_acts(n)
        for step in range(me.bits + 1):
            j = tick - step
            if 0 <= j < n_w:
                if step > 0:
                    wait_bits(j, step - 1)
                if step < me.bits:
                    start_bits(j, step)
        if tick == 0 and n_packs:
            for n in range(n_acts):
                pass_acts(n)
    if not n_packs:
        for n in range(n_acts):
            pass_acts(n)

    for j, kind in enumerate(kinds):
        mine = kind.one(w_out[j], me.slot, me.chip, me.core)
        copy = remote(w_in[j], mine, s_send.at[j], s_recv.at[j], me.across())
        pl.when(jnp.logical_not(me.home))(copy.wait_send)
        src = kind.piece(w_out[j], me.slot, me.chip)
        for s in range(1, n_tensor):
            copy = remote(src, src, z_send.at[j, s - 1], z_recv.at[j, 0], me.shifted(s))
            pl.when(me.home)(copy.wait_send)
        for step in range(me.bits):
            for slot in range(2):
                send = bit_copies(j, step, slot)
                _each(1 << step, lambda m: send(m).wait_send())
    for n in range(n_acts):
        end_acts(n)
    for n in range(n_packs):
        for slot in range(2):
            row = pack_out[n].at[slot]
            copy = remote(pack_in[n], row, k_send.at[n, 0], k_recv.at[n, slot], me.across())
            pl.when(me.core * half_z + slot != me.z)(copy.wait_recv)

        @pl.when(me.home)
        def _(n=n):
            local(pack_in[n], pack_out[n].at[me.slot], n_w + n_acts + n).wait()
            for s in range(1, n_tensor):
                pack_copy(n, s).wait_send()

    for n in range(n_pairs):
        there = remote(pair_in[n], pair_out[n], q_send.at[n], q_recv.at[n], me.across())

        @pl.when(me.home)
        def _(n=n, there=there):
            local(pair_in[n], pair_out[n], n_w + n_acts + n_packs + n).wait()
            there.wait_send()

        pl.when(jnp.logical_not(me.home))(there.wait_recv)


def _each(count, act):
    if count <= 4:
        for m in range(count):
            act(m)
    else:

        @pl.loop(0, count)
        def _(m):
            act(m)


def gather(acts, packs, pairs, weights, kinds, sizes, cid):
    n_dp, n_tensor = sizes
    bits = (n_dp // 2).bit_length() - 1
    n_a, n_k, n_q, n_w = len(acts), len(packs), len(pairs), len(weights)
    shapes = [jax.ShapeDtypeStruct((n_tensor,) + a.shape[1:], a.dtype) for a in acts]
    shapes += [jax.ShapeDtypeStruct((2,) + a.shape, a.dtype) for a in packs]
    shapes += [jax.ShapeDtypeStruct(a.shape, a.dtype) for a in pairs]
    shapes += [jax.ShapeDtypeStruct(k.whole, w.dtype) for k, w in zip(kinds, weights)]
    dma = pltpu.SemaphoreType.DMA
    na, nk, nq = max(n_a, 1), max(n_k, 1), max(n_q, 1)
    most = max(1 << max(bits - 1, 0), 1)
    out = pl.pallas_call(
        functools.partial(gather_kernel, kinds, n_a, n_k, n_q, sizes),
        out_shape=shapes,
        in_specs=[pl.BlockSpec(memory_space=pltpu.HBM)] * (n_a + n_k + n_q + n_w),
        out_specs=[pl.BlockSpec(memory_space=pltpu.HBM)] * len(shapes),
        scratch_shapes=[
            dma((na, n_tensor)),
            dma((na, n_tensor)),
            dma((na, n_tensor)),
            dma((na, n_tensor)),
            dma((nk, n_tensor)),
            dma((nk, 2)),
            dma((nq,)),
            dma((nq,)),
            dma((n_w,)),
            dma((n_w,)),
            dma((n_w, n_tensor)),
            dma((n_w, 2)),
            dma((n_w, bits, 2, most)),
            dma((n_w, bits, 2, most)),
            dma((n_w + n_a + n_k + n_q,)),
        ],
        compiler_params=pltpu.CompilerParams(collective_id=cid, has_side_effects=True),
        name=f"gather{cid}",
    )(*acts, *packs, *pairs, *[k.enter(w) for k, w in zip(kinds, weights)])
    a, k, q = out[:n_a], out[n_a : n_a + n_k], out[n_a + n_k : n_a + n_k + n_q]
    return a, k, q, [kind.join(w) for kind, w in zip(kinds, out[n_a + n_k + n_q :])]


def scatter_kernel(kinds, n_acts, sizes, *refs):
    n_dp, n_tensor = sizes
    n_w = len(kinds)
    me = Place(n_dp, n_tensor)
    half_z = n_tensor // 2
    act_in, vec_in, g_in = refs[:n_acts], refs[n_acts], refs[n_acts + 1 : n_acts + 1 + n_w]
    at = n_acts + 1 + n_w
    act_out, vec_out, g_out = refs[at : at + n_acts], refs[at + n_acts], refs[at + n_acts + 1 : at + n_acts + 1 + n_w]
    at += n_acts + 1 + n_w
    acc, got, gotz, stage = (refs[at + i * n_w : at + (i + 1) * n_w] for i in range(4))
    at += 4 * n_w
    (v_sum, v_got, v_all) = refs[at : at + 3]
    (a_send, a_recv, b_send, b_recv, z_send, z_recv, f_send, f_recv, vb_send, vb_recv, vz_send, vz_recv, vf_send, vf_recv, loc) = refs[at + 3 :]
    me.barrier()

    def local(src, dst, n):
        return pltpu.make_async_copy(src, dst, loc.at[n])

    def order(step, slot):
        if slot == 0:
            return me.bits - 1 - step, 1, 1 << (me.bits - 1 - step)
        return step, 1 << (step + 1), 1 << (me.bits - 1 - step)

    def copies(j, step, slot):
        bit, stride, count = order(step, slot)
        source = g_in[j] if step == 0 else acc[j]

        def send(m):
            src = kinds[j].piece(source, slot, flipped(me.chip, m * stride + (1 << bit)))
            dst = got[j].at[_base(me.bits, step) + m, slot]
            return remote(src, dst, b_send.at[j, step, slot, m], b_recv.at[j, step, slot, m], me.beside(bit))

        return send, count, stride

    def start_bits(j, step):
        for slot in range(2):
            send, count, _ = copies(j, step, slot)
            _each(count, lambda m: send(m).start())

    def add_bits(j, step):
        for slot in range(2):
            send, count, stride = copies(j, step, slot)

            def one(m):
                send(m).wait_recv()
                here = kinds[j].piece(acc[j], slot, flipped(me.chip, m * stride))
                here[...] = (
                    here[...].astype(F32) + got[j][_base(me.bits, step) + m, slot].astype(F32)
                ).astype(BF16)

            _each(count, one)

    def z_copy(j, slot):
        target = half_z * me.core + slot
        index = lax.rem(me.z - target + n_tensor - 1, n_tensor)
        src = kinds[j].piece(acc[j], slot, me.chip)
        return target, remote(src, gotz[j].at[index], z_send.at[j, slot], z_recv.at[j, index], (me.dp, target))

    def start_z(j):
        for slot in range(2):
            target, copy = z_copy(j, slot)
            pl.when(target != me.z)(copy.start)

    def last_copy(j):
        return remote(stage[j], g_out[j], f_send.at[j], f_recv.at[j], me.across())

    def end_z(j):
        @pl.when(me.home)
        def _():
            for index in range(n_tensor - 1):
                slab = gotz[j].at[index]
                remote(slab, slab, z_send.at[j, 0], z_recv.at[j, index], me.across()).wait_recv()

            def total(core):
                value = kinds[j].one(acc[j], me.slot, me.chip, core)[...].astype(F32)
                for index in range(n_tensor - 1):
                    value = value + kinds[j].half(gotz[j].at[index], core)[...].astype(F32)
                return value

            stage[j][...] = total(1 - me.core)
            last_copy(j).start()
            g_out[j][...] = total(me.core)

    def vec_bit(step):
        return remote(v_sum.at[step], v_got.at[step], vb_send.at[step], vb_recv.at[step], me.beside(step))

    def vec_z(s):
        return remote(v_sum.at[me.bits], v_all.at[me.z], vz_send.at[s - 1], vz_recv.at[me.z], me.shifted(s))

    def vec_last():
        return remote(v_sum.at[me.bits + 1], vec_out.at[me.core], vf_send.at[0], vf_recv.at[0], me.across())

    def vec_phase(step):
        if step == 0:
            v_sum[0] = vec_in[...]
            vec_bit(0).start()
        elif step <= me.bits:
            vec_bit(step - 1).wait_recv()
            v_sum[step] = v_sum[step - 1] + v_got[step - 1]
            if step < me.bits:
                vec_bit(step).start()
            else:
                for s in range(1, n_tensor):
                    vec_z(s).start()
                v_all[me.z] = v_sum[me.bits]
        elif step == me.bits + 1:
            for s in range(1, n_tensor):
                src = lax.rem(me.z + s, n_tensor)
                remote(v_all.at[src], v_all.at[src], vz_send.at[0], vz_recv.at[src], me.across()).wait_recv()
            value = v_all[0]
            for s in range(1, n_tensor):
                value = value + v_all[s]
            v_sum[me.bits + 1] = value
            vec_last().start()
            vec_out[me.core] = value
        else:
            there = vec_out.at[1 - me.core]
            remote(there, there, vf_send.at[0], vf_recv.at[0], me.across()).wait_recv()

    def act_copy(n, s):
        place = lax.rem(me.z + s, n_tensor)
        return remote(
            act_in[n].at[place], act_out[n].at[me.slot], a_send.at[n, s - 1], a_recv.at[n, me.slot], (me.dp, place)
        )

    def start_acts(n):
        @pl.when(me.home)
        def _():
            for s in range(1, n_tensor):
                act_copy(n, s).start()
            local(act_in[n].at[me.z], act_out[n].at[me.slot], n_w + n).start()

    for j in range(n_w):
        local(g_in[j], acc[j], j).start()
    for n in range(n_acts):
        start_acts(n)
    phase = 0
    lag = me.bits + 2
    for tick in range(n_w + lag):
        for step in range(lag):
            j = tick - step
            if 0 <= j < n_w:
                if step == 0:
                    start_bits(j, 0)
                    local(g_in[j], acc[j], j).wait()
                elif step <= me.bits:
                    add_bits(j, step - 1)
                    if step < me.bits:
                        start_bits(j, step)
                    else:
                        start_z(j)
                else:
                    end_z(j)
        if phase < me.bits + 3:
            vec_phase(phase)
            phase += 1
    while phase < me.bits + 3:
        vec_phase(phase)
        phase += 1

    for j in range(n_w):
        for step in range(me.bits):
            for slot in range(2):
                send, count, _ = copies(j, step, slot)
                _each(count, lambda m: send(m).wait_send())
        for slot in range(2):
            target, copy = z_copy(j, slot)
            pl.when(target != me.z)(copy.wait_send)
        pl.when(me.home)(last_copy(j).wait_send)
        pl.when(jnp.logical_not(me.home))(last_copy(j).wait_recv)
    for step in range(me.bits):
        vec_bit(step).wait_send()
    for s in range(1, n_tensor):
        vec_z(s).wait_send()
    vec_last().wait_send()
    for n in range(n_acts):

        @pl.when(me.home)
        def _(n=n):
            for s in range(1, n_tensor):
                act_copy(n, s).wait_send()
            local(act_in[n].at[me.z], act_out[n].at[me.slot], n_w + n).wait()

        for slot in range(2):
            row = act_out[n].at[slot]
            copy = remote(row, row, a_send.at[n, 0], a_recv.at[n, slot], me.across())
            pl.when(me.core * half_z + slot != me.z)(copy.wait_recv)


def _base(bits, step):
    return sum(1 << (bits - 1 - s) for s in range(step))


def scatter(acts, vec, grads, kinds, sizes, cid):
    n_dp, n_tensor = sizes
    chips = n_dp // 2
    bits = chips.bit_length() - 1
    n_a, n_w = len(acts), len(grads)
    grads = [kind.cut(g) for kind, g in zip(kinds, grads)]
    shapes = [jax.ShapeDtypeStruct((n_tensor // 2,) + a.shape[1:], a.dtype) for a in acts]
    shapes += [jax.ShapeDtypeStruct((2,) + vec.shape, F32)]
    shapes += [jax.ShapeDtypeStruct(k.shard, F32) for k in kinds]
    dma = pltpu.SemaphoreType.DMA
    hbm = pl.BlockSpec(memory_space=pltpu.HBM)
    vmem = pl.BlockSpec(memory_space=pltpu.VMEM)
    most = max(chips // 2, 1)
    out = pl.pallas_call(
        functools.partial(scatter_kernel, kinds, n_a, sizes),
        out_shape=shapes,
        in_specs=[hbm] * n_a + [vmem] + [hbm] * n_w,
        out_specs=[hbm] * n_a + [vmem] + [vmem] * n_w,
        scratch_shapes=[pltpu.VMEM(k.whole, BF16) for k in kinds]
        + [pltpu.VMEM((chips - 1, 2) + k.two, BF16) for k in kinds]
        + [pltpu.VMEM((n_tensor - 1,) + k.two, BF16) for k in kinds]
        + [pltpu.VMEM(k.shard, F32) for k in kinds]
        + [
            pltpu.VMEM((bits + 2,) + vec.shape, F32),
            pltpu.VMEM((bits,) + vec.shape, F32),
            pltpu.VMEM((n_tensor,) + vec.shape, F32),
            dma((n_a, n_tensor)),
            dma((n_a, 2)),
            dma((n_w, bits, 2, most)),
            dma((n_w, bits, 2, most)),
            dma((n_w, 2)),
            dma((n_w, n_tensor)),
            dma((n_w,)),
            dma((n_w,)),
            dma((bits,)),
            dma((bits,)),
            dma((n_tensor,)),
            dma((n_tensor,)),
            dma((1,)),
            dma((1,)),
            dma((n_w + n_a,)),
        ],
        compiler_params=pltpu.CompilerParams(
            collective_id=cid, has_side_effects=True, vmem_limit_bytes=56 * 2**20
        ),
        name=f"scatter{cid}",
    )(*acts, vec, *grads)
    return out[:n_a], out[n_a], [k.leave(g) for k, g in zip(kinds, out[n_a + 1 :])]


KEYS = 1152
TILE = 352
COLS = 384


def _turn(x, cos, sin_up, sin_down):
    quarter = HEAD // 4
    return (
        x * cos
        + pltpu.roll(x, 2 * HEAD - quarter, 1) * sin_up
        + pltpu.roll(x, quarter, 1) * sin_down
    )


def attention_forward_kernel(
    x_ref, wq_ref, wk_ref, wv_ref, cos_ref, up_ref, down_ref, qb_ref, vb_ref, base_ref,
    qa_ref, ka_ref, va_ref, mix_ref,
):
    rows = x_ref.shape[0]
    tiles = rows // TILE
    lane = lax.broadcasted_iota(jnp.int32, (TILE, 2 * HEAD), 1)
    low = lane < HEAD
    one = jnp.where(lane == HEAD, 1.0, 0.0)
    ones = jnp.where((lane >= HEAD) & (lane < HEAD + 3), 1.0, 0.0)

    @pl.loop(0, tiles)
    def _(t):
        here = pl.ds(pl.multiple_of(t * TILE, TILE), TILE)
        x = x_ref[here, :]
        both = matmul(x, jnp.concatenate([wq_ref[...], wk_ref[...]], axis=1))
        tables = (cos_ref[here, :], up_ref[here, :], down_ref[here, :])
        query = _turn(both[:, : 2 * HEAD] + qb_ref[0], *tables) * (SCALE * LOG2E)
        key = _turn(both[:, 2 * HEAD :], *tables)
        value = matmul(x, wv_ref[...]) + vb_ref[0]
        base = base_ref[here, :].astype(F32)
        for h in range(2):
            if h:
                query, key, value = (pltpu.roll(v, HEAD, 1) for v in (query, key, value))
            qa_ref[h, here, :] = jnp.where(low, query, one).astype(BF16)
            ka_ref[h, here, :] = jnp.where(low, key, base).astype(BF16)
            va_ref[h, here, :] = jnp.where(low, value, ones).astype(BF16)

    rest = pl.ds(rows, KEYS - rows)
    for h in range(2):
        qa_ref[h, rest, :] = jnp.zeros((KEYS - rows, 2 * HEAD), BF16)
        va_ref[h, rest, :] = jnp.zeros((KEYS - rows, 2 * HEAD), BF16)
        ka_ref[h, rest, :] = base_ref[rest, :]

    @pl.loop(0, tiles)
    def _(t):
        here = pl.ds(pl.multiple_of(t * TILE, TILE), TILE)
        outs = []
        for h in range(2):
            q = qa_ref[h, here, :]
            s = matmul_right_t(q, ka_ref[h])
            top = jnp.max(s, axis=1, keepdims=True)
            p = jnp.exp2(s - top).astype(BF16)
            o = matmul(p, va_ref[h])
            total = o[:, HEAD : HEAD + 1]
            outs.append(o / total)
            log = -(top + jnp.log2(total))
            first = log.astype(BF16)
            left = log - first.astype(F32)
            second = left.astype(BF16)
            third = (left - second.astype(F32)).astype(BF16)
            logs = jnp.where(
                lane == HEAD + 1,
                first.astype(F32),
                jnp.where(lane == HEAD + 2, second.astype(F32), third.astype(F32)),
            )
            inside = (lane > HEAD) & (lane <= HEAD + 3)
            qa_ref[h, here, :] = jnp.where(inside, logs, q.astype(F32)).astype(BF16)
        mix_ref[here, :] = jnp.where(low, outs[0], pltpu.roll(outs[1], HEAD, 1)).astype(BF16)


def attention_forward(x, w, tables, query_bias, value_bias, base):
    rows, width = x.shape
    pairs = query_bias.shape[0]
    sub = pairs // 2
    lanes = 2 * HEAD

    def column(part):
        return pl.BlockSpec((width, lanes), lambda g: (0, (g // sub) * (3 * sub) + part * sub + g % sub))

    def whole(shape):
        return pl.BlockSpec(shape, lambda g: (0,) * len(shape))

    bias = pl.BlockSpec((1, 1, lanes), lambda g: (g, 0, 0))
    heads = pl.BlockSpec((2, KEYS, lanes), lambda g: (g, 0, 0))
    return pl.pallas_call(
        attention_forward_kernel,
        grid=(pairs,),
        out_shape=[jax.ShapeDtypeStruct((2 * pairs, KEYS, lanes), BF16)] * 3
        + [jax.ShapeDtypeStruct((rows, pairs * lanes), BF16)],
        in_specs=[whole((rows, width)), column(0), column(1), column(2)]
        + [whole((rows, lanes))] * 3
        + [bias, bias, whole((KEYS, lanes))],
        out_specs=[heads, heads, heads, pl.BlockSpec((rows, lanes), lambda g: (0, g))],
        compiler_params=pltpu.CompilerParams(vmem_limit_bytes=48 * 2**20),
        name="attention_forward",
    )(x, w, w, w, *tables, query_bias, value_bias, base)


def attention_backward_kernel(
    sub, qa_ref, ka_ref, va_ref, do_ref, mix_ref, cos_ref, up_ref, down_ref,
    out_ref, sum_ref, da_ref, dq_ref, dk_ref, dv_ref,
):
    rows = do_ref.shape[0]
    lanes = 2 * HEAD
    tiles = rows // TILE
    lane = lax.broadcasted_iota(jnp.int32, (TILE, lanes), 1)
    low = lane < HEAD
    g = pl.program_id(0)

    da_ref[pl.ds(rows, KEYS - rows), :] = jnp.zeros((KEYS - rows, lanes), BF16)
    for h in range(2):

        @pl.loop(0, tiles)
        def _(t, h=h):
            here = pl.ds(pl.multiple_of(t * TILE, TILE), TILE)
            d = do_ref[here, :].astype(F32)
            mine = low if h == 0 else jnp.logical_not(low)
            delta = -jnp.sum(jnp.where(mine, d * mix_ref[here, :].astype(F32), 0.0), axis=1, keepdims=True)
            if h:
                d = pltpu.roll(d, HEAD, 1)
            first = delta.astype(BF16)
            left = delta - first.astype(F32)
            second = left.astype(BF16)
            third = (left - second.astype(F32)).astype(BF16)
            logs = jnp.where(
                lane == HEAD,
                first.astype(F32),
                jnp.where(lane == HEAD + 1, second.astype(F32), third.astype(F32)),
            )
            da_ref[here, :] = jnp.where(low, d, jnp.where(lane < HEAD + 3, logs, 0.0)).astype(BF16)

        dk_ref[h] = jnp.zeros((KEYS, lanes), F32)
        dv_ref[h] = jnp.zeros((KEYS, lanes), F32)

        @pl.loop(0, KEYS // COLS)
        def _(t, h=h):
            here = pl.ds(pl.multiple_of(t * COLS, COLS), COLS)
            q = qa_ref[h, here, :]
            d = da_ref[here, :]
            p = jnp.exp2(matmul_right_t(ka_ref[h], q))
            ds = (p * matmul_right_t(va_ref[h], d)).astype(BF16)
            dv_ref[h] += matmul(p.astype(BF16), d)
            dk_ref[h] += matmul(ds, q)
            dq_ref[h, here, :] = matmul_left_t(ds, ka_ref[h])

    def put(column, row, ref, factor, turn):
        total = jnp.zeros((1, lanes), F32)
        for t in range(tiles):
            here = pl.ds(t * TILE, TILE)
            value = jnp.where(low, ref[0, here, :], pltpu.roll(ref[1, here, :], HEAD, 1))
            if factor is not None:
                value = value * factor
            if turn:
                value = _turn(value, cos_ref[here, :], -up_ref[here, :], -down_ref[here, :])
            if row is not None:
                total = total + jnp.sum(value, axis=0, keepdims=True)
            at = pl.multiple_of(column * (sub * lanes) + lax.rem(g, sub) * lanes, lanes)
            out_ref[here, pl.ds(at, lanes)] = value.astype(BF16)
        if row is not None:
            sum_ref[0, pl.ds(row, 1), :] = total

    put(0, 0, dq_ref, SCALE, True)
    put(1, None, dk_ref, LN2, True)
    put(2, 1, dv_ref, None, False)


def attention_backward(qa, ka, va, d_mixed, mixed, tables):
    rows = mixed.shape[0]
    lanes = 2 * HEAD
    pairs = mixed.shape[1] // lanes
    sub = pairs // 2
    heads = pl.BlockSpec((2, KEYS, lanes), lambda g: (g, 0, 0))
    pair = pl.BlockSpec((rows, lanes), lambda g: (0, g))
    return pl.pallas_call(
        functools.partial(attention_backward_kernel, sub),
        grid=(pairs,),
        out_shape=[
            jax.ShapeDtypeStruct((rows, 3 * pairs * lanes), BF16),
            jax.ShapeDtypeStruct((pairs, 8, lanes), F32),
        ],
        in_specs=[heads, heads, heads, pair, pair]
        + [pl.BlockSpec((rows, lanes), lambda g: (0, 0))] * 3,
        out_specs=[
            pl.BlockSpec((rows, 3 * sub * lanes), lambda g: (0, g // sub)),
            pl.BlockSpec((1, 8, lanes), lambda g: (g, 0, 0)),
        ],
        scratch_shapes=[
            pltpu.VMEM((KEYS, lanes), BF16),
            pltpu.VMEM((2, KEYS, lanes), F32),
            pltpu.VMEM((2, KEYS, lanes), F32),
            pltpu.VMEM((2, KEYS, lanes), F32),
        ],
        compiler_params=pltpu.CompilerParams(vmem_limit_bytes=48 * 2**20),
        name="attention_backward",
    )(qa, ka, va, d_mixed, mixed, *tables)


def shards(
    tokens_in, cotangent, image_flag, key_mask, column_mask,
    attention_norm_gain, attention_norm_bias, w_query, w_key, w_value, query_bias, value_bias, w_out, out_bias,
    feedforward_norm_gain, feedforward_norm_bias, w_gate, gate_bias, w_up, up_bias, inner_gain, inner_shift,
    w_down, down_bias,
):
    n_dp, n_tensor = lax.axis_size("dp"), lax.axis_size("tensor")
    sizes = (n_dp, n_tensor)
    dp, z = lax.axis_index("dp"), lax.axis_index("tensor")
    core = dp % 2
    block = tokens_in.shape[1]
    width = tokens_in.shape[2]
    length = block * n_tensor
    block_pad = up_to(block, 8)
    rows = block_pad * n_tensor
    n_head = w_query.shape[1]
    n_ff = w_gate.shape[1]
    ff = up_to(n_ff, 16)
    count_live = float(FF - PADCOLS)
    swap = [(i, (i // n_tensor ^ 1) * n_tensor + i % n_tensor) for i in range(n_dp * n_tensor)]

    def other(value):
        return lax.ppermute(value, ("dp", "tensor"), swap)

    shard_qkv = jnp.concatenate([w_query, w_key, w_value], axis=1)
    kind_qkv = Kind(True, shard_qkv.shape, n_dp)
    kind_o = Kind(False, w_out.shape, n_dp)
    kind_f = Kind(False, (ff, w_down.shape[1]), n_dp)

    def pad_ff(vec):
        return jnp.pad(vec, (0, ff - n_ff))

    small = jnp.concatenate(
        [query_bias, value_bias]
        + [pad_ff(v) for v in (gate_bias, up_bias, inner_gain, inner_shift, column_mask.astype(F32))]
    )
    small_rows = up_to(up_to(small.shape[0], LANES) // LANES, 8)
    small = jnp.pad(small, (0, small_rows * LANES - small.shape[0])).reshape(small_rows, LANES)
    own_image = z % (n_tensor // 2)
    pair = jnp.concatenate(
        [
            lax.dynamic_index_in_dim(key_mask, own_image, 0, False).astype(F32),
            lax.dynamic_index_in_dim(image_flag, own_image, 0, True).astype(F32),
        ]
    )
    pair_rows = up_to(up_to(length + 1, LANES) // LANES, 8)
    pair = jnp.pad(pair, (0, pair_rows * LANES - pair.shape[0])).reshape(pair_rows, LANES)

    (image,), (packs,), (mask_flag,), (full_qkv,) = gather(
        [tokens_in], [small], [pair], [shard_qkv], [kind_qkv], sizes, 0
    )

    def turned(weight):
        return jnp.pad(weight.T, ((0, ff - n_ff), (0, 0)))

    (cot,), _, _, (full_g, full_u, full_o, full_d) = gather(
        [cotangent],
        [],
        [],
        [turned(w_gate), turned(w_up), w_out, jnp.pad(w_down, ((0, ff - n_ff), (0, 0)))],
        [kind_f, kind_f, kind_o, kind_f],
        sizes,
        1,
    )

    packs = packs.reshape(2, -1)
    cuts = [n_head] * 2 + [ff] * 5
    parts, at = [], 0
    for size in cuts:
        parts.append(packs[:, at : at + size].reshape(-1))
        at += size
    q_bias, v_bias, g_bias, u_bias, gain, shift, columns = parts
    mask_flag = mask_flag.reshape(-1)
    flag = mask_flag[length]

    def padded(value):
        return jnp.pad(value, ((0, 0), (0, block_pad - block), (0, 0))).reshape(rows, -1)

    def unpadded(value):
        return value.reshape(n_tensor, block_pad, width)[:, :block]

    live = padded(mask_flag[:length].reshape(n_tensor, block, 1)).reshape(rows)
    live = jnp.pad(live, (0, KEYS - rows))
    lane = jnp.arange(LANES)[None, :]
    base = jnp.where(
        lane == HEAD,
        jnp.where(live > 0, 0.0, -1e30)[:, None],
        jnp.where((lane > HEAD) & (lane <= HEAD + 3), 1.0, 0.0),
    ).astype(BF16)
    tables = lane_tables(length, HEAD // 4, block, block_pad)

    token_rows = padded(image).astype(F32)
    xhat1, s1 = norm_pieces(token_rows)
    normed = (xhat1 * attention_norm_gain + attention_norm_bias).astype(BF16)
    pairs = 2 * n_head // (2 * HEAD)
    qa, ka, va, mixed = attention_forward(
        normed, full_qkv, tables, q_bias.reshape(pairs, 1, 2 * HEAD), v_bias.reshape(pairs, 1, 2 * HEAD), base
    )
    part = matmul(mixed, full_o).astype(BF16)
    middle = token_rows + (part.astype(F32) + other(part).astype(F32)) + out_bias
    xhat2, s2 = norm_pieces(middle)
    normed2 = (xhat2 * feedforward_norm_gain + feedforward_norm_bias).astype(BF16)
    gate = matmul_right_t(normed2, full_g) + g_bias
    up = matmul_right_t(normed2, full_u) + u_bias
    sig = jax.nn.sigmoid(gate)
    act = gate * sig * up
    sums = jnp.stack([jnp.sum(act * columns, axis=-1), jnp.sum(act * act * columns, axis=-1)])
    sums = sums + other(sums)
    mean = sums[0][:, None] / count_live
    var = sums[1][:, None] / count_live - mean * mean
    r = lax.rsqrt(var + EPS)
    nhat = (act - mean) * r
    hidden = (columns * (nhat * gain + shift)).astype(BF16)
    part = matmul(hidden, full_d).astype(BF16)
    output = (middle + (part.astype(F32) + other(part).astype(F32)) + down_bias).astype(BF16)

    grad = padded(cot).astype(F32) * flag
    grad_low = grad.astype(BF16)
    g_down = matmul_left_t(hidden, grad_low).astype(BF16)
    dn = columns * lax.dot_general(
        grad_low, full_d, (((1,), (1,)), ((), ())), preferred_element_type=F32
    )
    g_gain = jnp.sum(dn * nhat, axis=0)
    g_shift = jnp.sum(dn, axis=0)
    dnh = dn * gain
    back = jnp.stack([jnp.sum(dnh, axis=-1), jnp.sum(dnh * nhat, axis=-1)])
    back = back + other(back)
    dact = r * (dnh - columns * (back[0][:, None] + nhat * back[1][:, None]) / count_live)
    dgate = dact * up * sig * (1.0 + gate * (1.0 - sig))
    dup = dact * gate * sig
    g_gate_bias = jnp.sum(dgate, axis=0)
    g_up_bias = jnp.sum(dup, axis=0)
    gate_low = dgate.astype(BF16)
    up_low = dup.astype(BF16)
    g_gate = matmul_left_t(gate_low, normed2).astype(BF16)
    g_up = matmul_left_t(up_low, normed2).astype(BF16)
    part = (matmul(gate_low, full_g) + matmul(up_low, full_u)).astype(BF16)
    dnormed2 = part.astype(F32) + other(part).astype(F32)
    g_mlp_gain = jnp.sum(dnormed2 * xhat2, axis=0)
    g_mlp_shift = jnp.sum(dnormed2, axis=0)
    dmiddle = grad + norm_backward(dnormed2, xhat2, s2, feedforward_norm_gain)
    g_out_bias = jnp.sum(dmiddle, axis=0)
    g_down_bias = jnp.sum(grad, axis=0)
    dmid_low = dmiddle.astype(BF16)
    g_out = matmul_left_t(mixed, dmid_low).astype(BF16)
    d_mixed = matmul_right_t(dmid_low, full_o).astype(BF16)
    d_qkv, qv_sums = attention_backward(qa, ka, va, d_mixed, mixed, tables)
    g_qkv = matmul_left_t(normed, d_qkv).astype(BF16)
    part = matmul_right_t(d_qkv, full_qkv).astype(BF16)
    dnormed = part.astype(F32) + other(part).astype(F32)
    g_attn_gain = jnp.sum(dnormed * xhat1, axis=0)
    g_attn_shift = jnp.sum(dnormed, axis=0)
    input_grad = dmiddle + norm_backward(dnormed, xhat1, s1, attention_norm_gain)

    def by_slot(vec):
        return vec.reshape(2, -1)

    vec = jnp.concatenate(
        [g_attn_gain, g_attn_shift, g_out_bias, g_mlp_gain, g_mlp_shift, g_down_bias]
        + [
            jnp.concatenate(
                [by_slot(v) for v in (qv_sums[:, 0], qv_sums[:, 1], g_gate_bias, g_up_bias, g_gain, g_shift)], axis=1
            ).reshape(-1)
        ]
    )
    vec_size = vec.shape[0]
    vec_rows = up_to(up_to(vec_size, LANES) // LANES, 8)
    vec = jnp.pad(vec, (0, vec_rows * LANES - vec_size)).reshape(vec_rows, LANES)
    (out_rows, in_rows), vec, (s_down, s_gate, s_up, s_out, s_qkv) = scatter(
        [unpadded(output), unpadded(input_grad.astype(BF16))],
        vec,
        [g_down, g_gate, g_up, g_out, g_qkv],
        [kind_f, kind_f, kind_f, kind_o, kind_qkv],
        sizes,
        2,
    )
    vec = vec.reshape(2, -1)
    wide = vec[0, : 6 * width].reshape(6, width)
    owner = z // (n_tensor // 2)
    tall = lax.dynamic_index_in_dim(vec, owner, 0, False)[6 * width : vec_size].reshape(2, -1)
    tall = lax.dynamic_index_in_dim(tall, z % (n_tensor // 2), 0, False)
    pieces, at = [], 0
    for size in [n_head] * 2 + [ff] * 4:
        pieces.append(tall[at : at + size])
        at += size
    return (
        out_rows,
        in_rows.astype(F32),
        wide[0],
        wide[1],
        s_qkv[:, :n_head],
        s_qkv[:, n_head : 2 * n_head],
        s_qkv[:, 2 * n_head :],
        pieces[0],
        pieces[1],
        s_out,
        wide[2],
        wide[3],
        wide[4],
        s_gate[:n_ff].T,
        pieces[2][:n_ff],
        s_up[:n_ff].T,
        pieces[3][:n_ff],
        pieces[4][:n_ff],
        pieces[5][:n_ff],
        s_down[:n_ff],
        wide[5],
    )


def solution(mesh):
    act, row, col, vec = P("dp", "tensor", None), P("dp", "tensor"), P("tensor", "dp"), P("tensor")
    in_specs = (
        act, act, P("dp"), P("dp", None), vec, P(), P(), row, row, row, vec, vec, col, P(), P(), P(),
        row, vec, row, vec, vec, vec, col, P(),
    )
    out_specs = (
        act, act, P(), P(), row, row, row, vec, vec, col, P(), P(), P(), row, vec, row, vec, vec, vec, col, P(),
    )
    return jax.shard_map(shards, mesh=mesh, in_specs=in_specs, out_specs=out_specs, check_vma=False)
```

time: 1430 us -> 584 us (0.41)
  waiting for transfers between devices: 571 us -> 0.76 us
  Pallas kernels: 0 us -> 378 us
  blocking collectives: 375 us -> 0 us
  matrix products: 236 us -> 79.8 us
  local copies, waits for them, and re-layouts: 118 us -> 45.1 us
  other arithmetic: 89.2 us -> 61.1 us
  between operations: 18.7 us -> 2.76 us
    pallas_call x0 -> x5, Pallas kernels: none -> 378 us  [the longest x2 168 us: gather(): pl.pallas_call(functools.partial(gather_kernel, kinds, n_a, n_k, n_q, siz...]
    reduce_scatter x7 -> x0, waiting for transfers between devices: 303 us -> none  [the longest x1 49.7 us: shards(): lax.psum_scatter(totals[5], 'dp', scatter_dimension=0, tiled=True)]
    unnamed x3 -> x0, blocking collectives: 297 us -> none
    all_gather x11 -> x0, waiting for transfers between devices: 196 us -> none  [the longest x2 74.3 us: shards(): lax.all_gather(normed_second_rows, 'tensor', axis=0, tiled=True)]
    dot_general x26 -> x5, matrix products: 148 us -> 27.4 us  [the longest x4 16.2 us: matmul(): return jnp.dot(left, right, preferred_element_type=F32)]
    psum x1 -> x0, waiting for transfers between devices: 66.8 us -> none  [shards(): lax.psum((totals[7], totals[8], totals[9], totals[10], totals[11], totals...]
    unnamed x363 -> x139, local copies, waits for them, and re-layouts: 86.2 us -> 24.3 us
    all_gather x4 -> x0, blocking collectives: 43.1 us -> none  [the longest x1 11.3 us: fetch_weights(): lax.all_gather(w_query, 'dp', axis=0, tiled=True)]
  transfers between devices with their start and end apart: 27 -> 6, of which waited for: 16 -> 1; matrix products, arithmetic and copies ran while one was open for 24% -> 9% of each run, Pallas kernels for 0% -> 0%
where the time goes in v1:
time: 584 us; the launch traced here: 574 us
  Pallas kernels  378 us (65%)
  matrix products  79.8 us (14%)
  other arithmetic  61.1 us (10%)
  local copies, waits for them, and re-layouts  45.1 us (8%)
  starting transfers between devices  6.75 us (1%)
    pallas_call x2, Pallas kernels, gather(): pl.pallas_call(functools.partial(gather_kernel, kinds, n_a, n_k, n_q, siz...  168 us
    pallas_call x1, Pallas kernels, scatter(): pl.pallas_call(functools.partial(scatter_kernel, kinds, n_a, sizes), out_...  130 us
    pallas_call x1, Pallas kernels, attention_backward(): pl.pallas_call(functools.partial(attention_backward_kernel, sub), grid=(p...  44.1 us
    pallas_call x1, Pallas kernels, attention_forward(): pl.pallas_call(attention_forward_kernel, grid=(pairs,), out_shape=[jax.Sh...  35.6 us
    dot_general x5, matrix products, matmul_left_t(): lax.dot_general(left, right, (((0,), (0,)), ((), ())), preferred_element_...  32.2 us
    unnamed x139, local copies, waits for them, and re-layouts  24.3 us
    dot_general x4, matrix products, matmul_right_t(): lax.dot_general(left, right, (((1,), (1,)), ((), ())), preferred_element_...  20.3 us
    dot_general x4, matrix products, matmul(): return jnp.dot(left, right, preferred_element_type=F32)  16.2 us
  transfers between devices with their start and end apart: 6, of which 1 were waited for; matrix products, arithmetic and copies ran while one was open for 9% of the time, Pallas kernels for 0%

profile of v1, /device:TPU:0, one launch (start us, length us, event | category | flops | bytes accessed | tf_op | source)
XLA Modules:
  0.0 574.0 jit_solution(11505862139849053649)
XLA Ops:
  13.1 63.8 %gather0.1 = (bf16[4,257,1024]{2,1,0:T(8,128)(2,1)}, f32[2,32,128]{2,1,0:T(8,128)}, f32[16,128]{1,0:T(8,128)}, bf16[1024,1536]{1,0:T(8,128)(2,1)}) custom-call(bf16[2,257,1024]{2,1,0:T(8,128)(2,1)} %copy.53.refs_0_, f32[32,128]{1,0:T(8,128)} %pad_bitcast_fusion.1.refs_1_, f32[16,128]{1,0:T(8,128)} %fusion.31.refs_2_, bf16[128,768]{1,0:T(8,128)(2,1)} %pad_maximum_fusion.refs_3_), custom_call_target="tpu_custom_call" | custom-call | tf_op jit(solution)/shard_map/gather0/pallas_call | solution.py:408
  100.8 4.0 fusion.2
  104.7 103.9 %gather1.1 = (bf16[4,257,1024]{2,1,0:T(8,128)(2,1)}, bf16[1376,1024]{1,0:T(8,128)(2,1)}, bf16[1376,1024]{1,0:T(8,128)(2,1)}, bf16[512,1024]{1,0:T(8,128)(2,1)}, bf16[1376,1024]{1,0:T(8,128)(2,1)}) custom-call(bf16[2,257,1024]{2,1,0:T(8,128)(2,1)} %copy.57.refs_0_, bf16[688,128]{1,0:T(8,128)(2,1)} %pad.76.refs_1_, bf16[688,128]{1,0:T(8,128)(2,1)} %pad.77.refs_2_, ...), custom_call_target="tpu_custom_call" | custom-call | tf_op jit(solution)/shard_map/gather1/pallas_call | solution.py:408
  209.7 35.6 %attention_forward.1 = (bf16[8,1152,128]{2,1,0:T(8,128)(2,1)}, bf16[8,1152,128]{2,1,0:T(8,128)(2,1)}, bf16[8,1152,128]{2,1,0:T(8,128)(2,1)}, bf16[1056,512]{1,0:T(8,128)(2,1)S(1)}) custom-call(bf16[1056,1024]{1,0:T(8,128)(2,1)S(1)} %get-tuple-element.167.x_ref, bf16[1024,1536]{1,0:T(8,128)(2,1)} %get-tuple-element.45.wq_ref.wk_ref.wv_ref, ...), custom_call_target="tpu_custom_call" | custom-call | tf_op jit(solution)/shard_map/attention_forward/pallas_call | solution.py:769
  247.9 5.3 collective-permute-start
  257.9 5.2 bitcast_add_fusion.1
  270.1 8.4 %multiply_reduce_fusion.3 = (f32[1056]{0:T(1024)S(1)}, f32[1056]{0:T(1024)S(1)}, f32[1056,1376]{1,0:T(8,128)}, f32[1056,1376]{1,0:T(8,128)}) fusion(f32[1376]{0:T(1024)S(1)} %mul.244, f32[1056,1376]{1,0:T(8,128)S(1)} %convolution_add_fusion.1, f32[1376]{0:T(1024)S(1)} %add.230, bf16[1056,1024]{1,0:T(8,128)(2,1)S(1)} %add_convert_fusion.2, ...), kind=kOutput, calls=%fused_computation.11 | convolution fusion | flops 2991840256 | bytes 22436864 | tf_op jit(solution)/shard_map/dot_general | solution.py:80
  280.5 11.2 %multiply_reduce_fusion = (f32[1376]{0:T(1024)S(1)}, f32[1056]{0:T(1024)S(1)}, f32[1056]{0:T(1024)S(1)}, f32[1376]{0:T(1024)S(1)}, f32[1056,1376]{1,0:T(8,128)}) fusion(f32[1056,1376]{1,0:T(8,128)} %get-tuple-element.162, f32[1056]{0:T(1024)S(1)} %add_rsqrt_fusion, f32[1056]{0:T(1024)S(1)} %get-tuple-element.154, f32[1376]{0:T(1024)S(1)} %mul.258, ...), kind=kOutput, calls=%fused_computation.3 | convolution fusion | flops 2990384640 | bytes 16644096 | tf_op jit(solution)/shard_map/dot_general | solution.py:1001
  293.2 10.7 %fusion.41 = (f32[1376]{0:T(1024)S(1)}, bf16[1056,1376]{1,0:T(8,128)(2,1)S(1)}, f32[1376]{0:T(1024)S(1)}, bf16[1056,1376]{1,0:T(8,128)(2,1)S(1)}) fusion(f32[1056,1376]{1,0:T(8,128)} %copy-done.12, f32[1056]{0:T(1024)S(1)} %get-tuple-element.153, f32[1056,1376]{1,0:T(8,128)} %get-tuple-element.162, f32[1056]{0:T(1024)S(1)} %get-tuple-element.154, ...), kind=kLoop, calls=%fused_computation.161 | loop fusion | flops 34870592 | bytes 29100032 | tf_op jit(solution)/shard_map/reduce_sum | solution.py:1013
  307.8 4.8 fusion.7
  313.0 5.2 convolution_convert_fusion
  318.4 6.4 %convolution_convert_fusion.4.refs_3_ = bf16[1376,1024]{1,0:T(8,128)(2,1)} fusion(bf16[1056,1024]{1,0:T(8,128)(2,1)S(1)} %copy-done.16, f32[1056,1376]{1,0:T(8,128)S(1)} %bitcast.93, f32[1376]{0:T(1024)S(1)} %add.235, f32[1376]{0:T(1024)S(1)} %mul.258, f32[1056]{0:T(1024)S(1)} %add_rsqrt_fusion, f32[1056]{0:T(1024)S(1)} %get-tuple-element.154, ...), kind=kOutput, calls=%fused_computation.46 | convolution fusion | flops 2985986048 | bytes 10817920 | tf_op jit(solution)/shard_map/dot_general | solution.py:84
  325.1 7.9 %convolution_convert_fusion.3.refs_4_ = bf16[1376,1024]{1,0:T(8,128)(2,1)} fusion(bf16[1056,1024]{1,0:T(8,128)(2,1)} %copy-done.17, bf16[1056,1376]{1,0:T(8,128)(2,1)} %copy-done.15), kind=kOutput, calls=%fused_computation.45 | convolution fusion | flops 2977267712 | bytes 7886848 | tf_op jit(solution)/shard_map/dot_general | solution.py:84
  333.0 5.2 multiply_reduce_fusion.5
  338.3 8.7 %fusion.43 = (f32[1024]{0:T(1024)S(1)}, f32[1056,1024]{1,0:T(8,128)S(1)}, bf16[1056,1024]{1,0:T(8,128)(2,1)}) fusion(f32[1056]{0:T(1024)S(1)} %broadcast_multiply_fusion.4, f32[1056]{0:T(1024)S(1)} %broadcast_multiply_fusion.6, f32[1056,1024]{1,0:T(8,128)} %copy-done.6, f32[1024]{0:T(1024)S(1)} %copy-done.34, f32[1056]{0:T(1024)S(1)} %broadcast_multiply_fusion.5, ...), kind=kLoop, calls=%fused_computation.163 | loop fusion | flops 20544512 | bytes 23822848 | tf_op jit(solution)/shard_map/reduce_sum | solution.py:1023
  350.7 44.1 %attention_backward.1 = (bf16[1056,1536]{1,0:T(8,128)(2,1)}, f32[4,8,128]{2,1,0:T(8,128)S(1)}) custom-call(bf16[8,1152,128]{2,1,0:T(8,128)(2,1)S(1)} %copy-done.2, bf16[8,1152,128]{2,1,0:T(8,128)(2,1)} %get-tuple-element.55.ka_ref, bf16[8,1152,128]{2,1,0:T(8,128)(2,1)} %get-tuple-element.56.va_ref, bf16[1056,512]{1,0:T(8,128)(2,1)S(1)} %convolution_convert_fusion.7.do_ref, ...), custom_call_target="tpu_custom_call" | custom-call | tf_op jit(solution)/shard_map/attention_backward/pallas_call | solution.py:858
  394.8 6.9 %convolution_convert_fusion.6 = bf16[1056,1024]{1,0:T(8,128)(2,1)} fusion(bf16[1056,1536]{1,0:T(8,128)(2,1)} %get-tuple-element.57, bf16[1024,1536]{1,0:T(8,128)(2,1)S(1)} %copy-done.10), kind=kOutput, calls=%fused_computation.49 | convolution fusion | flops 3322970112 | bytes 8552448 | tf_op jit(solution)/shard_map/dot_general | solution.py:80
  402.0 5.2 convolution_convert_fusion.2.refs_5_
  407.5 4.9 convolution_convert_fusion.8.refs_6_
  412.4 7.7 %convolution_convert_fusion.5.refs_7_ = bf16[1024,1536]{1,0:T(8,128)(2,1)} fusion(bf16[1056,1024]{1,0:T(8,128)(2,1)S(1)} %get-tuple-element.167.x_ref, bf16[1056,1536]{1,0:T(8,128)(2,1)} %get-tuple-element.57), kind=kOutput, calls=%fused_computation.48 | convolution fusion | flops 3323461632 | bytes 8552448 | tf_op jit(solution)/shard_map/dot_general | solution.py:84
  420.2 4.5 fusion.5
  425.5 4.8 add_convert_fusion
  430.2 130.3 %scatter2.1 = (bf16[2,257,1024]{2,1,0:T(8,128)(2,1)}, bf16[2,257,1024]{2,1,0:T(8,128)(2,1)}, f32[2,104,128]{2,1,0:T(8,128)}, f32[688,128]{1,0:T(8,128)}, f32[688...) custom-call(bf16[4,257,1024]{2,1,0:T(8,128)(2,1)} %bitcast.90, ...), custom_call_target="tpu_custom_call" | custom-call | tf_op jit(solution)/shard_map/scatter2/pallas_call | solution.py:643
  564.0 3.6 copy.59
  (253 shorter events, 72.9 us)
Async XLA Ops:
  0.7 80.7 %copy-start.19 = (bf16[2,257,1024]{2,0,1:T(2,128)(2,1)S(1)}, bf16[2,257,1024]{2,0,1:T(2,128)(2,1)}, u32[]{:S(2)}) copy-start(bf16[2,257,1024]{2,0,1:T(2,128)(2,1)} %param.25) | copy-start | bytes 3158020
  3.3 79.4 %copy-start.24 = (bf16[128,684]{0,1:T(8,128)(2,1)S(1)}, bf16[128,684]{0,1:T(8,128)(2,1)}, u32[]{:S(2)}) copy-start(bf16[128,684]{0,1:T(8,128)(2,1)} %param.40) | copy-start | bytes 525316
  11.4 71.9 %copy-start.25 = (bf16[128,684]{0,1:T(8,128)(2,1)S(1)}, bf16[128,684]{0,1:T(8,128)(2,1)}, u32[]{:S(2)}) copy-start(bf16[128,684]{0,1:T(8,128)(2,1)} %param.42) | copy-start | bytes 525316
  13.1 71.0 %copy-start.26 = (bf16[684,128]{1,0:T(8,128)(2,1)S(1)}, bf16[684,128]{1,0:T(8,128)(2,1)}, u32[]{:S(2)}) copy-start(bf16[684,128]{1,0:T(8,128)(2,1)} %param.46) | copy-start | bytes 525316
  81.3 19.4 %copy-start.30 = (f32[1056]{0:T(1024)}, f32[1056]{0:T(1024)S(1)}, u32[]{:S(2)}) copy-start(f32[1056]{0:T(1024)S(1)} %div.67) | copy-start | bytes 12676
  209.7 35.6 %copy-start.46 = (bf16[512,1024]{1,0:T(8,128)(2,1)S(1)}, bf16[512,1024]{1,0:T(8,128)(2,1)}, u32[]{:S(2)}) copy-start(bf16[512,1024]{1,0:T(8,128)(2,1)} %get-tuple-element.49) | copy-start | bytes 3145732
  245.3 9.2 %copy-start.28 = (f32[1,2,32,128]{3,1,2,0:T(2,128)S(1)}, f32[1,2,32,128]{3,1,2,0:T(2,128)}, u32[]{:S(2)}) copy-start(f32[1,2,32,128]{3,1,2,0:T(2,128)} %copy-done.27) | copy-start | bytes 98308
  247.9 10.0 %collective-permute-start = (bf16[1056,1024]{1,0:T(8,128)(2,1)}, bf16[1056,1024]{1,0:T(8,128)(2,1)}, u32[]{:S(2)}, u32[]{:S(2)}) collective-permute-start(bf16[1056,1024]{1,0:T(8,128)(2,1)} %convolution_convert_fusion.1), channel_id=1, source_target_pairs={{0,4},{1,5},{2,6},{3,7},{4,0},{5,1},{6,2},{7,3},{8,12},{9,13},{10,... | collective-permute-start | bytes 6488072 | tf_op jit(solution)/shard_map/ppermute | solution.py:904
  257.9 20.8 %copy-start.9 = (f32[4,264,1024]{2,1,0:T(8,128)}, f32[4,264,1024]{2,1,0:T(8,128)S(1)}, u32[]{:S(2)}) copy-start(f32[4,264,1024]{2,1,0:T(8,128)S(1)} %get-tuple-element.169) | copy-start | bytes 12976132
  278.6 1.8 collective-permute-start.1
  291.7 1.4 collective-permute-start.3
  293.2 10.7 %copy-start.45 = (bf16[1376,1024]{1,0:T(8,128)(2,1)S(1)}, bf16[1376,1024]{1,0:T(8,128)(2,1)}, u32[]{:S(2)}) copy-start(bf16[1376,1024]{1,0:T(8,128)(2,1)} %get-tuple-element.50) | copy-start | bytes 8454148
  303.9 9.1 %slice-start.4 = ((s8[5947392]{0:T(1024)(128)(4,1)}), s8[4194304]{0:T(1024)(128)(4,1)S(1)}, s32[]{:S(2)}) async-start(s8[5947392]{0:T(1024)(128)(4,1)} %bitcast.92), calls=%async_computation.4 | async-start | bytes 8388608
  312.6 20.4 %collective-permute-start.4 = (bf16[1056,1024]{1,0:T(8,128)(2,1)}, bf16[1056,1024]{1,0:T(8,128)(2,1)}, u32[]{:S(2)}, u32[]{:S(2)}) collective-permute-start(bf16[1056,1024]{1,0:T(8,128)(2,1)} %fusion.7), channel_id=1, source_target_pairs={{0,4},{1,5},{2,6},{3,7},{4,0},{5,1},{6,2},{7,3},{8,12},{9,13},{10,... | collective-permute-start | bytes 6488072 | tf_op jit(solution)/shard_map/ppermute | solution.py:904
  318.2 20.1 %collective-permute-start.2 = (bf16[1056,1024]{1,0:T(8,128)(2,1)}, bf16[1056,1024]{1,0:T(8,128)(2,1)}, u32[]{:S(2)}, u32[]{:S(2)}) collective-permute-start(bf16[1056,1024]{1,0:T(8,128)(2,1)} %convolution_convert_fusion), channel_id=1, source_target_pairs={{0,4},{1,5},{2,6},{3,7},{4,0},{5,1},{6,2},{7,3},{8,12},{9,13},{10,... | collective-permute-start | bytes 6488072 | tf_op jit(solution)/shard_map/ppermute | solution.py:904
  338.3 8.8 %copy-start.47 = (bf16[512,1024]{1,0:T(8,128)(2,1)S(1)}, bf16[512,1024]{1,0:T(8,128)(2,1)}, u32[]{:S(2)}) copy-start(bf16[512,1024]{1,0:T(8,128)(2,1)} %get-tuple-element.49) | copy-start | bytes 3145732
  350.7 44.1 %copy-start.10 = (bf16[1024,1536]{1,0:T(8,128)(2,1)S(1)}, bf16[1024,1536]{1,0:T(8,128)(2,1)}, u32[]{:S(2)}) copy-start(bf16[1024,1536]{1,0:T(8,128)(2,1)} %get-tuple-element.45.wq_ref.wk_ref.wv_ref) | copy-start | bytes 9437188
  401.7 18.5 %collective-permute-start.5 = (bf16[1056,1024]{1,0:T(8,128)(2,1)}, bf16[1056,1024]{1,0:T(8,128)(2,1)}, u32[]{:S(2)}, u32[]{:S(2)}) collective-permute-start(bf16[1056,1024]{1,0:T(8,128)(2,1)} %convolution_convert_fusion.6), channel_id=1, source_target_pairs={{0,4},{1,5},{2,6},{3,7},{4,0},{5,1},{6,2},{7,3},{8,12},{9,13},{10,... | collective-permute-start | bytes 6488072 | tf_op jit(solution)/shard_map/ppermute | solution.py:904
  407.5 12.7 %slice-start.2 = ((s8[4325376]{0:T(1024)(128)(4,1)}), s8[4194304]{0:T(1024)(128)(4,1)S(1)}, s32[]{:S(2)}) async-start(s8[4325376]{0:T(1024)(128)(4,1)} %bitcast.88), calls=%async_computation.2 | async-start | bytes 8388608
  407.5 17.9 %slice-start = ((s8[4325376]{0:T(1024)(128)(4,1)}), s8[4194304]{0:T(1024)(128)(4,1)S(1)}, s32[]{:S(2)}) async-start(s8[4325376]{0:T(1024)(128)(4,1)} %bitcast.86), calls=%async_computation | async-start | bytes 8388608
  412.4 13.0 %slice-start.1 = ((s8[4325376]{0:T(1024)(128)(4,1)}), s8[131072]{0:T(1024)(128)(4,1)S(1)}, s32[]{:S(2)}) async-start(s8[4325376]{0:T(1024)(128)(4,1)} %bitcast.86), calls=%async_computation.1 | async-start | bytes 262144
  560.6 9.5 %copy-start.22 = (f32[688,128]{1,0:T(8,128)S(1)}, f32[688,128]{1,0:T(8,128)}, u32[]{:S(2)}) copy-start(f32[688,128]{1,0:T(8,128)} %get-tuple-element.65) | copy-start | bytes 1056772
  560.6 11.6 %copy-start.29 = (f32[256,128]{1,0:T(8,128)S(1)}, f32[256,128]{1,0:T(8,128)}, u32[]{:S(2)}) copy-start(f32[256,128]{1,0:T(8,128)} %get-tuple-element.231) | copy-start | bytes 393220
  560.6 12.3 %copy-start.21 = (f32[688,128]{1,0:T(8,128)S(1)}, f32[688,128]{1,0:T(8,128)}, u32[]{:S(2)}) copy-start(f32[688,128]{1,0:T(8,128)} %get-tuple-element.66) | copy-start | bytes 1056772
  (36 other events, 179.3 us)

commit v2 on v1

--- a/solution.py
+++ b/solution.py
@@ -189,198 +189,204 @@
     return lax.bitwise_xor(chip, value)
 
 
-def gather_kernel(kinds, n_acts, n_packs, n_pairs, sizes, *refs):
-    n_dp, n_tensor = sizes
-    n_w = len(kinds)
-    me = Place(n_dp, n_tensor)
-    at = 0
-    groups = []
-    for count in (n_acts, n_packs, n_pairs, n_w) * 2:
-        groups.append(refs[at : at + count])
-        at += count
-    act_in, pack_in, pair_in, w_in, act_out, pack_out, pair_out, w_out = groups
-    (a_send, a_recv, a_fwd, a_back, k_send, k_recv, q_send, q_recv, s_send, s_recv, z_send, z_recv, b_send, b_recv, loc) = refs[at:]
-    half_z = n_tensor // 2
-    me.barrier()
-
-    def local(src, dst, n):
-        return pltpu.make_async_copy(src, dst, loc.at[n])
-
-    for j, kind in enumerate(kinds):
-        mine = kind.one(w_out[j], me.slot, me.chip, me.core)
-
-        @pl.when(me.home)
-        def _(j=j, mine=mine):
-            local(w_in[j], mine, j).start()
-
-        @pl.when(jnp.logical_not(me.home))
-        def _(j=j, mine=mine):
-            remote(w_in[j], mine, s_send.at[j], s_recv.at[j], me.across()).start()
-
-    def act_copy(n, i):
-        target = half_z * me.core + i
+class Gather:
+    def __init__(self, me, kinds, w_in, w_out, sems):
+        self.me, self.kinds, self.w_in, self.w_out = me, kinds, w_in, w_out
+        self.s_send, self.s_recv, self.z_send, self.z_recv, self.b_send, self.b_recv, self.loc = sems
+
+    @staticmethod
+    def semaphores(n_w, sizes):
+        dma = pltpu.SemaphoreType.DMA
+        bits = (sizes[0] // 2).bit_length() - 1
+        most = max(1 << max(bits - 1, 0), 1)
+        return [
+            dma((n_w,)),
+            dma((n_w,)),
+            dma((n_w, sizes[1])),
+            dma((n_w, 2)),
+            dma((n_w, bits, 2, most)),
+            dma((n_w, bits, 2, most)),
+            dma((n_w,)),
+        ]
+
+    def _hop(self, j):
+        me = self.me
+        mine = self.kinds[j].one(self.w_out[j], me.slot, me.chip, me.core)
+        return (
+            pltpu.make_async_copy(self.w_in[j], mine, self.loc.at[j]),
+            remote(self.w_in[j], mine, self.s_send.at[j], self.s_recv.at[j], me.across()),
+        )
+
+    def first_hop(self, j):
+        stay, leave = self._hop(j)
+        pl.when(self.me.home)(stay.start)
+        pl.when(jnp.logical_not(self.me.home))(leave.start)
+
+    def _along(self, j, s):
+        me = self.me
+        src = self.kinds[j].piece(self.w_out[j], me.slot, me.chip)
+        return remote(src, src, self.z_send.at[j, s - 1], self.z_recv.at[j, me.slot], me.shifted(s))
+
+    def start_z(self, j):
+        @pl.when(self.me.home)
+        def _():
+            stay, leave = self._hop(j)
+            stay.wait()
+            leave.wait_recv()
+            for s in range(1, self.me.nz):
+                self._along(j, s).start()
+
+    def wait_z(self, j):
+        me = self.me
+        for slot in range(2):
+            src = self.kinds[j].piece(self.w_out[j], slot, me.chip)
+            copy = remote(src, src, self.z_send.at[j, 0], self.z_recv.at[j, slot], me.across())
+            pl.when(me.core * (me.nz // 2) + slot != me.z)(copy.wait_recv)
+
+    def _bits(self, j, step, slot):
+        me = self.me
+        bit = step if slot == 0 else me.bits - 1 - step
+        low = 1 if slot == 0 else 1 << (me.bits - step)
+
+        def send(m):
+            src = self.kinds[j].piece(self.w_out[j], slot, flipped(me.chip, m * low))
+            return remote(
+                src, src, self.b_send.at[j, step, slot, m], self.b_recv.at[j, step, slot, m], me.beside(bit)
+            )
+
+        return send
+
+    def start_bits(self, j, step):
+        for slot in range(2):
+            send = self._bits(j, step, slot)
+            _each(1 << step, lambda m: send(m).start())
+
+    def wait_bits(self, j, step):
+        for slot in range(2):
+            send = self._bits(j, step, slot)
+            _each(1 << step, lambda m: send(m).wait_recv())
+
+    def finish(self, j):
+        me = self.me
+        pl.when(jnp.logical_not(me.home))(self._hop(j)[1].wait_send)
+        for s in range(1, me.nz):
+            pl.when(me.home)(self._along(j, s).wait_send)
+        for step in range(me.bits):
+            for slot in range(2):
+                send = self._bits(j, step, slot)
+                _each(1 << step, lambda m: send(m).wait_send())
+
+
+class Inward:
+    def __init__(self, me, src, dst, sems):
+        self.me, self.src, self.dst = me, src, dst
+        self.send, self.recv, self.fwd, self.back, self.loc = sems
+
+    @staticmethod
+    def semaphores(sizes):
+        dma = pltpu.SemaphoreType.DMA
+        return [dma((sizes[1],)), dma((sizes[1],)), dma((sizes[1],)), dma((sizes[1],)), dma((1,))]
+
+    def _copy(self, i):
+        me = self.me
+        target = me.nz // 2 * me.core + i
         return target, remote(
-            act_in[n].at[i], act_out[n].at[me.z], a_send.at[n, i], a_recv.at[n, me.z], (me.dp, target)
+            self.src.at[i], self.dst.at[me.z], self.send.at[i], self.recv.at[me.z], (me.dp, target)
         )
 
-    def start_acts(n):
-        for i in range(half_z):
-            target, copy = act_copy(n, i)
-            pl.when(target != me.z)(copy.start)
-
-            @pl.when(target == me.z)
-            def _(n=n, i=i):
-                local(act_in[n].at[i], act_out[n].at[me.z], n_w + n).start()
-
-    def pass_acts(n):
+    def _stay(self, i):
+        return pltpu.make_async_copy(self.src.at[i], self.dst.at[self.me.z], self.loc.at[0])
+
+    def _onward(self, place):
+        slab = self.dst.at[place]
+        return remote(slab, slab, self.fwd.at[place], self.back.at[place], self.me.across())
+
+    def start(self):
+        for i in range(self.me.nz // 2):
+            target, copy = self._copy(i)
+            pl.when(target != self.me.z)(copy.start)
+            pl.when(target == self.me.z)(self._stay(i).start)
+
+    def pass_on(self):
+        me = self.me
+
         @pl.when(me.home)
         def _():
-            for s in range(n_tensor):
-                src = lax.rem(me.z + s, n_tensor)
-                slab = act_out[n].at[src]
+            for s in range(me.nz):
+                place = lax.rem(me.z + s, me.nz)
                 if s == 0:
-                    local(slab, slab, n_w + n).wait()
+                    self._stay(0).wait()
                 else:
-                    remote(slab, slab, a_send.at[n, 0], a_recv.at[n, src], me.across()).wait_recv()
-                remote(slab, slab, a_fwd.at[n, src], a_back.at[n, src], me.across()).start()
-
-    def end_acts(n):
-        for i in range(half_z):
-            target, copy = act_copy(n, i)
-            pl.when(target != me.z)(copy.wait_send)
-        for src in range(n_tensor):
-            slab = act_out[n].at[src]
-            copy = remote(slab, slab, a_fwd.at[n, src], a_back.at[n, src], me.across())
-
-            pl.when(me.home)(copy.wait_send)
-            pl.when(jnp.logical_not(me.home))(copy.wait_recv)
-
-    def pack_copy(n, s):
-        return remote(
-            pack_in[n], pack_out[n].at[me.slot], k_send.at[n, s - 1], k_recv.at[n, me.slot], me.shifted(s)
+                    slab = self.dst.at[place]
+                    remote(slab, slab, self.send.at[0], self.recv.at[place], me.across()).wait_recv()
+                self._onward(place).start()
+
+    def ready(self):
+        for place in range(self.me.nz):
+            pl.when(jnp.logical_not(self.me.home))(self._onward(place).wait_recv)
+
+    def finish(self):
+        for i in range(self.me.nz // 2):
+            target, copy = self._copy(i)
+            pl.when(target != self.me.z)(copy.wait_send)
+        for place in range(self.me.nz):
+            pl.when(self.me.home)(self._onward(place).wait_send)
+
+
+class Packs:
+    def __init__(self, me, src, dst, pair_src, pair_dst, sems):
+        self.me, self.src, self.dst, self.pair_src, self.pair_dst = me, src, dst, pair_src, pair_dst
+        self.send, self.recv, self.loc = sems
+
+    @staticmethod
+    def semaphores(sizes):
+        dma = pltpu.SemaphoreType.DMA
+        return [dma((sizes[1],)), dma((3,)), dma((2,))]
+
+    def _copy(self, s):
+        me = self.me
+        return remote(self.src, self.dst.at[me.slot], self.send.at[s], self.recv.at[me.slot], me.shifted(s))
+
+    def _stay(self):
+        return pltpu.make_async_copy(self.src, self.dst.at[self.me.slot], self.loc.at[0])
+
+    def _pair(self):
+        return (
+            pltpu.make_async_copy(self.pair_src, self.pair_dst, self.loc.at[1]),
+            remote(self.pair_src, self.pair_dst, self.send.at[0], self.recv.at[2], self.me.across()),
         )
 
-    for n in range(n_packs):
-
-        @pl.when(me.home)
-        def _(n=n):
-            local(pack_in[n], pack_out[n].at[me.slot], n_w + n_acts + n).start()
-            for s in range(1, n_tensor):
-                pack_copy(n, s).start()
-
-    for n in range(n_pairs):
-        there = remote(pair_in[n], pair_out[n], q_send.at[n], q_recv.at[n], me.across())
-
-        @pl.when(me.home)
-        def _(n=n, there=there):
-            local(pair_in[n], pair_out[n], n_w + n_acts + n_packs + n).start()
+    def start(self):
+        @pl.when(self.me.home)
+        def _():
+            self._stay().start()
+            for s in range(1, self.me.nz):
+                self._copy(s).start()
+            stay, there = self._pair()
+            stay.start()
             there.start()
 
-    if n_acts and n_packs:
-        for n in range(n_acts):
-            start_acts(n)
-
-    def start_z(j):
-        kind = kinds[j]
-        mine = kind.one(w_out[j], me.slot, me.chip, me.core)
+    def ready(self):
+        me = self.me
+        for slot in range(2):
+            row = self.dst.at[slot]
+            copy = remote(row, row, self.send.at[0], self.recv.at[slot], me.across())
+            pl.when(me.core * (me.nz // 2) + slot != me.z)(copy.wait_recv)
+        stay, there = self._pair()
 
         @pl.when(me.home)
         def _():
-            local(w_in[j], mine, j).wait()
-            remote(w_in[j], mine, s_send.at[j], s_recv.at[j], me.across()).wait_recv()
-            src = kind.piece(w_out[j], me.slot, me.chip)
-            for s in range(1, n_tensor):
-                remote(src, src, z_send.at[j, s - 1], z_recv.at[j, me.slot], me.shifted(s)).start()
-
-    def wait_z(j):
-        for slot in range(2):
-            src = kinds[j].piece(w_out[j], slot, me.chip)
-            copy = remote(src, src, z_send.at[j, 0], z_recv.at[j, slot], me.across())
-            pl.when(me.core * half_z + slot != me.z)(copy.wait_recv)
-
-    def bit_copies(j, step, slot):
-        bit = step if slot == 0 else me.bits - 1 - step
-        low = 1 if slot == 0 else 1 << (me.bits - step)
-
-        def held(m):
-            return flipped(me.chip, m * low)
-
-        def send(m):
-            src = kinds[j].piece(w_out[j], slot, held(m))
-            return remote(src, src, b_send.at[j, step, slot, m], b_recv.at[j, step, slot, m], me.beside(bit))
-
-        return send
-
-    def start_bits(j, step):
-        for slot in range(2):
-            send = bit_copies(j, step, slot)
-            _each(1 << step, lambda m: send(m).start())
-
-    def wait_bits(j, step):
-        for slot in range(2):
-            send = bit_copies(j, step, slot)
-            _each(1 << step, lambda m: send(m).wait_recv())
-
-    lag = me.bits + 1
-    if n_w:
-        start_z(0)
-    for tick in range(n_w + lag):
-        if tick < n_w:
-            wait_z(tick)
-            if tick + 1 < n_w:
-                start_z(tick + 1)
-            elif not n_packs:
-                for n in range(n_acts):
-                    start_acts(n)
-        for step in range(me.bits + 1):
-            j = tick - step
-            if 0 <= j < n_w:
-                if step > 0:
-                    wait_bits(j, step - 1)
-                if step < me.bits:
-                    start_bits(j, step)
-        if tick == 0 and n_packs:
-            for n in range(n_acts):
-                pass_acts(n)
-    if not n_packs:
-        for n in range(n_acts):
-            pass_acts(n)
-
-    for j, kind in enumerate(kinds):
-        mine = kind.one(w_out[j], me.slot, me.chip, me.core)
-        copy = remote(w_in[j], mine, s_send.at[j], s_recv.at[j], me.across())
-        pl.when(jnp.logical_not(me.home))(copy.wait_send)
-        src = kind.piece(w_out[j], me.slot, me.chip)
-        for s in range(1, n_tensor):
-            copy = remote(src, src, z_send.at[j, s - 1], z_recv.at[j, 0], me.shifted(s))
-            pl.when(me.home)(copy.wait_send)
-        for step in range(me.bits):
-            for slot in range(2):
-                send = bit_copies(j, step, slot)
-                _each(1 << step, lambda m: send(m).wait_send())
-    for n in range(n_acts):
-        end_acts(n)
-    for n in range(n_packs):
-        for slot in range(2):
-            row = pack_out[n].at[slot]
-            copy = remote(pack_in[n], row, k_send.at[n, 0], k_recv.at[n, slot], me.across())
-            pl.when(me.core * half_z + slot != me.z)(copy.wait_recv)
-
-        @pl.when(me.home)
-        def _(n=n):
-            local(pack_in[n], pack_out[n].at[me.slot], n_w + n_acts + n).wait()
-            for s in range(1, n_tensor):
-                pack_copy(n, s).wait_send()
-
-    for n in range(n_pairs):
-        there = remote(pair_in[n], pair_out[n], q_send.at[n], q_recv.at[n], me.across())
-
-        @pl.when(me.home)
-        def _(n=n, there=there):
-            local(pair_in[n], pair_out[n], n_w + n_acts + n_packs + n).wait()
-            there.wait_send()
+            self._stay().wait()
+            stay.wait()
 
         pl.when(jnp.logical_not(me.home))(there.wait_recv)
+
+    def finish(self):
+        @pl.when(self.me.home)
+        def _():
+            for s in range(1, self.me.nz):
+                self._copy(s).wait_send()
+            self._pair()[1].wait_send()
 
 
 def _each(count, act):
@@ -392,46 +398,6 @@
         @pl.loop(0, count)
         def _(m):
             act(m)
-
-
-def gather(acts, packs, pairs, weights, kinds, sizes, cid):
-    n_dp, n_tensor = sizes
-    bits = (n_dp // 2).bit_length() - 1
-    n_a, n_k, n_q, n_w = len(acts), len(packs), len(pairs), len(weights)
-    shapes = [jax.ShapeDtypeStruct((n_tensor,) + a.shape[1:], a.dtype) for a in acts]
-    shapes += [jax.ShapeDtypeStruct((2,) + a.shape, a.dtype) for a in packs]
-    shapes += [jax.ShapeDtypeStruct(a.shape, a.dtype) for a in pairs]
-    shapes += [jax.ShapeDtypeStruct(k.whole, w.dtype) for k, w in zip(kinds, weights)]
-    dma = pltpu.SemaphoreType.DMA
-    na, nk, nq = max(n_a, 1), max(n_k, 1), max(n_q, 1)
-    most = max(1 << max(bits - 1, 0), 1)
-    out = pl.pallas_call(
-        functools.partial(gather_kernel, kinds, n_a, n_k, n_q, sizes),
-        out_shape=shapes,
-        in_specs=[pl.BlockSpec(memory_space=pltpu.HBM)] * (n_a + n_k + n_q + n_w),
-        out_specs=[pl.BlockSpec(memory_space=pltpu.HBM)] * len(shapes),
-        scratch_shapes=[
-            dma((na, n_tensor)),
-            dma((na, n_tensor)),
-            dma((na, n_tensor)),
-            dma((na, n_tensor)),
-            dma((nk, n_tensor)),
-            dma((nk, 2)),
-            dma((nq,)),
-            dma((nq,)),
-            dma((n_w,)),
-            dma((n_w,)),
-            dma((n_w, n_tensor)),
-            dma((n_w, 2)),
-            dma((n_w, bits, 2, most)),
-            dma((n_w, bits, 2, most)),
-            dma((n_w + n_a + n_k + n_q,)),
-        ],
-        compiler_params=pltpu.CompilerParams(collective_id=cid, has_side_effects=True),
-        name=f"gather{cid}",
-    )(*acts, *packs, *pairs, *[k.enter(w) for k, w in zip(kinds, weights)])
-    a, k, q = out[:n_a], out[n_a : n_a + n_k], out[n_a + n_k : n_a + n_k + n_q]
-    return a, k, q, [kind.join(w) for kind, w in zip(kinds, out[n_a + n_k + n_q :])]
 
 
 def scatter_kernel(kinds, n_acts, sizes, *refs):
@@ -678,7 +644,7 @@
 
 
 KEYS = 1152
-TILE = 352
+TILE = 272
 COLS = 384
 
 
@@ -691,93 +657,189 @@
     )
 
 
-def attention_forward_kernel(
-    x_ref, wq_ref, wk_ref, wv_ref, cos_ref, up_ref, down_ref, qb_ref, vb_ref, base_ref,
-    qa_ref, ka_ref, va_ref, mix_ref,
+def front_kernel(
+    kinds, sizes,
+    tok_in, cot_in, pack_in, base_in, qkv_in, o_in, g_in, u_in, d_in,
+    gain_ref, bias_ref, cos_ref, up_ref, down_ref,
+    tok, cot, pack, base, w_qkv, w_o, w_g, w_u, w_d, normed, qa_ref, ka_ref, va_ref, mix_ref,
+    *sems,
 ):
-    rows = x_ref.shape[0]
-    tiles = rows // TILE
-    lane = lax.broadcasted_iota(jnp.int32, (TILE, 2 * HEAD), 1)
+    me = Place(*sizes)
+    nz = sizes[1]
+    gather = Gather(me, kinds, (qkv_in, o_in, g_in, u_in, d_in), (w_qkv, w_o, w_g, w_u, w_d), sems[:7])
+    tokens = Inward(me, tok_in, tok, sems[7:12])
+    cots = Inward(me, cot_in, cot, sems[12:17])
+    packs = Packs(me, pack_in, pack, base_in, base, sems[17:20])
+    n_w = len(kinds)
+    me.barrier()
+    for j in range(n_w):
+        gather.first_hop(j)
+    gather.start_z(0)
+    tokens.start()
+    packs.start()
+    gather.wait_z(0)
+    for step in range(me.bits):
+        if step > 0:
+            gather.wait_bits(0, step - 1)
+        gather.start_bits(0, step)
+    tokens.pass_on()
+    gather.start_z(1)
+
+    def on_the_way():
+        for j in range(1, n_w):
+            gather.wait_z(j)
+            if j + 1 < n_w:
+                gather.start_z(j + 1)
+            else:
+                cots.start()
+            gather.start_bits(j, 0)
+            yield
+            for step in range(1, me.bits):
+                gather.wait_bits(j, step - 1)
+                gather.start_bits(j, step)
+                yield
+
+    events = on_the_way()
+    tokens.ready()
+    packs.ready()
+
+    block = tok.shape[1]
+    rows = block * nz
+    width = tok.shape[2]
+    lanes = 2 * HEAD
+    lane = lax.broadcasted_iota(jnp.int32, (block, lanes), 1)
     low = lane < HEAD
     one = jnp.where(lane == HEAD, 1.0, 0.0)
     ones = jnp.where((lane >= HEAD) & (lane < HEAD + 3), 1.0, 0.0)
 
-    @pl.loop(0, tiles)
+    @pl.loop(0, nz)
     def _(t):
-        here = pl.ds(pl.multiple_of(t * TILE, TILE), TILE)
-        x = x_ref[here, :]
-        both = matmul(x, jnp.concatenate([wq_ref[...], wk_ref[...]], axis=1))
-        tables = (cos_ref[here, :], up_ref[here, :], down_ref[here, :])
-        query = _turn(both[:, : 2 * HEAD] + qb_ref[0], *tables) * (SCALE * LOG2E)
-        key = _turn(both[:, 2 * HEAD :], *tables)
-        value = matmul(x, wv_ref[...]) + vb_ref[0]
-        base = base_ref[here, :].astype(F32)
+        x = tok[t].astype(F32)
+        mean = jnp.sum(x, axis=1, keepdims=True) * (1.0 / width)
+        x = x - mean
+        var = jnp.sum(x * x, axis=1, keepdims=True) * (1.0 / width)
+        x = x * lax.rsqrt(var + EPS)
+        normed[pl.ds(pl.multiple_of(t * block, block), block), :] = (x * gain_ref[...] + bias_ref[...]).astype(BF16)
+
+    gather.wait_bits(0, me.bits - 1)
+    pairs = mix_ref.shape[1] // lanes
+    sub = pairs // 2
+
+    def project(g):
+        at = (g // sub) * (3 * sub) + g % sub
+
+        def column(part):
+            return w_qkv[:, (at + part * sub) * lanes : (at + part * sub + 1) * lanes]
+
+        q_bias = pack[g // sub, g % sub : g % sub + 1, :]
+        v_bias = pack[g // sub, sub + g % sub : sub + g % sub + 1, :]
+
+        @pl.loop(0, nz)
+        def _(t):
+            here = pl.ds(pl.multiple_of(t * block, block), block)
+            x = normed[here, :]
+            both = matmul(x, jnp.concatenate([column(0), column(1)], axis=1))
+            tables = (cos_ref[here, :], up_ref[here, :], down_ref[here, :])
+            query = _turn(both[:, :lanes] + q_bias, *tables) * (SCALE * LOG2E)
+            key = _turn(both[:, lanes:], *tables)
+            value = matmul(x, column(2)) + v_bias
+            mask = base[here, :].astype(F32)
+            for h in range(2):
+                if h:
+                    query, key, value = (pltpu.roll(v, HEAD, 1) for v in (query, key, value))
+                qa_ref[2 * g + h, here, :] = jnp.where(low, query, one).astype(BF16)
+                ka_ref[2 * g + h, here, :] = jnp.where(low, key, mask).astype(BF16)
+                va_ref[2 * g + h, here, :] = jnp.where(low, value, ones).astype(BF16)
+
+        rest = pl.ds(rows, KEYS - rows)
         for h in range(2):
-            if h:
-                query, key, value = (pltpu.roll(v, HEAD, 1) for v in (query, key, value))
-            qa_ref[h, here, :] = jnp.where(low, query, one).astype(BF16)
-            ka_ref[h, here, :] = jnp.where(low, key, base).astype(BF16)
-            va_ref[h, here, :] = jnp.where(low, value, ones).astype(BF16)
-
-    rest = pl.ds(rows, KEYS - rows)
-    for h in range(2):
-        qa_ref[h, rest, :] = jnp.zeros((KEYS - rows, 2 * HEAD), BF16)
-        va_ref[h, rest, :] = jnp.zeros((KEYS - rows, 2 * HEAD), BF16)
-        ka_ref[h, rest, :] = base_ref[rest, :]
-
-    @pl.loop(0, tiles)
-    def _(t):
-        here = pl.ds(pl.multiple_of(t * TILE, TILE), TILE)
-        outs = []
-        for h in range(2):
-            q = qa_ref[h, here, :]
-            s = matmul_right_t(q, ka_ref[h])
-            top = jnp.max(s, axis=1, keepdims=True)
-            p = jnp.exp2(s - top).astype(BF16)
-            o = matmul(p, va_ref[h])
-            total = o[:, HEAD : HEAD + 1]
-            outs.append(o / total)
-            log = -(top + jnp.log2(total))
-            first = log.astype(BF16)
-            left = log - first.astype(F32)
-            second = left.astype(BF16)
-            third = (left - second.astype(F32)).astype(BF16)
-            logs = jnp.where(
-                lane == HEAD + 1,
-                first.astype(F32),
-                jnp.where(lane == HEAD + 2, second.astype(F32), third.astype(F32)),
-            )
-            inside = (lane > HEAD) & (lane <= HEAD + 3)
-            qa_ref[h, here, :] = jnp.where(inside, logs, q.astype(F32)).astype(BF16)
-        mix_ref[here, :] = jnp.where(low, outs[0], pltpu.roll(outs[1], HEAD, 1)).astype(BF16)
-
-
-def attention_forward(x, w, tables, query_bias, value_bias, base):
-    rows, width = x.shape
-    pairs = query_bias.shape[0]
-    sub = pairs // 2
+            qa_ref[2 * g + h, rest, :] = jnp.zeros((KEYS - rows, lanes), BF16)
+            va_ref[2 * g + h, rest, :] = jnp.zeros((KEYS - rows, lanes), BF16)
+            ka_ref[2 * g + h, rest, :] = base[rest, :]
+
+    def attend(g):
+        @pl.loop(0, nz)
+        def _(t):
+            here = pl.ds(pl.multiple_of(t * block, block), block)
+            outs = []
+            for h in range(2):
+                q = qa_ref[2 * g + h, here, :]
+                s = matmul_right_t(q, ka_ref[2 * g + h])
+                top = jnp.max(s, axis=1, keepdims=True)
+                p = jnp.exp2(s - top).astype(BF16)
+                o = matmul(p, va_ref[2 * g + h])
+                total = o[:, HEAD : HEAD + 1]
+                outs.append(o / total)
+                log = -(top + jnp.log2(total))
+                first = log.astype(BF16)
+                left = log - first.astype(F32)
+                second = left.astype(BF16)
+                third = (left - second.astype(F32)).astype(BF16)
+                logs = jnp.where(
+                    lane == HEAD + 1,
+                    first.astype(F32),
+                    jnp.where(lane == HEAD + 2, second.astype(F32), third.astype(F32)),
+                )
+                inside = (lane > HEAD) & (lane <= HEAD + 3)
+                qa_ref[2 * g + h, here, :] = jnp.where(inside, logs, q.astype(F32)).astype(BF16)
+            mix_ref[here, g * lanes : (g + 1) * lanes] = jnp.where(
+                low, outs[0], pltpu.roll(outs[1], HEAD, 1)
+            ).astype(BF16)
+
+    next(events, None)
+    for g in range(pairs):
+        project(g)
+        next(events, None)
+        attend(g)
+        next(events, None)
+    for _ in events:
+        pass
+    cots.pass_on()
+    for j in range(1, n_w):
+        gather.wait_bits(j, me.bits - 1)
+    cots.ready()
+    for j in range(n_w):
+        gather.finish(j)
+    tokens.finish()
+    cots.finish()
+    packs.finish()
+
+
+def front(tokens, cotangent, pack, base, weights, kinds, gain, bias, tables, n_head, sizes, cid):
+    nz = sizes[1]
+    block, width = tokens.shape[1:]
+    rows = block * nz
     lanes = 2 * HEAD
-
-    def column(part):
-        return pl.BlockSpec((width, lanes), lambda g: (0, (g // sub) * (3 * sub) + part * sub + g % sub))
-
-    def whole(shape):
-        return pl.BlockSpec(shape, lambda g: (0,) * len(shape))
-
-    bias = pl.BlockSpec((1, 1, lanes), lambda g: (g, 0, 0))
-    heads = pl.BlockSpec((2, KEYS, lanes), lambda g: (g, 0, 0))
-    return pl.pallas_call(
-        attention_forward_kernel,
-        grid=(pairs,),
-        out_shape=[jax.ShapeDtypeStruct((2 * pairs, KEYS, lanes), BF16)] * 3
-        + [jax.ShapeDtypeStruct((rows, pairs * lanes), BF16)],
-        in_specs=[whole((rows, width)), column(0), column(1), column(2)]
-        + [whole((rows, lanes))] * 3
-        + [bias, bias, whole((KEYS, lanes))],
-        out_specs=[heads, heads, heads, pl.BlockSpec((rows, lanes), lambda g: (0, g))],
-        compiler_params=pltpu.CompilerParams(vmem_limit_bytes=48 * 2**20),
-        name="attention_forward",
-    )(x, w, w, w, *tables, query_bias, value_bias, base)
+    heads = 2 * n_head // HEAD
+    hbm = pl.BlockSpec(memory_space=pltpu.HBM)
+    vmem = pl.BlockSpec(memory_space=pltpu.VMEM)
+    shape = jax.ShapeDtypeStruct
+    weights = [k.enter(w) for k, w in zip(kinds, weights)]
+    shapes = [
+        shape((nz, block, width), BF16),
+        shape((nz, block, width), BF16),
+        shape((2,) + pack.shape, F32),
+        shape(base.shape, BF16),
+        *[shape(k.whole, BF16) for k in kinds],
+        shape((rows, width), BF16),
+        *[shape((heads, KEYS, lanes), BF16)] * 3,
+        shape((rows, heads * HEAD), BF16),
+    ]
+    out = pl.pallas_call(
+        functools.partial(front_kernel, kinds, sizes),
+        out_shape=shapes,
+        in_specs=[hbm] * 9 + [vmem] * 5,
+        out_specs=[vmem, hbm, vmem, vmem, vmem, hbm, hbm, hbm, hbm] + [vmem] * 5,
+        scratch_shapes=Gather.semaphores(len(kinds), sizes)
+        + Inward.semaphores(sizes)
+        + Inward.semaphores(sizes)
+        + Packs.semaphores(sizes),
+        compiler_params=pltpu.CompilerParams(
+            collective_id=cid, has_side_effects=True, vmem_limit_bytes=48 * 2**20
+        ),
+        name="front",
+    )(tokens, cotangent, pack, base, *weights, gain[None], bias[None], *tables)
+    return out[:4], [k.join(w) for k, w in zip(kinds, out[4:9])], out[9:]
 
 
 def attention_backward_kernel(
@@ -892,7 +954,7 @@
     block = tokens_in.shape[1]
     width = tokens_in.shape[2]
     length = block * n_tensor
-    block_pad = up_to(block, 8)
+    block_pad = up_to(block, 16)
     rows = block_pad * n_tensor
     n_head = w_query.shape[1]
     n_ff = w_gate.shape[1]
@@ -910,6 +972,15 @@
 
     def pad_ff(vec):
         return jnp.pad(vec, (0, ff - n_ff))
+
+    def turned(weight):
+        return jnp.pad(weight.T, ((0, ff - n_ff), (0, 0)))
+
+    def pad_rows(value):
+        return jnp.pad(value, ((0, 0), (0, block_pad - block), (0, 0)))
+
+    def unpadded(value):
+        return value.reshape(n_tensor, block_pad, width)[:, :block]
 
     small = jnp.concatenate(
         [query_bias, value_bias]
@@ -918,65 +989,46 @@
     small_rows = up_to(up_to(small.shape[0], LANES) // LANES, 8)
     small = jnp.pad(small, (0, small_rows * LANES - small.shape[0])).reshape(small_rows, LANES)
     own_image = z % (n_tensor // 2)
-    pair = jnp.concatenate(
-        [
-            lax.dynamic_index_in_dim(key_mask, own_image, 0, False).astype(F32),
-            lax.dynamic_index_in_dim(image_flag, own_image, 0, True).astype(F32),
-        ]
+    live = lax.dynamic_index_in_dim(key_mask, own_image, 0, False)
+    live = jnp.pad(live.reshape(n_tensor, block), ((0, 0), (0, block_pad - block))).reshape(rows)
+    live = jnp.pad(live, (0, KEYS - rows))
+    lane = jnp.arange(LANES)[None, :]
+    base = jnp.where(
+        lane == HEAD,
+        jnp.where(live > 0, 0.0, -1e30)[:, None],
+        jnp.where(
+            (lane > HEAD) & (lane <= HEAD + 3),
+            1.0,
+            jnp.where(lane == LANES - 1, lax.dynamic_index_in_dim(image_flag, own_image, 0, False).astype(F32), 0.0),
+        ),
+    ).astype(BF16)
+    tables = lane_tables(length, HEAD // 4, block, block_pad)
+
+    (image, cot, packs, base), full, (normed, qa, ka, va, mixed) = front(
+        pad_rows(tokens_in),
+        pad_rows(cotangent),
+        small,
+        base,
+        [shard_qkv, w_out, turned(w_gate), turned(w_up), jnp.pad(w_down, ((0, ff - n_ff), (0, 0)))],
+        [kind_qkv, kind_o, kind_f, kind_f, kind_f],
+        attention_norm_gain,
+        attention_norm_bias,
+        tables,
+        n_head,
+        sizes,
+        0,
     )
-    pair_rows = up_to(up_to(length + 1, LANES) // LANES, 8)
-    pair = jnp.pad(pair, (0, pair_rows * LANES - pair.shape[0])).reshape(pair_rows, LANES)
-
-    (image,), (packs,), (mask_flag,), (full_qkv,) = gather(
-        [tokens_in], [small], [pair], [shard_qkv], [kind_qkv], sizes, 0
-    )
-
-    def turned(weight):
-        return jnp.pad(weight.T, ((0, ff - n_ff), (0, 0)))
-
-    (cot,), _, _, (full_g, full_u, full_o, full_d) = gather(
-        [cotangent],
-        [],
-        [],
-        [turned(w_gate), turned(w_up), w_out, jnp.pad(w_down, ((0, ff - n_ff), (0, 0)))],
-        [kind_f, kind_f, kind_o, kind_f],
-        sizes,
-        1,
-    )
-
+    full_qkv, full_o, full_g, full_u, full_d = full
     packs = packs.reshape(2, -1)
     cuts = [n_head] * 2 + [ff] * 5
     parts, at = [], 0
     for size in cuts:
         parts.append(packs[:, at : at + size].reshape(-1))
         at += size
-    q_bias, v_bias, g_bias, u_bias, gain, shift, columns = parts
-    mask_flag = mask_flag.reshape(-1)
-    flag = mask_flag[length]
-
-    def padded(value):
-        return jnp.pad(value, ((0, 0), (0, block_pad - block), (0, 0))).reshape(rows, -1)
-
-    def unpadded(value):
-        return value.reshape(n_tensor, block_pad, width)[:, :block]
-
-    live = padded(mask_flag[:length].reshape(n_tensor, block, 1)).reshape(rows)
-    live = jnp.pad(live, (0, KEYS - rows))
-    lane = jnp.arange(LANES)[None, :]
-    base = jnp.where(
-        lane == HEAD,
-        jnp.where(live > 0, 0.0, -1e30)[:, None],
-        jnp.where((lane > HEAD) & (lane <= HEAD + 3), 1.0, 0.0),
-    ).astype(BF16)
-    tables = lane_tables(length, HEAD // 4, block, block_pad)
-
-    token_rows = padded(image).astype(F32)
+    _, _, g_bias, u_bias, gain, shift, columns = parts
+    flag = base[0, LANES - 1].astype(F32)
+    token_rows = image.reshape(rows, width).astype(F32)
     xhat1, s1 = norm_pieces(token_rows)
-    normed = (xhat1 * attention_norm_gain + attention_norm_bias).astype(BF16)
-    pairs = 2 * n_head // (2 * HEAD)
-    qa, ka, va, mixed = attention_forward(
-        normed, full_qkv, tables, q_bias.reshape(pairs, 1, 2 * HEAD), v_bias.reshape(pairs, 1, 2 * HEAD), base
-    )
     part = matmul(mixed, full_o).astype(BF16)
     middle = token_rows + (part.astype(F32) + other(part).astype(F32)) + out_bias
     xhat2, s2 = norm_pieces(middle)
@@ -995,7 +1047,7 @@
     part = matmul(hidden, full_d).astype(BF16)
     output = (middle + (part.astype(F32) + other(part).astype(F32)) + down_bias).astype(BF16)
 
-    grad = padded(cot).astype(F32) * flag
+    grad = cot.reshape(rows, width).astype(F32) * flag
     grad_low = grad.astype(BF16)
     g_down = matmul_left_t(hidden, grad_low).astype(BF16)
     dn = columns * lax.dot_general(

time: 584 us -> 512 us (0.88)
  Pallas kernels: 378 us -> 328 us
  other arithmetic: 61.1 us -> 48.5 us
  local copies, waits for them, and re-layouts: 45.1 us -> 34.1 us
  matrix products: 79.8 us -> 88.5 us
    pallas_call x3 -> x1, Pallas kernels: 203 us -> 150 us  [front(): pl.pallas_call(functools.partial(front_kernel, kinds, sizes), out_shape=s...]
    dot_general x4, matrix products: 16.2 us -> 22.9 us  [matmul(): return jnp.dot(left, right, preferred_element_type=F32)]
    unnamed x139 -> x143, local copies, waits for them, and re-layouts: 24.3 us -> 17.6 us
  transfers between devices with their start and end apart: 6 -> 6, of which waited for: 1 -> 1; matrix products, arithmetic and copies ran while one was open for 9% -> 12% of each run, Pallas kernels for 0% -> 0%
where the time goes in v2:
time: 512 us; the launch traced here: 506 us
  Pallas kernels  328 us (64%)
  matrix products  88.5 us (17%)
  other arithmetic  48.5 us (9%)
  local copies, waits for them, and re-layouts  34.1 us (7%)
    pallas_call x1, Pallas kernels, front(): pl.pallas_call(functools.partial(front_kernel, kinds, sizes), out_shape=s...  150 us
    pallas_call x1, Pallas kernels, scatter(): pl.pallas_call(functools.partial(scatter_kernel, kinds, n_a, sizes), out_...  132 us
    pallas_call x1, Pallas kernels, attention_backward(): pl.pallas_call(functools.partial(attention_backward_kernel, sub), grid=(p...  46.1 us
    dot_general x5, matrix products, matmul_left_t(): lax.dot_general(left, right, (((0,), (0,)), ((), ())), preferred_element_...  35.6 us
    dot_general x4, matrix products, matmul(): return jnp.dot(left, right, preferred_element_type=F32)  22.9 us
    dot_general x4, matrix products, matmul_right_t(): lax.dot_general(left, right, (((1,), (1,)), ((), ())), preferred_element_...  20.9 us
    unnamed x143, local copies, waits for them, and re-layouts  17.6 us
  transfers between devices with their start and end apart: 6, of which 1 were waited for; matrix products, arithmetic and copies ran while one was open for 12% of the time, Pallas kernels for 0%

profile of v2, /device:TPU:0, one launch (start us, length us, event | category | flops | bytes accessed | tf_op | source)
XLA Modules:
  0.0 505.6 jit_solution(17410560350647458497)
XLA Ops:
  17.9 150.1 %front.1 = (bf16[4,272,1024]{2,1,0:T(8,128)(2,1)}, bf16[4,272,1024]{2,1,0:T(8,128)(2,1)}, f32[2,32,128]{2,1,0:T(8,128)S(1)}, bf16[1152,128]{1,0:T(8,128)(2,1)S(1...) custom-call(bf16[2,272,1024]{2,1,0:T(8,128)(2,1)} %pad.59.tok_in, ...), custom_call_target="tpu_custom_call" | custom-call | tf_op jit(solution)/shard_map/front/pallas_call | solution.py:828
  176.0 3.1 fusion.17
  179.1 5.9 %fusion.2 = (f32[1088,1024]{1,0:T(8,128)}, f32[1088,1024]{1,0:T(8,128)S(1)}) fusion(bf16[4,272,1024]{2,1,0:T(8,128)(2,1)S(1)} %copy-done.10, f32[1088]{0:T(1024)S(1)} %div.83, f32[1088]{0:T(1024)S(1)} %rsqrt.30, bf16[1088,1024]{1,0:T(8,128)(2,1)} %collective-permute-done, bf16[1088,1024]{1,0:T(8,128)(2,1)} %convolution_convert_fusion), kind=kLoop, calls=%fused_computation.24 | loop fusion | flops 7798784 | bytes 15606272 | tf_op jit(solution)/shard_map/mul | solution.py:63
  188.4 3.7 convolution_add_fusion.1
  192.1 8.8 %multiply_reduce_fusion.3 = (f32[1088]{0:T(1024)S(1)}, f32[1088]{0:T(1024)S(1)}, f32[1088,1376]{1,0:T(8,128)}, f32[1088,1376]{1,0:T(8,128)}) fusion(f32[1376]{0:T(1024)S(1)} %mul.234, f32[1088,1376]{1,0:T(8,128)S(1)} %convolution_add_fusion.1, f32[1376]{0:T(1024)S(1)} %add.217, bf16[1088,1024]{1,0:T(8,128)(2,1)S(1)} %add_convert_fusion.2, ...), kind=kOutput, calls=%fused_computation.11 | convolution fusion | flops 3082502144 | bytes 23031040 | tf_op jit(solution)/shard_map/dot_general | solution.py:80
  203.4 9.1 %multiply_reduce_fusion = (f32[1376]{0:T(1024)S(1)}, f32[1088]{0:T(1024)S(1)}, f32[1088]{0:T(1024)S(1)}, f32[1376]{0:T(1024)S(1)}, f32[1088,1376]{1,0:T(8,128)S(1)}) fusion(f32[1088,1376]{1,0:T(8,128)} %get-tuple-element.164, f32[1088]{0:T(1024)S(1)} %add_rsqrt_fusion, f32[1088]{0:T(1024)S(1)} %get-tuple-element.156, f32[1376]{0:T(1024)S(1)} %mul.248, ...), kind=kOutput, calls=%fused_computation.3 | convolution fusion | flops 3081002496 | bytes 17062400 | tf_op jit(solution)/shard_map/dot_general | solution.py:1053
  213.9 7.3 %fusion.40 = (f32[1376]{0:T(1024)S(1)}, bf16[1088,1376]{1,0:T(8,128)(2,1)}, f32[1376]{0:T(1024)S(1)}, bf16[1088,1376]{1,0:T(8,128)(2,1)}) fusion(f32[1088,1376]{1,0:T(8,128)S(1)} %copy-done.17, f32[1088]{0:T(1024)S(1)} %get-tuple-element.155, f32[1088,1376]{1,0:T(8,128)S(1)} %copy-done.15, f32[1088]{0:T(1024)S(1)} %get-tuple-element.156, ...), kind=kLoop, calls=%fused_computation.158 | loop fusion | flops 35927360 | bytes 29981184 | tf_op jit(solution)/shard_map/reduce_sum | solution.py:1065
  221.3 6.5 %fusion.13 = f32[1088,1024]{1,0:T(8,128)S(1)} fusion(bf16[1376,1024]{1,0:T(8,128)(2,1)} %get-tuple-element.49, bf16[1088,1376]{1,0:T(8,128)(2,1)} %get-tuple-element.166), kind=kOutput, calls=%fused_computation.56 | convolution fusion | flops 3066036224 | bytes 10268672 | tf_op jit(solution)/shard_map/dot_general | solution.py:76
  227.8 5.0 fusion.7
  233.1 8.6 %convolution_convert_fusion.4 = bf16[1088,1024]{1,0:T(8,128)(2,1)} fusion(bf16[1376,1024]{1,0:T(8,128)(2,1)} %get-tuple-element.51, f32[1088,1376]{1,0:T(8,128)} %get-tuple-element.164, f32[1376]{0:T(1024)S(1)} %add.222, f32[1376]{0:T(1024)S(1)} %mul.248, f32[1088]{0:T(1024)S(1)} %add_rsqrt_fusion, f32[1088]{0:T(1024)S(1)} %get-tuple-element.156, ...), kind=kOutput, calls=%fused_computation.46 | convolution fusion | flops 3076132864 | bytes 11059840 | tf_op jit(solution)/shard_map/dot_general | solution.py:76
  242.3 9.2 %convolution_convert_fusion.3.refs_3_ = bf16[1376,1024]{1,0:T(8,128)(2,1)} fusion(bf16[1088,1024]{1,0:T(8,128)(2,1)} %bitcast_convert_fusion, f32[1088,1376]{1,0:T(8,128)} %get-tuple-element.164, f32[1376]{0:T(1024)S(1)} %add.222, f32[1376]{0:T(1024)S(1)} %mul.248, f32[1088]{0:T(1024)S(1)} %add_rsqrt_fusion, f32[1088]{0:T(1024)S(1)} %get-tuple-element.156, ...), kind=kOutput, calls=%fused_computation.45 | convolution fusion | flops 3076427776 | bytes 11059840 | tf_op jit(solution)/shard_map/dot_general | solution.py:84
  251.5 5.5 %multiply_reduce_fusion.5 = (f32[1024]{0:T(1024)S(1)}, f32[1088]{0:T(1024)S(1)}, f32[1088]{0:T(1024)S(1)}, f32[1024]{0:T(1024)S(1)}) fusion(bf16[1088,1024]{1,0:T(8,128)(2,1)} %collective-permute-done.4, bf16[1088,1024]{1,0:T(8,128)(2,1)} %fusion.7, f32[1088]{0:T(1024)S(1)} %add_rsqrt_fusion.1, f32[1088]{0:T(1024)S(1)} %broadcast_multiply_fusion.6, ...), kind=kLoop, calls=%fused_computation.25 | loop fusion | flops 14479232 | bytes 8946688 | tf_op jit(solution)/shard_map/reduce_sum | solution.py:1072
  257.0 9.0 %fusion.42 = (f32[1024]{0:T(1024)S(1)}, f32[1088,1024]{1,0:T(8,128)S(1)}, bf16[1088,1024]{1,0:T(8,128)(2,1)}) fusion(f32[1088]{0:T(1024)S(1)} %broadcast_multiply_fusion.4, f32[1088]{0:T(1024)S(1)} %broadcast_multiply_fusion.6, f32[1088,1024]{1,0:T(8,128)} %copy-done.8, f32[1024]{0:T(1024)S(1)} %copy-done.32, f32[1088]{0:T(1024)S(1)} %broadcast_multiply_fusion.5, ...), kind=kLoop, calls=%fused_computation.160 | loop fusion | flops 21167104 | bytes 24544256 | tf_op jit(solution)/shard_map/reduce_sum | solution.py:1075
  267.4 46.1 %attention_backward.1 = (bf16[1088,1536]{1,0:T(8,128)(2,1)}, f32[4,8,128]{2,1,0:T(8,128)S(1)}) custom-call(bf16[8,1152,128]{2,1,0:T(8,128)(2,1)} %get-tuple-element.54.qa_ref, bf16[8,1152,128]{2,1,0:T(8,128)(2,1)} %get-tuple-element.55.ka_ref, bf16[8,1152,128]{2,1,0:T(8,128)(2,1)} %get-tuple-element.56.va_ref, ...), custom_call_target="tpu_custom_call" | custom-call | tf_op jit(solution)/shard_map/attention_backward/pallas_call | solution.py:920
  313.5 7.1 %convolution_convert_fusion.6 = bf16[1088,1024]{1,0:T(8,128)(2,1)} fusion(bf16[1088,1536]{1,0:T(8,128)(2,1)} %get-tuple-element.57, bf16[1024,1536]{1,0:T(8,128)(2,1)S(1)} %copy-done.47), kind=kOutput, calls=%fused_computation.48 | convolution fusion | flops 3423666176 | bytes 8716288 | tf_op jit(solution)/shard_map/dot_general | solution.py:80
  320.7 5.2 %convolution_convert_fusion.2.refs_4_ = bf16[1376,1024]{1,0:T(8,128)(2,1)} fusion(bf16[1088,1024]{1,0:T(8,128)(2,1)S(1)} %copy-done.22, bf16[1088,1376]{1,0:T(8,128)(2,1)S(1)} %copy-done.20), kind=kOutput, calls=%fused_computation.44 | convolution fusion | flops 3067445248 | bytes 8040448 | tf_op jit(solution)/shard_map/dot_general | solution.py:84
  326.1 8.2 %convolution_convert_fusion.1.refs_5_ = bf16[1376,1024]{1,0:T(8,128)(2,1)} fusion(bf16[1088,1024]{1,0:T(8,128)(2,1)} %copy-done.21, bf16[1088,1376]{1,0:T(8,128)(2,1)} %get-tuple-element.159), kind=kOutput, calls=%fused_computation.43 | convolution fusion | flops 3067445248 | bytes 8040448 | tf_op jit(solution)/shard_map/dot_general | solution.py:84
  336.2 5.0 convolution_convert_fusion.8.refs_6_
  341.2 8.0 %convolution_convert_fusion.5.refs_7_ = bf16[1024,1536]{1,0:T(8,128)(2,1)} fusion(bf16[1088,1024]{1,0:T(8,128)(2,1)} %get-tuple-element.60, bf16[1088,1536]{1,0:T(8,128)(2,1)S(1)} %copy-done.46), kind=kOutput, calls=%fused_computation.47 | convolution fusion | flops 3424124928 | bytes 8716288 | tf_op jit(solution)/shard_map/dot_general | solution.py:84
  349.2 4.8 fusion.5
  354.1 3.6 add_convert_fusion
  360.0 132.0 %scatter2.1 = (bf16[2,257,1024]{2,1,0:T(8,128)(2,1)}, bf16[2,257,1024]{2,1,0:T(8,128)(2,1)}, f32[2,104,128]{2,1,0:T(8,128)}, f32[688,128]{1,0:T(8,128)}, f32[688...) custom-call(bf16[4,257,1024]{2,1,0:T(8,128)(2,1)} %slice.223.refs_0_, ...), custom_call_target="tpu_custom_call" | custom-call | tf_op jit(solution)/shard_map/scatter2/pallas_call | solution.py:609
  492.2 3.4 copy.58
  495.6 3.6 copy.59
  (253 shorter events, 43.0 us)
Async XLA Ops:
  170.8 8.3 %collective-permute-start = (bf16[1088,1024]{1,0:T(8,128)(2,1)}, bf16[1088,1024]{1,0:T(8,128)(2,1)}, u32[]{:S(2)}, u32[]{:S(2)}) collective-permute-start(bf16[1088,1024]{1,0:T(8,128)(2,1)} %convolution_convert_fusion), channel_id=1, source_target_pairs={{0,4},{1,5},{2,6},{3,7},{4,0},{5,1},{6,2},{7,3},{8,12},{9,13},{10,... | collective-permute-start | bytes 6684680 | tf_op jit(solution)/shard_map/ppermute | solution.py:966
  179.1 22.5 %copy-start.12 = (f32[4,272,1024]{2,1,0:T(8,128)}, f32[4,272,1024]{2,1,0:T(8,128)S(1)}, u32[]{:S(2)}) copy-start(f32[4,272,1024]{2,1,0:T(8,128)S(1)} %get-tuple-element.169) | copy-start | bytes 13369348
  192.0 8.9 %copy-start.16 = (f32[1088,1376]{1,0:T(8,128)}, f32[1088,1376]{1,0:T(8,128)S(1)}, u32[]{:S(2)}) copy-start(f32[1088,1376]{1,0:T(8,128)S(1)} %convolution_add_fusion.1) | copy-start | bytes 17965060
  201.0 2.4 collective-permute-start.1
  203.4 10.5 %copy-start.15 = (f32[1088,1376]{1,0:T(8,128)S(1)}, f32[1088,1376]{1,0:T(8,128)}, u32[]{:S(2)}) copy-start(f32[1088,1376]{1,0:T(8,128)} %get-tuple-element.164) | copy-start | bytes 17965060
  203.4 10.5 %copy-start.17 = (f32[1088,1376]{1,0:T(8,128)S(1)}, f32[1088,1376]{1,0:T(8,128)}, u32[]{:S(2)}) copy-start(f32[1088,1376]{1,0:T(8,128)} %copy-done.16) | copy-start | bytes 17965060
  203.4 10.5 %copy-start.18 = (f32[1088,1376]{1,0:T(8,128)S(1)}, f32[1088,1376]{1,0:T(8,128)}, u32[]{:S(2)}) copy-start(f32[1088,1376]{1,0:T(8,128)} %get-tuple-element.193) | copy-start | bytes 17965060
  212.6 1.2 collective-permute-start.3
  232.8 18.7 %collective-permute-start.4 = (bf16[1088,1024]{1,0:T(8,128)(2,1)}, bf16[1088,1024]{1,0:T(8,128)(2,1)}, u32[]{:S(2)}, u32[]{:S(2)}) collective-permute-start(bf16[1088,1024]{1,0:T(8,128)(2,1)} %fusion.7), channel_id=1, source_target_pairs={{0,4},{1,5},{2,6},{3,7},{4,0},{5,1},{6,2},{7,3},{8,12},{9,13},{10,... | collective-permute-start | bytes 6684680 | tf_op jit(solution)/shard_map/ppermute | solution.py:966
  241.8 15.2 %collective-permute-start.2 = (bf16[1088,1024]{1,0:T(8,128)(2,1)}, bf16[1088,1024]{1,0:T(8,128)(2,1)}, u32[]{:S(2)}, u32[]{:S(2)}) collective-permute-start(bf16[1088,1024]{1,0:T(8,128)(2,1)} %convolution_convert_fusion.4), channel_id=1, source_target_pairs={{0,4},{1,5},{2,6},{3,7},{4,0},{5,1},{6,2},{7,3},{8,12},{9,13},{10,... | collective-permute-start | bytes 6684680 | tf_op jit(solution)/shard_map/ppermute | solution.py:966
  257.0 9.0 %copy-start.6 = (bf16[512,1024]{1,0:T(8,128)(2,1)S(1)}, bf16[512,1024]{1,0:T(8,128)(2,1)}, u32[]{:S(2)}) copy-start(bf16[512,1024]{1,0:T(8,128)(2,1)} %copy-done.5) | copy-start | bytes 3145732
  266.0 47.5 %copy-start.13 = (f32[1088,1024]{1,0:T(8,128)}, f32[1088,1024]{1,0:T(8,128)S(1)}, u32[]{:S(2)}) copy-start(f32[1088,1024]{1,0:T(8,128)S(1)} %get-tuple-element.163) | copy-start | bytes 13369348
  267.4 46.1 %copy-start.47 = (bf16[1024,1536]{1,0:T(8,128)(2,1)S(1)}, bf16[1024,1536]{1,0:T(8,128)(2,1)}, u32[]{:S(2)}) copy-start(bf16[1024,1536]{1,0:T(8,128)(2,1)} %get-tuple-element.58) | copy-start | bytes 9437188
  320.6 28.7 %collective-permute-start.5 = (bf16[1088,1024]{1,0:T(8,128)(2,1)}, bf16[1088,1024]{1,0:T(8,128)(2,1)}, u32[]{:S(2)}, u32[]{:S(2)}) collective-permute-start(bf16[1088,1024]{1,0:T(8,128)(2,1)} %convolution_convert_fusion.6), channel_id=1, source_target_pairs={{0,4},{1,5},{2,6},{3,7},{4,0},{5,1},{6,2},{7,3},{8,12},{9,13},{10,... | collective-permute-start | bytes 6684680 | tf_op jit(solution)/shard_map/ppermute | solution.py:966
  326.1 8.2 %copy-start.14 = (bf16[1088,1024]{1,0:T(8,128)(2,1)S(1)}, bf16[1088,1024]{1,0:T(8,128)(2,1)}, u32[]{:S(2)}) copy-start(bf16[1088,1024]{1,0:T(8,128)(2,1)} %get-tuple-element.167) | copy-start | bytes 6684676
  336.2 13.0 %slice-start.2 = ((s8[4456448]{0:T(1024)(128)(4,1)}), s8[4194304]{0:T(1024)(128)(4,1)S(1)}, s32[]{:S(2)}) async-start(s8[4456448]{0:T(1024)(128)(4,1)} %bitcast.85), calls=%async_computation.2 | async-start | bytes 8388608
  336.2 17.9 %slice-start = ((s8[4456448]{0:T(1024)(128)(4,1)}), s8[4194304]{0:T(1024)(128)(4,1)S(1)}, s32[]{:S(2)}) async-start(s8[4456448]{0:T(1024)(128)(4,1)} %bitcast.83), calls=%async_computation | async-start | bytes 8388608
  341.2 8.1 %slice-start.3 = ((s8[4456448]{0:T(1024)(128)(4,1)}), s8[262144]{0:T(1024)(128)(4,1)S(1)}, s32[]{:S(2)}) async-start(s8[4456448]{0:T(1024)(128)(4,1)} %bitcast.85), calls=%async_computation.3 | async-start | bytes 524288
  341.2 12.9 %slice-start.1 = ((s8[4456448]{0:T(1024)(128)(4,1)}), s8[262144]{0:T(1024)(128)(4,1)S(1)}, s32[]{:S(2)}) async-start(s8[4456448]{0:T(1024)(128)(4,1)} %bitcast.83), calls=%async_computation.1 | async-start | bytes 524288
  492.1 8.8 %copy-start.26 = (f32[688,128]{1,0:T(8,128)S(1)}, f32[688,128]{1,0:T(8,128)}, u32[]{:S(2)}) copy-start(f32[688,128]{1,0:T(8,128)} %get-tuple-element.66) | copy-start | bytes 1056772
  492.1 9.5 %copy-start.25 = (f32[688,128]{1,0:T(8,128)S(1)}, f32[688,128]{1,0:T(8,128)}, u32[]{:S(2)}) copy-start(f32[688,128]{1,0:T(8,128)} %get-tuple-element.67) | copy-start | bytes 1056772
  492.1 11.6 %copy-start.30 = (f32[256,128]{1,0:T(8,128)S(1)}, f32[256,128]{1,0:T(8,128)}, u32[]{:S(2)}) copy-start(f32[256,128]{1,0:T(8,128)} %get-tuple-element.231) | copy-start | bytes 393220
  492.1 12.3 %copy-start.24 = (f32[688,128]{1,0:T(8,128)S(1)}, f32[688,128]{1,0:T(8,128)}, u32[]{:S(2)}) copy-start(f32[688,128]{1,0:T(8,128)} %get-tuple-element.68) | copy-start | bytes 1056772
  492.1 13.0 %copy-start.1 = (s32[2,1028]{1,0:T(2,128)S(1)}, s32[2,1028]{1,0:T(2,128)}, u32[]{:S(2)}) copy-start(s32[2,1028]{1,0:T(2,128)} %param.27) | copy-start | bytes 24676
  (38 other events, 212.7 us)

commit v3 on v2

--- a/solution.py
+++ b/solution.py
@@ -400,247 +400,237 @@
             act(m)
 
 
-def scatter_kernel(kinds, n_acts, sizes, *refs):
-    n_dp, n_tensor = sizes
-    n_w = len(kinds)
-    me = Place(n_dp, n_tensor)
-    half_z = n_tensor // 2
-    act_in, vec_in, g_in = refs[:n_acts], refs[n_acts], refs[n_acts + 1 : n_acts + 1 + n_w]
-    at = n_acts + 1 + n_w
-    act_out, vec_out, g_out = refs[at : at + n_acts], refs[at + n_acts], refs[at + n_acts + 1 : at + n_acts + 1 + n_w]
-    at += n_acts + 1 + n_w
-    acc, got, gotz, stage = (refs[at + i * n_w : at + (i + 1) * n_w] for i in range(4))
-    at += 4 * n_w
-    (v_sum, v_got, v_all) = refs[at : at + 3]
-    (a_send, a_recv, b_send, b_recv, z_send, z_recv, f_send, f_recv, vb_send, vb_recv, vz_send, vz_recv, vf_send, vf_recv, loc) = refs[at + 3 :]
-    me.barrier()
-
-    def local(src, dst, n):
-        return pltpu.make_async_copy(src, dst, loc.at[n])
-
-    def order(step, slot):
+class Scatter:
+    def __init__(self, me, kinds, g_in, keep, got, gotz, stage, g_out, sems):
+        self.me, self.kinds, self.g_in, self.keep, self.got = me, kinds, g_in, keep, got
+        self.gotz, self.stage, self.g_out = gotz, stage, g_out
+        self.b_send, self.b_recv, self.z_send, self.z_recv, self.f_send, self.f_recv, self.loc = sems
+
+    @staticmethod
+    def semaphores(n_w, sizes):
+        dma = pltpu.SemaphoreType.DMA
+        chips = sizes[0] // 2
+        bits = chips.bit_length() - 1
+        return [
+            dma((n_w, bits, 2, chips // 2)),
+            dma((n_w, bits, 2, chips // 2)),
+            dma((n_w, 2)),
+            dma((n_w, sizes[1])),
+            dma((n_w,)),
+            dma((n_w,)),
+            dma((n_w, 2, chips // 2)),
+        ]
+
+    def _count(self, step):
+        return 1 << (self.me.bits - 1 - step)
+
+    def _base(self, step):
+        return sum(self._count(s) for s in range(step))
+
+    def _first(self, j, slot, m, sent):
+        bits = self.me.bits
         if slot == 0:
-            return me.bits - 1 - step, 1, 1 << (me.bits - 1 - step)
-        return step, 1 << (step + 1), 1 << (me.bits - 1 - step)
-
-    def copies(j, step, slot):
-        bit, stride, count = order(step, slot)
-        source = g_in[j] if step == 0 else acc[j]
-
-        def send(m):
-            src = kinds[j].piece(source, slot, flipped(me.chip, m * stride + (1 << bit)))
-            dst = got[j].at[_base(me.bits, step) + m, slot]
-            return remote(src, dst, b_send.at[j, step, slot, m], b_recv.at[j, step, slot, m], me.beside(bit))
-
-        return send, count, stride
-
-    def start_bits(j, step):
+            flip = m + (1 << (bits - 1)) * sent
+        else:
+            flip = m * 2 + sent
+        return self.kinds[j].piece(self.g_in[j], slot, flipped(self.me.chip, flip))
+
+    def _held(self, j, step, slot, m, sent):
+        index = m + self._count(step) * sent if slot == 0 else 2 * m + sent
+        return self.got[j].at[self._base(step - 1) + index, slot]
+
+    def _copy(self, j, step, slot, m):
+        me = self.me
+        bit = me.bits - 1 - step if slot == 0 else step
+        src = self._first(j, slot, m, 1) if step == 0 else self._held(j, step, slot, m, 1)
+        return remote(
+            src,
+            self.got[j].at[self._base(step) + m, slot],
+            self.b_send.at[j, step, slot, m],
+            self.b_recv.at[j, step, slot, m],
+            me.beside(bit),
+        )
+
+    def _load(self, j, slot, m):
+        return pltpu.make_async_copy(self._first(j, slot, m, 0), self.keep[j].at[slot, m], self.loc.at[j, slot, m])
+
+    def start(self, j, step):
         for slot in range(2):
-            send, count, _ = copies(j, step, slot)
-            _each(count, lambda m: send(m).start())
-
-    def add_bits(j, step):
+            _each(self._count(step), lambda m: self._copy(j, step, slot, m).start())
+        if step == 0 and self.keep[j] is not None:
+            for slot in range(2):
+                _each(self._count(step), lambda m: self._load(j, slot, m).start())
+
+    def add(self, j, step):
         for slot in range(2):
-            send, count, stride = copies(j, step, slot)
 
             def one(m):
-                send(m).wait_recv()
-                here = kinds[j].piece(acc[j], slot, flipped(me.chip, m * stride))
-                here[...] = (
-                    here[...].astype(F32) + got[j][_base(me.bits, step) + m, slot].astype(F32)
-                ).astype(BF16)
-
-            _each(count, one)
-
-    def z_copy(j, slot):
-        target = half_z * me.core + slot
-        index = lax.rem(me.z - target + n_tensor - 1, n_tensor)
-        src = kinds[j].piece(acc[j], slot, me.chip)
-        return target, remote(src, gotz[j].at[index], z_send.at[j, slot], z_recv.at[j, index], (me.dp, target))
-
-    def start_z(j):
+                self._copy(j, step, slot, m).wait_recv()
+                if step > 0:
+                    mine = self._held(j, step, slot, m, 0)
+                elif self.keep[j] is not None:
+                    self._load(j, slot, m).wait()
+                    mine = self.keep[j].at[slot, m]
+                else:
+                    mine = self._first(j, slot, m, 0)
+                here = self.got[j].at[self._base(step) + m, slot]
+                here[...] = (here[...].astype(F32) + mine[...].astype(F32)).astype(BF16)
+
+            _each(self._count(step), one)
+
+    def _last(self, j, slot):
+        return self.got[j].at[self._base(self.me.bits - 1), slot]
+
+    def _z(self, j, slot):
+        me = self.me
+        target = me.nz // 2 * me.core + slot
+        index = lax.rem(me.z - target + me.nz - 1, me.nz)
+        return target, remote(
+            self._last(j, slot), self.gotz[j].at[index], self.z_send.at[j, slot], self.z_recv.at[j, index], (me.dp, target)
+        )
+
+    def start_z(self, j):
         for slot in range(2):
-            target, copy = z_copy(j, slot)
-            pl.when(target != me.z)(copy.start)
-
-    def last_copy(j):
-        return remote(stage[j], g_out[j], f_send.at[j], f_recv.at[j], me.across())
-
-    def end_z(j):
+            target, copy = self._z(j, slot)
+            pl.when(target != self.me.z)(copy.start)
+
+    def _hand(self, j):
+        return remote(self.stage[j], self.g_out[j], self.f_send.at[j], self.f_recv.at[j], self.me.across())
+
+    def end_z(self, j):
+        me = self.me
+
         @pl.when(me.home)
         def _():
-            for index in range(n_tensor - 1):
-                slab = gotz[j].at[index]
-                remote(slab, slab, z_send.at[j, 0], z_recv.at[j, index], me.across()).wait_recv()
+            for index in range(me.nz - 1):
+                slab = self.gotz[j].at[index]
+                remote(slab, slab, self.z_send.at[j, 0], self.z_recv.at[j, index], me.across()).wait_recv()
 
             def total(core):
-                value = kinds[j].one(acc[j], me.slot, me.chip, core)[...].astype(F32)
-                for index in range(n_tensor - 1):
-                    value = value + kinds[j].half(gotz[j].at[index], core)[...].astype(F32)
+                value = self.kinds[j].half(self._last(j, me.slot), core)[...].astype(F32)
+                for index in range(me.nz - 1):
+                    value = value + self.kinds[j].half(self.gotz[j].at[index], core)[...].astype(F32)
                 return value
 
-            stage[j][...] = total(1 - me.core)
-            last_copy(j).start()
-            g_out[j][...] = total(me.core)
-
-    def vec_bit(step):
-        return remote(v_sum.at[step], v_got.at[step], vb_send.at[step], vb_recv.at[step], me.beside(step))
-
-    def vec_z(s):
-        return remote(v_sum.at[me.bits], v_all.at[me.z], vz_send.at[s - 1], vz_recv.at[me.z], me.shifted(s))
-
-    def vec_last():
-        return remote(v_sum.at[me.bits + 1], vec_out.at[me.core], vf_send.at[0], vf_recv.at[0], me.across())
-
-    def vec_phase(step):
-        if step == 0:
-            v_sum[0] = vec_in[...]
-            vec_bit(0).start()
-        elif step <= me.bits:
-            vec_bit(step - 1).wait_recv()
-            v_sum[step] = v_sum[step - 1] + v_got[step - 1]
-            if step < me.bits:
-                vec_bit(step).start()
-            else:
-                for s in range(1, n_tensor):
-                    vec_z(s).start()
-                v_all[me.z] = v_sum[me.bits]
-        elif step == me.bits + 1:
-            for s in range(1, n_tensor):
-                src = lax.rem(me.z + s, n_tensor)
-                remote(v_all.at[src], v_all.at[src], vz_send.at[0], vz_recv.at[src], me.across()).wait_recv()
-            value = v_all[0]
-            for s in range(1, n_tensor):
-                value = value + v_all[s]
-            v_sum[me.bits + 1] = value
-            vec_last().start()
-            vec_out[me.core] = value
-        else:
-            there = vec_out.at[1 - me.core]
-            remote(there, there, vf_send.at[0], vf_recv.at[0], me.across()).wait_recv()
-
-    def act_copy(n, s):
-        place = lax.rem(me.z + s, n_tensor)
-        return remote(
-            act_in[n].at[place], act_out[n].at[me.slot], a_send.at[n, s - 1], a_recv.at[n, me.slot], (me.dp, place)
-        )
-
-    def start_acts(n):
-        @pl.when(me.home)
-        def _():
-            for s in range(1, n_tensor):
-                act_copy(n, s).start()
-            local(act_in[n].at[me.z], act_out[n].at[me.slot], n_w + n).start()
-
-    for j in range(n_w):
-        local(g_in[j], acc[j], j).start()
-    for n in range(n_acts):
-        start_acts(n)
-    phase = 0
-    lag = me.bits + 2
-    for tick in range(n_w + lag):
-        for step in range(lag):
-            j = tick - step
-            if 0 <= j < n_w:
-                if step == 0:
-                    start_bits(j, 0)
-                    local(g_in[j], acc[j], j).wait()
-                elif step <= me.bits:
-                    add_bits(j, step - 1)
-                    if step < me.bits:
-                        start_bits(j, step)
-                    else:
-                        start_z(j)
-                else:
-                    end_z(j)
-        if phase < me.bits + 3:
-            vec_phase(phase)
-            phase += 1
-    while phase < me.bits + 3:
-        vec_phase(phase)
-        phase += 1
-
-    for j in range(n_w):
+            self.stage[j][...] = total(1 - me.core)
+            self._hand(j).start()
+            self.g_out[j][...] = total(me.core)
+
+    def finish(self, j):
+        me = self.me
         for step in range(me.bits):
             for slot in range(2):
-                send, count, _ = copies(j, step, slot)
-                _each(count, lambda m: send(m).wait_send())
+                _each(self._count(step), lambda m: self._copy(j, step, slot, m).wait_send())
         for slot in range(2):
-            target, copy = z_copy(j, slot)
+            target, copy = self._z(j, slot)
             pl.when(target != me.z)(copy.wait_send)
-        pl.when(me.home)(last_copy(j).wait_send)
-        pl.when(jnp.logical_not(me.home))(last_copy(j).wait_recv)
-    for step in range(me.bits):
-        vec_bit(step).wait_send()
-    for s in range(1, n_tensor):
-        vec_z(s).wait_send()
-    vec_last().wait_send()
-    for n in range(n_acts):
-
-        @pl.when(me.home)
-        def _(n=n):
-            for s in range(1, n_tensor):
-                act_copy(n, s).wait_send()
-            local(act_in[n].at[me.z], act_out[n].at[me.slot], n_w + n).wait()
-
+        hand = self._hand(j)
+        pl.when(me.home)(hand.wait_send)
+        pl.when(jnp.logical_not(me.home))(hand.wait_recv)
+
+
+class Sums:
+    def __init__(self, me, v_sum, v_got, v_all, out, sems):
+        self.me, self.v_sum, self.v_got, self.v_all, self.out = me, v_sum, v_got, v_all, out
+        self.b_send, self.b_recv, self.z_send, self.z_recv, self.f_send, self.f_recv = sems
+
+    @staticmethod
+    def semaphores(sizes):
+        dma = pltpu.SemaphoreType.DMA
+        bits = (sizes[0] // 2).bit_length() - 1
+        return [dma((bits,)), dma((bits,)), dma((sizes[1],)), dma((sizes[1],)), dma((1,)), dma((1,))]
+
+    @staticmethod
+    def scratch(shape, sizes):
+        bits = (sizes[0] // 2).bit_length() - 1
+        return [
+            pltpu.VMEM((bits + 2,) + shape, F32),
+            pltpu.VMEM((bits,) + shape, F32),
+            pltpu.VMEM((sizes[1],) + shape, F32),
+        ]
+
+    def _bit(self, step):
+        return remote(
+            self.v_sum.at[step], self.v_got.at[step], self.b_send.at[step], self.b_recv.at[step], self.me.beside(step)
+        )
+
+    def _z(self, s):
+        me = self.me
+        return remote(
+            self.v_sum.at[me.bits], self.v_all.at[me.z], self.z_send.at[s], self.z_recv.at[me.z], me.shifted(s)
+        )
+
+    def _last(self):
+        me = self.me
+        return remote(self.v_sum.at[me.bits + 1], self.out.at[me.core], self.f_send.at[0], self.f_recv.at[0], me.across())
+
+    def phases(self):
+        me = self.me
+        self._bit(0).start()
+        yield
+        for step in range(1, me.bits + 1):
+            self._bit(step - 1).wait_recv()
+            self.v_sum[step] = self.v_sum[step - 1] + self.v_got[step - 1]
+            if step < me.bits:
+                self._bit(step).start()
+                yield
+        for s in range(1, me.nz):
+            self._z(s).start()
+        self.v_all[me.z] = self.v_sum[me.bits]
+        yield
+        for s in range(1, me.nz):
+            slab = self.v_all.at[lax.rem(me.z + s, me.nz)]
+            place = lax.rem(me.z + s, me.nz)
+            remote(slab, slab, self.z_send.at[0], self.z_recv.at[place], me.across()).wait_recv()
+        value = self.v_all[0]
+        for s in range(1, me.nz):
+            value = value + self.v_all[s]
+        self.v_sum[me.bits + 1] = value
+        self._last().start()
+        self.out[me.core] = value
+        yield
+        there = self.out.at[1 - me.core]
+        remote(there, there, self.f_send.at[0], self.f_recv.at[0], me.across()).wait_recv()
+        for step in range(me.bits):
+            self._bit(step).wait_send()
+        for s in range(1, me.nz):
+            self._z(s).wait_send()
+        self._last().wait_send()
+
+
+class Outward:
+    def __init__(self, me, src, dst, sems):
+        self.me, self.src, self.dst = me, src, dst
+        self.send, self.recv, self.loc = sems
+
+    @staticmethod
+    def semaphores(sizes):
+        dma = pltpu.SemaphoreType.DMA
+        return [dma((sizes[1],)), dma((2,)), dma((1,))]
+
+    def _copy(self, place):
+        me = self.me
+        return remote(
+            self.src.at[place], self.dst.at[me.slot], self.send.at[place], self.recv.at[me.slot], (me.dp, place)
+        )
+
+    def _stay(self, place):
+        return pltpu.make_async_copy(self.src.at[place], self.dst.at[self.me.slot], self.loc.at[0])
+
+    def start(self, place):
+        me = self.me
+        pl.when(jnp.logical_and(me.home, place != me.z))(lambda: self._copy(place).start())
+        pl.when(jnp.logical_and(me.home, place == me.z))(lambda: self._stay(place).start())
+
+    def finish(self):
+        me = self.me
+        for place in range(me.nz):
+            pl.when(jnp.logical_and(me.home, place != me.z))(lambda place=place: self._copy(place).wait_send())
+            pl.when(jnp.logical_and(me.home, place == me.z))(lambda place=place: self._stay(place).wait())
         for slot in range(2):
-            row = act_out[n].at[slot]
-            copy = remote(row, row, a_send.at[n, 0], a_recv.at[n, slot], me.across())
-            pl.when(me.core * half_z + slot != me.z)(copy.wait_recv)
-
-
-def _base(bits, step):
-    return sum(1 << (bits - 1 - s) for s in range(step))
-
-
-def scatter(acts, vec, grads, kinds, sizes, cid):
-    n_dp, n_tensor = sizes
-    chips = n_dp // 2
-    bits = chips.bit_length() - 1
-    n_a, n_w = len(acts), len(grads)
-    grads = [kind.cut(g) for kind, g in zip(kinds, grads)]
-    shapes = [jax.ShapeDtypeStruct((n_tensor // 2,) + a.shape[1:], a.dtype) for a in acts]
-    shapes += [jax.ShapeDtypeStruct((2,) + vec.shape, F32)]
-    shapes += [jax.ShapeDtypeStruct(k.shard, F32) for k in kinds]
-    dma = pltpu.SemaphoreType.DMA
-    hbm = pl.BlockSpec(memory_space=pltpu.HBM)
-    vmem = pl.BlockSpec(memory_space=pltpu.VMEM)
-    most = max(chips // 2, 1)
-    out = pl.pallas_call(
-        functools.partial(scatter_kernel, kinds, n_a, sizes),
-        out_shape=shapes,
-        in_specs=[hbm] * n_a + [vmem] + [hbm] * n_w,
-        out_specs=[hbm] * n_a + [vmem] + [vmem] * n_w,
-        scratch_shapes=[pltpu.VMEM(k.whole, BF16) for k in kinds]
-        + [pltpu.VMEM((chips - 1, 2) + k.two, BF16) for k in kinds]
-        + [pltpu.VMEM((n_tensor - 1,) + k.two, BF16) for k in kinds]
-        + [pltpu.VMEM(k.shard, F32) for k in kinds]
-        + [
-            pltpu.VMEM((bits + 2,) + vec.shape, F32),
-            pltpu.VMEM((bits,) + vec.shape, F32),
-            pltpu.VMEM((n_tensor,) + vec.shape, F32),
-            dma((n_a, n_tensor)),
-            dma((n_a, 2)),
-            dma((n_w, bits, 2, most)),
-            dma((n_w, bits, 2, most)),
-            dma((n_w, 2)),
-            dma((n_w, n_tensor)),
-            dma((n_w,)),
-            dma((n_w,)),
-            dma((bits,)),
-            dma((bits,)),
-            dma((n_tensor,)),
-            dma((n_tensor,)),
-            dma((1,)),
-            dma((1,)),
-            dma((n_w + n_a,)),
-        ],
-        compiler_params=pltpu.CompilerParams(
-            collective_id=cid, has_side_effects=True, vmem_limit_bytes=56 * 2**20
-        ),
-        name=f"scatter{cid}",
-    )(*acts, vec, *grads)
-    return out[:n_a], out[n_a], [k.leave(g) for k, g in zip(kinds, out[n_a + 1 :])]
+            row = self.dst.at[slot]
+            copy = remote(row, row, self.send.at[0], self.recv.at[slot], me.across())
+            pl.when(me.core * (me.nz // 2) + slot != me.z)(copy.wait_recv)
 
 
 KEYS = 1152
@@ -842,26 +832,106 @@
     return out[:4], [k.join(w) for k, w in zip(kinds, out[4:9])], out[9:]
 
 
-def attention_backward_kernel(
-    sub, qa_ref, ka_ref, va_ref, do_ref, mix_ref, cos_ref, up_ref, down_ref,
-    out_ref, sum_ref, da_ref, dq_ref, dk_ref, dv_ref,
+def back_kernel(
+    kinds, sizes, n_late,
+    out_in, g_d, g_g, g_u, g_o, qa_in, ka_in, va_in, do_in, mix_in, normed_in, w_in, x_in, dmid_in,
+    cos_ref, up_ref, down_ref, gain_ref, vec_ref,
+    out_rows, in_rows, vec_out, s_d, s_g, s_u, s_o, s_qkv,
+    *rest,
 ):
-    rows = do_ref.shape[0]
+    me = Place(*sizes)
+    nz, bits = me.nz, me.bits
+    n_w = len(kinds)
+    keep = rest[: n_w - 1] + (None,)
+    rest = rest[n_w - 1 :]
+    got, gotz, stage = (rest[i * n_w : (i + 1) * n_w] for i in range(3))
+    rest = rest[3 * n_w :]
+    v_sum, v_got, v_all = rest[:3]
+    (qa, ka, va, do, mix, normed, w, x_ref, dmid, d_qkv, g_qkv, part, theirs, da, dq, dk, dv, dgain, dshift) = rest[3:22]
+    sems = rest[22:]
+    scatter = Scatter(
+        me, kinds, (g_d, g_g, g_u, g_o, g_qkv), keep, got, gotz, stage, (s_d, s_g, s_u, s_o, s_qkv), sems[:7]
+    )
+    sums = Sums(me, v_sum, v_got, v_all, vec_out, sems[7:13])
+    outs = Outward(me, out_in, out_rows, sems[13:16])
+    ins = Outward(me, theirs, in_rows, sems[16:19])
+    pair_sem, late_sem, tile_sem, p_send, p_recv = sems[19:24]
+
+    block, width = x_ref.shape[1:]
+    rows = block * nz
     lanes = 2 * HEAD
-    tiles = rows // TILE
-    lane = lax.broadcasted_iota(jnp.int32, (TILE, lanes), 1)
+    pairs = mix_in.shape[1] // lanes
+    sub = pairs // 2
+    lane = lax.broadcasted_iota(jnp.int32, (block, lanes), 1)
     low = lane < HEAD
-    g = pl.program_id(0)
-
-    da_ref[pl.ds(rows, KEYS - rows), :] = jnp.zeros((KEYS - rows, lanes), BF16)
-    for h in range(2):
-
-        @pl.loop(0, tiles)
-        def _(t, h=h):
-            here = pl.ds(pl.multiple_of(t * TILE, TILE), TILE)
-            d = do_ref[here, :].astype(F32)
+
+    def loads(g):
+        slot = g % 2
+        heads = pl.ds(2 * g, 2)
+        cols = pl.ds(g * lanes, lanes)
+        return [
+            pltpu.make_async_copy(qa_in.at[heads], qa.at[slot], pair_sem.at[slot, 0]),
+            pltpu.make_async_copy(ka_in.at[heads], ka.at[slot], pair_sem.at[slot, 1]),
+            pltpu.make_async_copy(va_in.at[heads], va.at[slot], pair_sem.at[slot, 2]),
+            pltpu.make_async_copy(do_in.at[:, cols], do.at[slot], pair_sem.at[slot, 3]),
+            pltpu.make_async_copy(mix_in.at[:, cols], mix.at[slot], pair_sem.at[slot, 4]),
+        ]
+
+    late = [
+        pltpu.make_async_copy(normed_in, normed, late_sem.at[0]),
+        pltpu.make_async_copy(w_in, w, late_sem.at[1]),
+    ]
+
+    def tile_loads(t):
+        slot = t % 2
+        return [
+            pltpu.make_async_copy(x_in.at[t], x_ref.at[slot], tile_sem.at[slot, 0]),
+            pltpu.make_async_copy(dmid_in.at[t], dmid.at[slot], tile_sem.at[slot, 1]),
+        ]
+
+    me.barrier()
+    scatter.start(0, 0)
+    for copy in loads(0):
+        copy.start()
+    for place in range(nz):
+        outs.start(place)
+    for copy in late:
+        copy.start()
+    for t in range(2):
+        for copy in tile_loads(t):
+            copy.start()
+    v_sum[0] = vec_ref[...]
+
+    def on_the_way():
+        for j in range(n_w - 1):
+            for step in range(bits):
+                scatter.add(j, step)
+                if step + 1 < bits:
+                    scatter.start(j, step + 1)
+                else:
+                    scatter.start_z(j)
+                if step == 0 and j + 1 < n_w - 1:
+                    scatter.start(j + 1, 0)
+                yield
+            if j > 0:
+                scatter.end_z(j - 1)
+                yield
+        scatter.end_z(n_w - 2)
+        yield
+
+    events = on_the_way()
+
+    def head(g, h):
+        slot = g % 2
+
+        @pl.loop(0, nz)
+        def _(t):
+            here = pl.ds(pl.multiple_of(t * block, block), block)
+            d = do[slot, here, :].astype(F32)
             mine = low if h == 0 else jnp.logical_not(low)
-            delta = -jnp.sum(jnp.where(mine, d * mix_ref[here, :].astype(F32), 0.0), axis=1, keepdims=True)
+            delta = -jnp.sum(
+                jnp.where(mine, d * mix[slot, here, :].astype(F32), 0.0), axis=1, keepdims=True
+            )
             if h:
                 d = pltpu.roll(d, HEAD, 1)
             first = delta.astype(BF16)
@@ -873,72 +943,180 @@
                 first.astype(F32),
                 jnp.where(lane == HEAD + 1, second.astype(F32), third.astype(F32)),
             )
-            da_ref[here, :] = jnp.where(low, d, jnp.where(lane < HEAD + 3, logs, 0.0)).astype(BF16)
-
-        dk_ref[h] = jnp.zeros((KEYS, lanes), F32)
-        dv_ref[h] = jnp.zeros((KEYS, lanes), F32)
+            da[here, :] = jnp.where(low, d, jnp.where(lane < HEAD + 3, logs, 0.0)).astype(BF16)
+
+        dk[h] = jnp.zeros((KEYS, lanes), F32)
+        dv[h] = jnp.zeros((KEYS, lanes), F32)
 
         @pl.loop(0, KEYS // COLS)
-        def _(t, h=h):
+        def _(t):
             here = pl.ds(pl.multiple_of(t * COLS, COLS), COLS)
-            q = qa_ref[h, here, :]
-            d = da_ref[here, :]
-            p = jnp.exp2(matmul_right_t(ka_ref[h], q))
-            ds = (p * matmul_right_t(va_ref[h], d)).astype(BF16)
-            dv_ref[h] += matmul(p.astype(BF16), d)
-            dk_ref[h] += matmul(ds, q)
-            dq_ref[h, here, :] = matmul_left_t(ds, ka_ref[h])
-
-    def put(column, row, ref, factor, turn):
-        total = jnp.zeros((1, lanes), F32)
-        for t in range(tiles):
-            here = pl.ds(t * TILE, TILE)
+            q = qa[slot, h, here, :]
+            d = da[here, :]
+            p = jnp.exp2(matmul_right_t(ka[slot, h], q))
+            ds = (p * matmul_right_t(va[slot, h], d)).astype(BF16)
+            dv[h] += matmul(p.astype(BF16), d)
+            dk[h] += matmul(ds, q)
+            dq[h, here, :] = matmul_left_t(ds, ka[slot, h])
+
+    def put(g, part_of, row, ref, factor, turn):
+        at = ((g // sub) * (3 * sub) + part_of * sub + g % sub) * lanes
+
+        def one(t, total):
+            here = pl.ds(pl.multiple_of(t * block, block), block)
             value = jnp.where(low, ref[0, here, :], pltpu.roll(ref[1, here, :], HEAD, 1))
             if factor is not None:
                 value = value * factor
             if turn:
                 value = _turn(value, cos_ref[here, :], -up_ref[here, :], -down_ref[here, :])
-            if row is not None:
-                total = total + jnp.sum(value, axis=0, keepdims=True)
-            at = pl.multiple_of(column * (sub * lanes) + lax.rem(g, sub) * lanes, lanes)
-            out_ref[here, pl.ds(at, lanes)] = value.astype(BF16)
+            d_qkv[here, at : at + lanes] = value.astype(BF16)
+            return total + jnp.sum(value, axis=0, keepdims=True)
+
+        total = lax.fori_loop(0, nz, one, jnp.zeros((1, lanes), F32))
         if row is not None:
-            sum_ref[0, pl.ds(row, 1), :] = total
-
-    put(0, 0, dq_ref, SCALE, True)
-    put(1, None, dk_ref, LN2, True)
-    put(2, 1, dv_ref, None, False)
-
-
-def attention_backward(qa, ka, va, d_mixed, mixed, tables):
-    rows = mixed.shape[0]
+            v_sum[0, row : row + 1, :] = total
+
+    da[pl.ds(rows, KEYS - rows), :] = jnp.zeros((KEYS - rows, lanes), BF16)
+
+    def weight_gradient(slot):
+        chunk = kinds[-1].two[0]
+        columns = pl.ds(slot * 3 * sub * lanes, 3 * sub * lanes)
+        grad = d_qkv[:, slot * 3 * sub * lanes : (slot + 1) * 3 * sub * lanes]
+        step = max(chunk, lanes)
+        for c in range(width // step):
+            left = normed[:, c * step : (c + 1) * step]
+            g_qkv[c * step : (c + 1) * step, columns] = matmul_left_t(left, grad).astype(BF16)
+
+    for g in range(pairs):
+        for copy in loads(g):
+            copy.wait()
+        if g + 1 < pairs:
+            for copy in loads(g + 1):
+                copy.start()
+        for h in range(2):
+            head(g, h)
+            next(events, None)
+        base_row = n_late + (g // sub) * (2 * sub) + g % sub
+        put(g, 0, base_row, dq, SCALE, True)
+        put(g, 1, None, dk, LN2, True)
+        put(g, 2, base_row + sub, dv, None, False)
+        if g == 0:
+            for copy in late:
+                copy.wait()
+        if g % sub == sub - 1:
+            weight_gradient(g // sub)
+        next(events, None)
+
+    def swap(t):
+        return remote(part.at[t], theirs.at[t], p_send.at[t], p_recv.at[t], me.across())
+
+    for t in range(nz):
+        here = slice(t * block, (t + 1) * block)
+        part[t] = matmul_right_t(d_qkv[here, :], w[...]).astype(BF16)
+        swap(t).start()
+    for _ in range(2):
+        next(events, None)
+    dgain[...] = jnp.zeros_like(dgain)
+    dshift[...] = jnp.zeros_like(dshift)
+    for t in range(nz):
+        for copy in tile_loads(t):
+            copy.wait()
+        x = x_ref[t % 2].astype(F32)
+        x = x - jnp.sum(x, axis=1, keepdims=True) * (1.0 / width)
+        var = jnp.sum(x * x, axis=1, keepdims=True) * (1.0 / width)
+        scale = lax.rsqrt(var + EPS)
+        x = x * scale
+        swap(t).wait_recv()
+        dn = part[t].astype(F32) + theirs[t].astype(F32)
+        dgain[...] += jnp.sum(dn * x, axis=0, keepdims=True)
+        dshift[...] += jnp.sum(dn, axis=0, keepdims=True)
+        v = dn * gain_ref[...]
+        mean = jnp.sum(v, axis=1, keepdims=True) * (1.0 / width)
+        along = jnp.sum(v * x, axis=1, keepdims=True) * (1.0 / width)
+        theirs[t] = (dmid[t % 2] + scale * (v - mean - x * along)).astype(BF16)
+        ins.start(t)
+        if t + 2 < nz:
+            for copy in tile_loads(t + 2):
+                copy.start()
+    per = width // lanes
+    for i in range(per):
+        v_sum[0, i : i + 1, :] = dgain[:, i * lanes : (i + 1) * lanes]
+        v_sum[0, per + i : per + i + 1, :] = dshift[:, i * lanes : (i + 1) * lanes]
+    small = sums.phases()
+    next(small, None)
+    started = False
+    for _ in events:
+        next(small, None)
+    last = n_w - 1
+    scatter.start(last, 0)
+    for step in range(bits):
+        next(small, None)
+        scatter.add(last, step)
+        if step + 1 < bits:
+            scatter.start(last, step + 1)
+        else:
+            scatter.start_z(last)
+    for _ in small:
+        pass
+    scatter.end_z(last)
+    for t in range(nz):
+        swap(t).wait_send()
+    outs.finish()
+    ins.finish()
+    for j in range(n_w):
+        scatter.finish(j)
+
+
+def back(out_act, grads, heads, d_mixed, mixed, normed, w, x, dmid, tables, gain, vec, kinds, n_late, sizes, cid):
+    n_dp, nz = sizes
+    chips = n_dp // 2
+    n_w = len(kinds)
+    block, width = x.shape[1:]
+    rows = block * nz
     lanes = 2 * HEAD
-    pairs = mixed.shape[1] // lanes
-    sub = pairs // 2
-    heads = pl.BlockSpec((2, KEYS, lanes), lambda g: (g, 0, 0))
-    pair = pl.BlockSpec((rows, lanes), lambda g: (0, g))
-    return pl.pallas_call(
-        functools.partial(attention_backward_kernel, sub),
-        grid=(pairs,),
-        out_shape=[
-            jax.ShapeDtypeStruct((rows, 3 * pairs * lanes), BF16),
-            jax.ShapeDtypeStruct((pairs, 8, lanes), F32),
-        ],
-        in_specs=[heads, heads, heads, pair, pair]
-        + [pl.BlockSpec((rows, lanes), lambda g: (0, 0))] * 3,
-        out_specs=[
-            pl.BlockSpec((rows, 3 * sub * lanes), lambda g: (0, g // sub)),
-            pl.BlockSpec((1, 8, lanes), lambda g: (g, 0, 0)),
-        ],
-        scratch_shapes=[
+    hbm = pl.BlockSpec(memory_space=pltpu.HBM)
+    vmem = pl.BlockSpec(memory_space=pltpu.VMEM)
+    shape = jax.ShapeDtypeStruct
+    dma = pltpu.SemaphoreType.DMA
+    grads = [k.cut(g) for k, g in zip(kinds, grads)]
+    out = pl.pallas_call(
+        functools.partial(back_kernel, kinds, sizes, n_late),
+        out_shape=[shape((nz // 2, block, width), BF16)] * 2
+        + [shape((2,) + vec.shape, F32)]
+        + [shape(k.shard, F32) for k in kinds],
+        in_specs=[hbm] * 14 + [vmem] * 5,
+        out_specs=[hbm, hbm] + [vmem] * (1 + n_w),
+        scratch_shapes=[pltpu.VMEM((2, chips // 2) + k.two, BF16) for k in kinds[:-1]]
+        + [pltpu.VMEM((chips - 1, 2) + k.two, BF16) for k in kinds]
+        + [pltpu.VMEM((nz - 1,) + k.two, BF16) for k in kinds]
+        + [pltpu.VMEM(k.shard, F32) for k in kinds]
+        + Sums.scratch(vec.shape, sizes)
+        + [pltpu.VMEM((2, 2, KEYS, lanes), BF16)] * 3
+        + [pltpu.VMEM((2, rows, lanes), BF16)] * 2
+        + [
+            pltpu.VMEM((rows, width), BF16),
+            pltpu.VMEM(w.shape, BF16),
+            pltpu.VMEM((2, block, width), BF16),
+            pltpu.VMEM((2, block, width), F32),
+            pltpu.VMEM((rows, w.shape[1]), BF16),
+            pltpu.VMEM((width, w.shape[1]), BF16),
+            pltpu.VMEM((nz, block, width), BF16),
+            pltpu.VMEM((nz, block, width), BF16),
             pltpu.VMEM((KEYS, lanes), BF16),
-            pltpu.VMEM((2, KEYS, lanes), F32),
-            pltpu.VMEM((2, KEYS, lanes), F32),
-            pltpu.VMEM((2, KEYS, lanes), F32),
-        ],
-        compiler_params=pltpu.CompilerParams(vmem_limit_bytes=48 * 2**20),
-        name="attention_backward",
-    )(qa, ka, va, d_mixed, mixed, *tables)
+        ]
+        + [pltpu.VMEM((2, KEYS, lanes), F32)] * 3
+        + [pltpu.VMEM((1, width), F32)] * 2
+        + Scatter.semaphores(n_w, sizes)
+        + Sums.semaphores(sizes)
+        + Outward.semaphores(sizes)
+        + Outward.semaphores(sizes)
+        + [dma((2, 5)), dma((2,)), dma((2, 2)), dma((nz,)), dma((nz,))],
+        compiler_params=pltpu.CompilerParams(
+            collective_id=cid, has_side_effects=True, vmem_limit_bytes=62 * 2**20
+        ),
+        name="back",
+    )(out_act, *grads, *heads, d_mixed, mixed, normed, w, x, dmid, *tables, gain[None], vec)
+    return out[:2], out[2], [k.leave(g) for k, g in zip(kinds, out[3:])]
 
 
 def shards(
@@ -978,9 +1156,6 @@
 
     def pad_rows(value):
         return jnp.pad(value, ((0, 0), (0, block_pad - block), (0, 0)))
-
-    def unpadded(value):
-        return value.reshape(n_tensor, block_pad, width)[:, :block]
 
     small = jnp.concatenate(
         [query_bias, value_bias]
@@ -1056,9 +1231,9 @@
     g_gain = jnp.sum(dn * nhat, axis=0)
     g_shift = jnp.sum(dn, axis=0)
     dnh = dn * gain
-    back = jnp.stack([jnp.sum(dnh, axis=-1), jnp.sum(dnh * nhat, axis=-1)])
-    back = back + other(back)
-    dact = r * (dnh - columns * (back[0][:, None] + nhat * back[1][:, None]) / count_live)
+    rsums = jnp.stack([jnp.sum(dnh, axis=-1), jnp.sum(dnh * nhat, axis=-1)])
+    rsums = rsums + other(rsums)
+    dact = r * (dnh - columns * (rsums[0][:, None] + nhat * rsums[1][:, None]) / count_live)
     dgate = dact * up * sig * (1.0 + gate * (1.0 - sig))
     dup = dact * gate * sig
     g_gate_bias = jnp.sum(dgate, axis=0)
@@ -1077,43 +1252,44 @@
     dmid_low = dmiddle.astype(BF16)
     g_out = matmul_left_t(mixed, dmid_low).astype(BF16)
     d_mixed = matmul_right_t(dmid_low, full_o).astype(BF16)
-    d_qkv, qv_sums = attention_backward(qa, ka, va, d_mixed, mixed, tables)
-    g_qkv = matmul_left_t(normed, d_qkv).astype(BF16)
-    part = matmul_right_t(d_qkv, full_qkv).astype(BF16)
-    dnormed = part.astype(F32) + other(part).astype(F32)
-    g_attn_gain = jnp.sum(dnormed * xhat1, axis=0)
-    g_attn_shift = jnp.sum(dnormed, axis=0)
-    input_grad = dmiddle + norm_backward(dnormed, xhat1, s1, attention_norm_gain)
-
-    def by_slot(vec):
-        return vec.reshape(2, -1)
-
-    vec = jnp.concatenate(
-        [g_attn_gain, g_attn_shift, g_out_bias, g_mlp_gain, g_mlp_shift, g_down_bias]
-        + [
-            jnp.concatenate(
-                [by_slot(v) for v in (qv_sums[:, 0], qv_sums[:, 1], g_gate_bias, g_up_bias, g_gain, g_shift)], axis=1
-            ).reshape(-1)
-        ]
+    early = jnp.concatenate([g_out_bias, g_mlp_gain, g_mlp_shift, g_down_bias])
+    late_rows = 2 * width // LANES
+    qv_rows = 4 * n_head // LANES
+    tall = jnp.concatenate(
+        [v.reshape(2, -1) for v in (g_gate_bias, g_up_bias, g_gain, g_shift)], axis=1
+    ).reshape(-1)
+    vec = jnp.concatenate([jnp.zeros(((late_rows + qv_rows) * LANES,), F32), early, tall])
+    vec_rows = up_to(up_to(vec.shape[0], LANES) // LANES, 8)
+    vec = jnp.pad(vec, (0, vec_rows * LANES - vec.shape[0])).reshape(vec_rows, LANES)
+    (out_rows, in_rows), vec, (s_down, s_gate, s_up, s_out, s_qkv) = back(
+        output.reshape(n_tensor, block_pad, width),
+        [g_down, g_gate, g_up, g_out],
+        [qa, ka, va],
+        d_mixed,
+        mixed,
+        normed,
+        full_qkv,
+        image,
+        dmiddle.reshape(n_tensor, block_pad, width),
+        tables,
+        attention_norm_gain,
+        vec,
+        [kind_f, kind_f, kind_f, kind_o, kind_qkv],
+        late_rows,
+        sizes,
+        1,
     )
-    vec_size = vec.shape[0]
-    vec_rows = up_to(up_to(vec_size, LANES) // LANES, 8)
-    vec = jnp.pad(vec, (0, vec_rows * LANES - vec_size)).reshape(vec_rows, LANES)
-    (out_rows, in_rows), vec, (s_down, s_gate, s_up, s_out, s_qkv) = scatter(
-        [unpadded(output), unpadded(input_grad.astype(BF16))],
-        vec,
-        [g_down, g_gate, g_up, g_out, g_qkv],
-        [kind_f, kind_f, kind_f, kind_o, kind_qkv],
-        sizes,
-        2,
-    )
+    out_rows, in_rows = out_rows[:, :block], in_rows[:, :block]
     vec = vec.reshape(2, -1)
-    wide = vec[0, : 6 * width].reshape(6, width)
     owner = z // (n_tensor // 2)
-    tall = lax.dynamic_index_in_dim(vec, owner, 0, False)[6 * width : vec_size].reshape(2, -1)
+    mine = lax.dynamic_index_in_dim(vec, owner, 0, False)
+    d_at = (late_rows + qv_rows) * LANES
+    wide = jnp.concatenate([vec[0, : 2 * width], vec[0, d_at : d_at + 4 * width]]).reshape(6, width)
+    qv = lax.dynamic_index_in_dim(mine[late_rows * LANES : d_at].reshape(2, -1), z % (n_tensor // 2), 0, False)
+    tall = mine[d_at + 4 * width : d_at + 4 * width + 8 * ff].reshape(2, -1)
     tall = lax.dynamic_index_in_dim(tall, z % (n_tensor // 2), 0, False)
-    pieces, at = [], 0
-    for size in [n_head] * 2 + [ff] * 4:
+    pieces, at = [qv[:n_head], qv[n_head:]], 0
+    for size in [ff] * 4:
         pieces.append(tall[at : at + size])
         at += size
     return (

time: 512 us -> 449 us (0.88)
  the two profiles are of different devices: /device:TPU:0 before, /device:TPU:27 now
where the time goes in v3:
time: 449 us; the launch traced here: 445 us
  Pallas kernels  311 us (69%)
  matrix products  62.7 us (14%)
  other arithmetic  33.3 us (7%)
  local copies, waits for them, and re-layouts  26.4 us (6%)
  starting transfers between devices  5.74 us (1%)
    pallas_call x1, Pallas kernels, back(): pl.pallas_call(functools.partial(back_kernel, kinds, sizes, n_late), out_...  163 us
    pallas_call x1, Pallas kernels, front(): pl.pallas_call(functools.partial(front_kernel, kinds, sizes), out_shape=s...  148 us
    dot_general x4, matrix products, matmul_left_t(): lax.dot_general(left, right, (((0,), (0,)), ((), ())), preferred_element_...  22.3 us
    dot_general x4, matrix products, matmul(): return jnp.dot(left, right, preferred_element_type=F32)  15.5 us
    unnamed x138, local copies, waits for them, and re-layouts  15 us
    dot_general x3, matrix products, matmul_right_t(): lax.dot_general(left, right, (((1,), (1,)), ((), ())), preferred_element_...  14.6 us
    reduce_sum x1, other arithmetic, shards(): g_up_bias = jnp.sum(dup, axis=0)  11 us
    dot_general x1, matrix products, shards(): lax.dot_general(grad_low, full_d, (((1,), (1,)), ((), ())), preferred_ele...  10.3 us
  transfers between devices with their start and end apart: 5, of which 2 were waited for; matrix products, arithmetic and copies ran while one was open for 12% of the time, Pallas kernels for 0%

profile of v3, /device:TPU:27, one launch (start us, length us, event | category | flops | bytes accessed | tf_op | source)
XLA Modules:
  0.0 445.0 jit_solution(17193870592583852854)
XLA Ops:
  6.4 1.9 copy.53
  12.8 147.9 %front.1 = (bf16[4,272,1024]{2,1,0:T(8,128)(2,1)}, bf16[4,272,1024]{2,1,0:T(8,128)(2,1)}, f32[2,32,128]{2,1,0:T(8,128)S(1)}, bf16[1152,128]{1,0:T(8,128)(2,1)S(1...) custom-call(bf16[2,272,1024]{2,1,0:T(8,128)(2,1)} %pad.59.tok_in, ...), custom_call_target="tpu_custom_call" | custom-call | tf_op jit(solution)/shard_map/front/pallas_call | solution.py:818
  160.8 2.7 convolution_convert_fusion
  163.5 4.9 %collective-permute-start = (bf16[1088,1024]{1,0:T(8,128)(2,1)}, bf16[1088,1024]{1,0:T(8,128)(2,1)}, u32[]{:S(2)}, u32[]{:S(2)}) collective-permute-start(bf16[1088,1024]{1,0:T(8,128)(2,1)} %convolution_convert_fusion), channel_id=1, source_target_pairs={{0,4},{1,5},{2,6},{3,7},{4,0},{5,1},{6,2},{7,3},{8,12},{9,13},{10,... | collective-permute-start | bytes 6684680 | tf_op jit(solution)/shard_map/ppermute | solution.py:1144
  171.0 1.7 collective-permute-done
  173.9 3.4 fusion.38
  179.3 2.2 copy-done.49
  181.5 3.7 convolution_add_fusion.1
  185.3 8.4 %multiply_reduce_fusion.3 = (f32[1088]{0:T(1024)S(1)}, f32[1088]{0:T(1024)S(1)}, f32[1088,1376]{1,0:T(8,128)}, f32[1088,1376]{1,0:T(8,128)}) fusion(f32[1376]{0:T(1024)S(1)} %mul.198, f32[1088,1376]{1,0:T(8,128)S(1)} %convolution_add_fusion.1, f32[1376]{0:T(1024)S(1)} %add.205, bf16[1088,1024]{1,0:T(8,128)(2,1)S(1)} %add_convert_fusion.1, ...), kind=kOutput, calls=%fused_computation.11 | convolution fusion | flops 3082502144 | bytes 23031040 | tf_op jit(solution)/shard_map/dot_general | solution.py:80
  195.1 10.3 %multiply_reduce_fusion = (f32[1376]{0:T(1024)S(1)}, f32[1088]{0:T(1024)S(1)}, f32[1088]{0:T(1024)S(1)}, f32[1376]{0:T(1024)S(1)}, f32[1088,1376]{1,0:T(8,128)}) fusion(f32[1088,1376]{1,0:T(8,128)} %get-tuple-element.152, f32[1088]{0:T(1024)S(1)} %add_rsqrt_fusion, f32[1088]{0:T(1024)S(1)} %get-tuple-element.144, f32[1376]{0:T(1024)S(1)} %mul.212, ...), kind=kOutput, calls=%fused_computation.3 | convolution fusion | flops 3081002496 | bytes 17062400 | tf_op jit(solution)/shard_map/dot_general | solution.py:1228
  205.6 5.2 %convolution_convert_fusion.4 = bf16[1088,1024]{1,0:T(8,128)(2,1)} fusion(bf16[1376,1024]{1,0:T(8,128)(2,1)S(1)} %copy-done.51, f32[1088,1376]{1,0:T(8,128)S(1)} %copy-done.15, f32[1376]{0:T(1024)S(1)} %add.210, f32[1376]{0:T(1024)S(1)} %mul.212, f32[1088]{0:T(1024)S(1)} %add_rsqrt_fusion, f32[1088]{0:T(1024)S(1)} %get-tuple-element.144, f32[1376]{0:T(1024)S(1)} %mul.198), kind=kOutput, calls=%fused_computation.35 | convolution fusion | flops 3076132864 | bytes 11059840 | tf_op jit(solution)/shard_map/dot_general | solution.py:76
  211.4 11.0 %fusion.35 = (f32[1376]{0:T(1024)S(1)}, bf16[1088,1376]{1,0:T(8,128)(2,1)S(1)}, f32[1376]{0:T(1024)S(1)}, bf16[1088,1376]{1,0:T(8,128)(2,1)S(1)}) fusion(f32[1088,1376]{1,0:T(8,128)} %copy-done.16, f32[1088]{0:T(1024)S(1)} %get-tuple-element.143, f32[1088,1376]{1,0:T(8,128)} %get-tuple-element.152, f32[1088]{0:T(1024)S(1)} %get-tuple-element.144, ...), kind=kLoop, calls=%fused_computation.138 | loop fusion | flops 35927360 | bytes 29981184 | tf_op jit(solution)/shard_map/reduce_sum | solution.py:1240
  222.4 3.6 fusion.7
  226.1 3.9 fusion.3
  230.3 6.2 %convolution_convert_fusion.3.g_d = bf16[1376,1024]{1,0:T(8,128)(2,1)} fusion(bf16[1088,1024]{1,0:T(8,128)(2,1)S(1)} %copy-done.21, f32[1088,1376]{1,0:T(8,128)S(1)} %bitcast.77, f32[1376]{0:T(1024)S(1)} %add.210, f32[1376]{0:T(1024)S(1)} %mul.212, f32[1088]{0:T(1024)S(1)} %add_rsqrt_fusion, f32[1088]{0:T(1024)S(1)} %get-tuple-element.144, f32[1376]{0:T(1024)S(1)} %mul.198), kind=kOutput, calls=%fused_computation.34 | convolution fusion | flops 3076427776 | bytes 11059840 | tf_op jit(solution)/shard_map/dot_general | solution.py:84
  236.5 5.6 %convolution_convert_fusion.1.g_u = bf16[1376,1024]{1,0:T(8,128)(2,1)} fusion(bf16[1088,1024]{1,0:T(8,128)(2,1)S(1)} %copy-done.19, bf16[1088,1376]{1,0:T(8,128)(2,1)S(1)} %get-tuple-element.147), kind=kOutput, calls=%fused_computation.32 | convolution fusion | flops 3067445248 | bytes 8040448 | tf_op jit(solution)/shard_map/dot_general | solution.py:84
  242.4 8.0 %convolution_convert_fusion.2.g_g = bf16[1376,1024]{1,0:T(8,128)(2,1)} fusion(bf16[1088,1024]{1,0:T(8,128)(2,1)} %copy-done.18, bf16[1088,1376]{1,0:T(8,128)(2,1)} %copy-done.17), kind=kOutput, calls=%fused_computation.33 | convolution fusion | flops 3067445248 | bytes 8040448 | tf_op jit(solution)/shard_map/dot_general | solution.py:84
  250.4 5.1 %multiply_reduce_fusion.5 = (f32[1024]{0:T(1024)S(1)}, f32[1088]{0:T(1024)S(1)}, f32[1088]{0:T(1024)S(1)}, f32[1024]{0:T(1024)S(1)}) fusion(bf16[1088,1024]{1,0:T(8,128)(2,1)} %collective-permute-done.4, bf16[1088,1024]{1,0:T(8,128)(2,1)S(1)} %fusion.3, f32[1088,1024]{1,0:T(8,128)} %copy-done.11, f32[1088]{0:T(1024)S(1)} %add_rsqrt_fusion.1, ...), kind=kLoop, calls=%fused_computation.20 | loop fusion | flops 13365120 | bytes 8942592 | tf_op jit(solution)/shard_map/reduce_sum | solution.py:1247
  255.6 7.9 %fusion.37 = (f32[1024]{0:T(1024)S(1)}, f32[1088,1024]{1,0:T(8,128)S(1)}, bf16[1088,1024]{1,0:T(8,128)(2,1)}) fusion(f32[1088]{0:T(1024)S(1)} %broadcast_multiply_fusion.2, f32[1088,1024]{1,0:T(8,128)} %copy-done.11, f32[1088]{0:T(1024)S(1)} %broadcast_multiply_fusion.4, f32[1088]{0:T(1024)S(1)} %broadcast_multiply_fusion.3, f32[1024]{0:T(1024)S(1)} %copy-done.36, ...), kind=kLoop, calls=%fused_computation.140 | loop fusion | flops 20052992 | bytes 24540160 | tf_op jit(solution)/shard_map/reduce_sum | solution.py:1250
  263.5 2.4 convolution_convert_fusion.5.do_in
  266.0 2.6 convolution_convert_fusion.6.g_o
  269.2 162.9 %back.1 = (bf16[2,272,1024]{2,1,0:T(8,128)(2,1)}, bf16[2,272,1024]{2,1,0:T(8,128)(2,1)}, f32[2,104,128]{2,1,0:T(8,128)}, f32[688,128]{1,0:T(8,128)}, f32[688,128...) custom-call(bf16[4,272,1024]{2,1,0:T(8,128)(2,1)} %bitcast.74, ...), custom_call_target="tpu_custom_call" | custom-call | tf_op jit(solution)/shard_map/back/pallas_call | solution.py:1082
  433.8 2.9 copy.59
  436.8 2.1 copy.58
  (229 shorter events, 25.0 us)
Async XLA Ops:
  5.9 6.9 %copy-start.2 = (f32[4,272,128]{2,1,0:T(8,128)}, f32[4,272,128]{2,1,0:T(8,128)S(1)}, u32[]{:S(2)}) copy-start(f32[4,272,128]{2,1,0:T(8,128)S(1)} %pad.74) | copy-start | bytes 1671172
  5.9 6.8 %copy-start.3 = (f32[4,272,128]{2,1,0:T(8,128)}, f32[4,272,128]{2,1,0:T(8,128)S(1)}, u32[]{:S(2)}) copy-start(f32[4,272,128]{2,1,0:T(8,128)S(1)} %pad.73) | copy-start | bytes 1671172
  6.3 6.5 %copy-start.4 = (f32[4,272,128]{2,1,0:T(8,128)}, f32[4,272,128]{2,1,0:T(8,128)S(1)}, u32[]{:S(2)}) copy-start(f32[4,272,128]{2,1,0:T(8,128)S(1)} %pad.72) | copy-start | bytes 1671172
  160.7 105.2 %copy-start.5 = (bf16[1088,512]{1,0:T(8,128)(2,1)}, bf16[1088,512]{1,0:T(8,128)(2,1)S(1)}, u32[]{:S(2)}) copy-start(bf16[1088,512]{1,0:T(8,128)(2,1)S(1)} %get-tuple-element.44.mix_in) | copy-start | bytes 3342340
  160.8 9.2 %copy-start.22 = (bf16[4,272,1024]{2,1,0:T(8,128)(2,1)S(1)}, bf16[4,272,1024]{2,1,0:T(8,128)(2,1)}, u32[]{:S(2)}) copy-start(bf16[4,272,1024]{2,1,0:T(8,128)(2,1)} %get-tuple-element.50) | copy-start | bytes 6684676
  163.5 9.2 %collective-permute-start = (bf16[1088,1024]{1,0:T(8,128)(2,1)}, bf16[1088,1024]{1,0:T(8,128)(2,1)}, u32[]{:S(2)}, u32[]{:S(2)}) collective-permute-start(bf16[1088,1024]{1,0:T(8,128)(2,1)} %convolution_convert_fusion), channel_id=1, source_target_pairs={{0,4},{1,5},{2,6},{3,7},{4,0},{5,1},{6,2},{7,3},{8,12},{9,13},{10,... | collective-permute-start | bytes 6684680 | tf_op jit(solution)/shard_map/ppermute | solution.py:1144
  171.0 24.0 %copy-start.20 = (bf16[1088,1024]{1,0:T(8,128)(2,1)}, bf16[1088,1024]{1,0:T(8,128)(2,1)S(1)}, u32[]{:S(2)}) copy-start(bf16[1088,1024]{1,0:T(8,128)(2,1)S(1)} %bitcast_convert_fusion) | copy-start | bytes 6684676
  185.3 8.4 %copy-start.16 = (f32[1088,1376]{1,0:T(8,128)}, f32[1088,1376]{1,0:T(8,128)S(1)}, u32[]{:S(2)}) copy-start(f32[1088,1376]{1,0:T(8,128)S(1)} %convolution_add_fusion.1) | copy-start | bytes 17965060
  193.7 1.2 collective-permute-start.1
  195.0 10.6 %copy-start.15 = (f32[1088,1376]{1,0:T(8,128)S(1)}, f32[1088,1376]{1,0:T(8,128)}, u32[]{:S(2)}) copy-start(f32[1088,1376]{1,0:T(8,128)} %get-tuple-element.152) | copy-start | bytes 17965060
  195.0 10.6 %copy-start.51 = (bf16[1376,1024]{1,0:T(8,128)(2,1)S(1)}, bf16[1376,1024]{1,0:T(8,128)(2,1)}, u32[]{:S(2)}) copy-start(bf16[1376,1024]{1,0:T(8,128)(2,1)} %get-tuple-element.49) | copy-start | bytes 8454148
  205.4 5.9 %collective-permute-start.3 = (f32[2,1088]{1,0:T(2,128)S(1)}, f32[2,1088]{1,0:T(2,128)S(1)}, u32[]{:S(2)}, u32[]{:S(2)}) collective-permute-start(f32[2,1088]{1,0:T(2,128)S(1)} %pad_maximum_fusion.3), channel_id=1, source_target_pairs={{0,4},{1,5},{2,6},{3,7},{4,0},{5,1},{6,2},{7,3},{8,12},{9,13},{10,... | collective-permute-start | bytes 26120 | tf_op jit(solution)/shard_map/ppermute | solution.py:1144
  211.0 44.6 %collective-permute-start.2 = (bf16[1088,1024]{1,0:T(8,128)(2,1)}, bf16[1088,1024]{1,0:T(8,128)(2,1)}, u32[]{:S(2)}, u32[]{:S(2)}) collective-permute-start(bf16[1088,1024]{1,0:T(8,128)(2,1)} %convolution_convert_fusion.4), channel_id=1, source_target_pairs={{0,4},{1,5},{2,6},{3,7},{4,0},{5,1},{6,2},{7,3},{8,12},{9,13},{10,... | collective-permute-start | bytes 6684680 | tf_op jit(solution)/shard_map/ppermute | solution.py:1144
  211.4 11.0 %copy-start.50 = (bf16[1376,1024]{1,0:T(8,128)(2,1)S(1)}, bf16[1376,1024]{1,0:T(8,128)(2,1)}, u32[]{:S(2)}) copy-start(bf16[1376,1024]{1,0:T(8,128)(2,1)} %get-tuple-element.47) | copy-start | bytes 8454148
  222.4 7.9 %slice-start = ((s8[6127616]{0:T(1024)(128)(4,1)}), s8[4194304]{0:T(1024)(128)(4,1)S(1)}, s32[]{:S(2)}) async-start(s8[6127616]{0:T(1024)(128)(4,1)} %bitcast.76), calls=%async_computation | async-start | bytes 8388608
  230.0 6.4 %copy-start.19 = (bf16[1088,1024]{1,0:T(8,128)(2,1)S(1)}, bf16[1088,1024]{1,0:T(8,128)(2,1)}, u32[]{:S(2)}) copy-start(bf16[1088,1024]{1,0:T(8,128)(2,1)} %copy-done.18) | copy-start | bytes 6684676
  230.0 20.4 %collective-permute-start.4 = (bf16[1088,1024]{1,0:T(8,128)(2,1)S(1)}, bf16[1088,1024]{1,0:T(8,128)(2,1)}, u32[]{:S(2)}, u32[]{:S(2)}) collective-permute-start(bf16[1088,1024]{1,0:T(8,128)(2,1)S(1)} %fusion.3), channel_id=1, source_target_pairs={{0,4},{1,5},{2,6},{3,7},{4,0},{5,1},{6,2},{7,3},{8,12},{9,13},{10,... | collective-permute-start | bytes 6684680 | tf_op jit(solution)/shard_map/ppermute | solution.py:1144
  255.6 7.9 %copy-start.10 = (bf16[512,1024]{1,0:T(8,128)(2,1)S(1)}, bf16[512,1024]{1,0:T(8,128)(2,1)}, u32[]{:S(2)}) copy-start(bf16[512,1024]{1,0:T(8,128)(2,1)} %copy-done.9) | copy-start | bytes 3145732
  433.7 6.1 %copy-start.24 = (f32[128,768]{1,0:T(8,128)S(1)}, f32[128,768]{1,0:T(8,128)}, u32[]{:S(2)}) copy-start(f32[128,768]{1,0:T(8,128)} %get-tuple-element.60) | copy-start | bytes 1179652
  433.7 6.8 %copy-start.27 = (f32[688,128]{1,0:T(8,128)S(1)}, f32[688,128]{1,0:T(8,128)}, u32[]{:S(2)}) copy-start(f32[688,128]{1,0:T(8,128)} %get-tuple-element.63) | copy-start | bytes 1056772
  433.7 7.5 %copy-start.26 = (f32[688,128]{1,0:T(8,128)S(1)}, f32[688,128]{1,0:T(8,128)}, u32[]{:S(2)}) copy-start(f32[688,128]{1,0:T(8,128)} %get-tuple-element.62) | copy-start | bytes 1056772
  433.7 11.0 %copy-start.1 = (s32[2,1028]{1,0:T(2,128)S(1)}, s32[2,1028]{1,0:T(2,128)}, u32[]{:S(2)}) copy-start(s32[2,1028]{1,0:T(2,128)} %param.27) | copy-start | bytes 24676
  436.7 6.7 %copy-start.31 = (f32[256,128]{1,0:T(8,128)S(1)}, f32[256,128]{1,0:T(8,128)}, u32[]{:S(2)}) copy-start(f32[256,128]{1,0:T(8,128)} %get-tuple-element.220) | copy-start | bytes 393220
  436.7 7.3 %copy-start.25 = (f32[688,128]{1,0:T(8,128)S(1)}, f32[688,128]{1,0:T(8,128)}, u32[]{:S(2)}) copy-start(f32[688,128]{1,0:T(8,128)} %get-tuple-element.64) | copy-start | bytes 1056772
  (35 other events, 150.7 us)

commit v4 on v3

--- a/solution.py
+++ b/solution.py
@@ -3,6 +3,7 @@
 
 import jax
 import jax.numpy as jnp
+import numpy as np
 from jax import lax
 from jax.experimental import pallas as pl
 from jax.experimental.pallas import tpu as pltpu
@@ -29,31 +30,31 @@
 
 def rotary_tables(length, head):
     quarter = head // 4
-    place = jnp.arange(length, dtype=jnp.int32)
+    place = np.arange(length, dtype=np.int32)
     inside = (place >= 1) & (place <= GRID * GRID)
-    cell = jnp.maximum(place - 1, 0)
-    row_pos = jnp.where(inside, cell // GRID, 0).astype(F32)
-    col_pos = jnp.where(inside, cell % GRID, 0).astype(F32)
-    freq = ROPE_BASE ** (-jnp.arange(quarter, dtype=F32) / quarter)
-    angle = jnp.concatenate(
+    cell = np.maximum(place - 1, 0)
+    row_pos = np.where(inside, cell // GRID, 0).astype(np.float32)
+    col_pos = np.where(inside, cell % GRID, 0).astype(np.float32)
+    freq = ROPE_BASE ** (-np.arange(quarter, dtype=np.float32) / quarter)
+    angle = np.concatenate(
         [row_pos[:, None] * freq[None, :], col_pos[:, None] * freq[None, :]], axis=1
     )
-    return jnp.cos(angle), jnp.sin(angle)
+    return np.cos(angle), np.sin(angle)
 
 
 def lane_tables(length, quarter, block, rows_padded):
     cosv, sinv = rotary_tables(length, HEAD)
 
     def lay(first, second):
-        one = jnp.concatenate(
+        one = np.concatenate(
             [first[:, :quarter], second[:, :quarter], first[:, quarter:], second[:, quarter:]], axis=1
         )
-        two = jnp.concatenate([one, one], axis=1)
+        two = np.concatenate([one, one], axis=1)
         cut = two.reshape(length // block, block, 2 * HEAD)
-        return jnp.pad(cut, ((0, 0), (0, rows_padded - block), (0, 0))).reshape(-1, 2 * HEAD)
-
-    zero = jnp.zeros_like(sinv)
-    return lay(cosv, cosv), lay(-sinv, zero), lay(zero, sinv)
+        return np.pad(cut, ((0, 0), (0, rows_padded - block), (0, 0))).reshape(-1, 2 * HEAD)
+
+    zero = np.zeros_like(sinv)
+    return [jnp.asarray(t, F32) for t in (lay(cosv, cosv), lay(-sinv, zero), lay(zero, sinv))]
 
 
 def norm_pieces(values):
@@ -169,6 +170,12 @@
     def shifted(self, by):
         return (self.dp, lax.rem(self.z + by, self.nz))
 
+    def opposite(self):
+        return (self.dp, lax.rem(self.z + self.nz // 2, self.nz))
+
+    def neighbour(self):
+        return (self.dp, self.z + 1 - 2 * self.slot)
+
     def barrier(self):
         everyone = [self.across()]
         everyone += [self.shifted(s) for s in range(1, self.nz)]
@@ -202,7 +209,7 @@
         return [
             dma((n_w,)),
             dma((n_w,)),
-            dma((n_w, sizes[1])),
+            dma((n_w, 2)),
             dma((n_w, 2)),
             dma((n_w, bits, 2, most)),
             dma((n_w, bits, 2, most)),
@@ -222,26 +229,31 @@
         pl.when(self.me.home)(stay.start)
         pl.when(jnp.logical_not(self.me.home))(leave.start)
 
-    def _along(self, j, s):
-        me = self.me
-        src = self.kinds[j].piece(self.w_out[j], me.slot, me.chip)
-        return remote(src, src, self.z_send.at[j, s - 1], self.z_recv.at[j, me.slot], me.shifted(s))
+    def _along(self, j, slot, number, to):
+        src = self.kinds[j].piece(self.w_out[j], slot, self.me.chip)
+        return remote(src, src, self.z_send.at[j, number], self.z_recv.at[j, slot], to)
 
     def start_z(self, j):
-        @pl.when(self.me.home)
+        me = self.me
+
+        @pl.when(me.home)
         def _():
             stay, leave = self._hop(j)
             stay.wait()
             leave.wait_recv()
-            for s in range(1, self.me.nz):
-                self._along(j, s).start()
+            self._along(j, me.slot, 0, me.opposite()).start()
+            self._along(j, me.slot, 1, me.neighbour()).start()
+
+    def pass_z(self, j):
+        me = self.me
+
+        @pl.when(jnp.logical_not(me.home))
+        def _():
+            self._along(j, me.slot, 0, me.neighbour()).wait_recv()
+            self._along(j, me.slot, 0, me.neighbour()).start()
 
     def wait_z(self, j):
-        me = self.me
-        for slot in range(2):
-            src = self.kinds[j].piece(self.w_out[j], slot, me.chip)
-            copy = remote(src, src, self.z_send.at[j, 0], self.z_recv.at[j, slot], me.across())
-            pl.when(me.core * (me.nz // 2) + slot != me.z)(copy.wait_recv)
+        self._along(j, 1 - self.me.slot, 0, self.me.neighbour()).wait_recv()
 
     def _bits(self, j, step, slot):
         me = self.me
@@ -269,8 +281,10 @@
     def finish(self, j):
         me = self.me
         pl.when(jnp.logical_not(me.home))(self._hop(j)[1].wait_send)
-        for s in range(1, me.nz):
-            pl.when(me.home)(self._along(j, s).wait_send)
+        copy = self._along(j, me.slot, 0, me.neighbour())
+        copy.wait_send()
+        copy = self._along(j, me.slot, 1, me.neighbour())
+        pl.when(me.home)(copy.wait_send)
         for step in range(me.bits):
             for slot in range(2):
                 send = self._bits(j, step, slot)
@@ -401,8 +415,9 @@
 
 
 class Scatter:
-    def __init__(self, me, kinds, g_in, keep, got, gotz, stage, g_out, sems):
+    def __init__(self, me, kinds, g_in, keep, got, gotz, stage, g_out, before, sems):
         self.me, self.kinds, self.g_in, self.keep, self.got = me, kinds, g_in, keep, got
+        self.before = before
         self.gotz, self.stage, self.g_out = gotz, stage, g_out
         self.b_send, self.b_recv, self.z_send, self.z_recv, self.f_send, self.f_recv, self.loc = sems
 
@@ -415,7 +430,7 @@
             dma((n_w, bits, 2, chips // 2)),
             dma((n_w, bits, 2, chips // 2)),
             dma((n_w, 2)),
-            dma((n_w, sizes[1])),
+            dma((n_w, 2)),
             dma((n_w,)),
             dma((n_w,)),
             dma((n_w, 2, chips // 2)),
@@ -451,12 +466,20 @@
             me.beside(bit),
         )
 
+    def _came(self, j, slot, m):
+        return pltpu.make_async_copy(
+            self.before[j][slot].at[m], self.got[j].at[m, slot], self.b_recv.at[j, 0, slot, m]
+        )
+
     def _load(self, j, slot, m):
         return pltpu.make_async_copy(self._first(j, slot, m, 0), self.keep[j].at[slot, m], self.loc.at[j, slot, m])
 
     def start(self, j, step):
         for slot in range(2):
-            _each(self._count(step), lambda m: self._copy(j, step, slot, m).start())
+            if step == 0 and self.before[j] is not None:
+                _each(self._count(step), lambda m: self._came(j, slot, m).start())
+            else:
+                _each(self._count(step), lambda m: self._copy(j, step, slot, m).start())
         if step == 0 and self.keep[j] is not None:
             for slot in range(2):
                 _each(self._count(step), lambda m: self._load(j, slot, m).start())
@@ -465,7 +488,10 @@
         for slot in range(2):
 
             def one(m):
-                self._copy(j, step, slot, m).wait_recv()
+                if step == 0 and self.before[j] is not None:
+                    self._came(j, slot, m).wait()
+                else:
+                    self._copy(j, step, slot, m).wait_recv()
                 if step > 0:
                     mine = self._held(j, step, slot, m, 0)
                 elif self.keep[j] is not None:
@@ -481,18 +507,24 @@
     def _last(self, j, slot):
         return self.got[j].at[self._base(self.me.bits - 1), slot]
 
-    def _z(self, j, slot):
-        me = self.me
-        target = me.nz // 2 * me.core + slot
-        index = lax.rem(me.z - target + me.nz - 1, me.nz)
-        return target, remote(
-            self._last(j, slot), self.gotz[j].at[index], self.z_send.at[j, slot], self.z_recv.at[j, index], (me.dp, target)
+    def _z(self, j, slot, number, to):
+        return remote(
+            self._last(j, slot), self.gotz[j].at[number], self.z_send.at[j, number], self.z_recv.at[j, number], to
         )
 
     def start_z(self, j):
-        for slot in range(2):
-            target, copy = self._z(j, slot)
-            pl.when(target != self.me.z)(copy.start)
+        self._z(j, 1 - self.me.slot, 0, self.me.neighbour()).start()
+
+    def pass_z(self, j):
+        me = self.me
+        copy = self._z(j, me.slot, 0, me.neighbour())
+
+        @pl.when(jnp.logical_not(me.home))
+        def _():
+            copy.wait_recv()
+            here = self._last(j, me.slot)
+            here[...] = (here[...].astype(F32) + self.gotz[j][0].astype(F32)).astype(BF16)
+            self._z(j, me.slot, 1, me.opposite()).start()
 
     def _hand(self, j):
         return remote(self.stage[j], self.g_out[j], self.f_send.at[j], self.f_recv.at[j], self.me.across())
@@ -502,14 +534,13 @@
 
         @pl.when(me.home)
         def _():
-            for index in range(me.nz - 1):
-                slab = self.gotz[j].at[index]
-                remote(slab, slab, self.z_send.at[j, 0], self.z_recv.at[j, index], me.across()).wait_recv()
+            for number in range(2):
+                self._z(j, me.slot, number, me.neighbour()).wait_recv()
 
             def total(core):
                 value = self.kinds[j].half(self._last(j, me.slot), core)[...].astype(F32)
-                for index in range(me.nz - 1):
-                    value = value + self.kinds[j].half(self.gotz[j].at[index], core)[...].astype(F32)
+                for number in range(2):
+                    value = value + self.kinds[j].half(self.gotz[j].at[number], core)[...].astype(F32)
                 return value
 
             self.stage[j][...] = total(1 - me.core)
@@ -518,12 +549,12 @@
 
     def finish(self, j):
         me = self.me
-        for step in range(me.bits):
+        for step in range(0 if self.before[j] is None else 1, me.bits):
             for slot in range(2):
                 _each(self._count(step), lambda m: self._copy(j, step, slot, m).wait_send())
-        for slot in range(2):
-            target, copy = self._z(j, slot)
-            pl.when(target != me.z)(copy.wait_send)
+        self._z(j, 1 - me.slot, 0, me.neighbour()).wait_send()
+        far = self._z(j, me.slot, 1, me.opposite())
+        pl.when(jnp.logical_not(me.home))(far.wait_send)
         hand = self._hand(j)
         pl.when(me.home)(hand.wait_send)
         pl.when(jnp.logical_not(me.home))(hand.wait_recv)
@@ -633,6 +664,28 @@
             pl.when(me.core * (me.nz // 2) + slot != me.z)(copy.wait_recv)
 
 
+def send_first(kind, grad, sizes):
+    n_dp, nz = sizes
+    chips = n_dp // 2
+    bits = chips.bit_length() - 1
+    chip = lax.axis_index("dp") // 2
+    grad = kind.cut(grad)
+    a, b = kind.shard
+    came = []
+    for slot in range(2):
+        bit = bits - 1 if slot == 0 else 0
+        parts = []
+        for m in range(chips // 2):
+            there = lax.bitwise_xor(chip, m + (1 << bit) if slot == 0 else 2 * m + 1)
+            if kind.by_rows:
+                parts.append(lax.dynamic_slice(grad, (there * (2 * a), slot * b), kind.two))
+            else:
+                parts.append(lax.dynamic_slice(grad, (slot * a, there * (2 * b)), kind.two))
+        pairs = [(i, (i // nz ^ (2 << bit)) * nz + i % nz) for i in range(n_dp * nz)]
+        came.append(lax.ppermute(jnp.stack(parts), ("dp", "tensor"), pairs))
+    return came
+
+
 KEYS = 1152
 TILE = 272
 COLS = 384
@@ -649,49 +702,64 @@
 
 def front_kernel(
     kinds, sizes,
-    tok_in, cot_in, pack_in, base_in, qkv_in, o_in, g_in, u_in, d_in,
-    gain_ref, bias_ref, cos_ref, up_ref, down_ref,
-    tok, cot, pack, base, w_qkv, w_o, w_g, w_u, w_d, normed, qa_ref, ka_ref, va_ref, mix_ref,
+    tok_in, cot_in, pack_in, base_in, a_in, b_in, o_in, g_in, u_in, d_in,
+    gain_ref, bias_ref, cos_ref, up_ref, down_ref, out_bias, gain2_ref, bias2_ref,
+    tok_out, cot, pack, base, a_out, b_out, w_o, w_g, w_u, w_d, normed_out, qa_out, ka_out, va_out, mix_out,
+    mid_out, normed2_out, gate_out, up_out, hidden_out, totals,
+    tok, w_a, w_b, normed, qa_ref, ka_ref, va_ref, mix_ref, normed2, hidden, done_sem,
+    wo_v, wg_v, wu_v, part, theirs, mid_v, gate_v, up_v, act_v, own_sums, their_sums, p_send, p_recv, r_send, r_recv, out_sem, w_sem,
     *sems,
 ):
     me = Place(*sizes)
     nz = sizes[1]
-    gather = Gather(me, kinds, (qkv_in, o_in, g_in, u_in, d_in), (w_qkv, w_o, w_g, w_u, w_d), sems[:7])
+    gather = Gather(me, kinds, (a_in, b_in, o_in, g_in, u_in, d_in), (w_a, w_b, w_o, w_g, w_u, w_d), sems[:7])
     tokens = Inward(me, tok_in, tok, sems[7:12])
     cots = Inward(me, cot_in, cot, sems[12:17])
     packs = Packs(me, pack_in, pack, base_in, base, sems[17:20])
     n_w = len(kinds)
+    leaving = []
+
+    def leave(src, dst):
+        copy = pltpu.make_async_copy(src, dst, done_sem.at[len(leaving)])
+        copy.start()
+        leaving.append(copy)
+
     me.barrier()
     for j in range(n_w):
         gather.first_hop(j)
-    gather.start_z(0)
+    for j in (0, 1, 3, 2):
+        gather.start_z(j)
+    packs.start()
+
+    def flow(j):
+        gather.wait_z(j)
+        gather.start_bits(j, 0)
+        yield
+        for step in range(1, me.bits):
+            gather.wait_bits(j, step - 1)
+            gather.start_bits(j, step)
+        yield
+
+    flows = [flow(j) for j in range(n_w)]
+    gather.pass_z(0)
+    next(flows[0])
+    gather.pass_z(1)
+    next(flows[1])
+    next(flows[0])
+    gather.pass_z(3)
+    next(flows[1])
+    next(flows[3])
+    gather.pass_z(2)
     tokens.start()
-    packs.start()
-    gather.wait_z(0)
-    for step in range(me.bits):
-        if step > 0:
-            gather.wait_bits(0, step - 1)
-        gather.start_bits(0, step)
+    for j in (4, 5):
+        gather.start_z(j)
+    next(flows[2])
+    next(flows[3])
     tokens.pass_on()
-    gather.start_z(1)
-
-    def on_the_way():
-        for j in range(1, n_w):
-            gather.wait_z(j)
-            if j + 1 < n_w:
-                gather.start_z(j + 1)
-            else:
-                cots.start()
-            gather.start_bits(j, 0)
-            yield
-            for step in range(1, me.bits):
-                gather.wait_bits(j, step - 1)
-                gather.start_bits(j, step)
-                yield
-
-    events = on_the_way()
     tokens.ready()
     packs.ready()
+    gather.pass_z(4)
+    next(flows[2])
 
     block = tok.shape[1]
     rows = block * nz
@@ -712,17 +780,23 @@
         normed[pl.ds(pl.multiple_of(t * block, block), block), :] = (x * gain_ref[...] + bias_ref[...]).astype(BF16)
 
     gather.wait_bits(0, me.bits - 1)
+    gather.wait_bits(1, me.bits - 1)
+    leave(tok, tok_out)
+    leave(w_a, a_out)
+    leave(w_b, b_out)
+    leave(normed, normed_out)
     pairs = mix_ref.shape[1] // lanes
     sub = pairs // 2
 
     def project(g):
-        at = (g // sub) * (3 * sub) + g % sub
+        weight = (w_a, w_b)[g % sub]
 
         def column(part):
-            return w_qkv[:, (at + part * sub) * lanes : (at + part * sub + 1) * lanes]
-
-        q_bias = pack[g // sub, g % sub : g % sub + 1, :]
-        v_bias = pack[g // sub, sub + g % sub : sub + g % sub + 1, :]
+            at = ((g // sub) * 3 + part) * lanes
+            return weight[:, at : at + lanes]
+
+        q_bias = pack[g // sub, 0:1, (g % sub) * lanes : (g % sub + 1) * lanes]
+        v_bias = pack[g // sub, 1:2, (g % sub) * lanes : (g % sub + 1) * lanes]
 
         @pl.loop(0, nz)
         def _(t):
@@ -776,17 +850,123 @@
                 low, outs[0], pltpu.roll(outs[1], HEAD, 1)
             ).astype(BF16)
 
-    next(events, None)
-    for g in range(pairs):
-        project(g)
-        next(events, None)
-        attend(g)
-        next(events, None)
-    for _ in events:
-        pass
+        for src, dst in ((qa_ref, qa_out), (ka_ref, ka_out), (va_ref, va_out)):
+            leave(src.at[pl.ds(2 * g, 2)], dst.at[pl.ds(2 * g, 2)])
+
+    project(0)
+    next(flows[4])
+    gather.pass_z(5)
+    attend(0)
+    next(flows[5])
+    project(1)
+    attend(1)
+    next(flows[4])
+    project(2)
+    attend(2)
+    next(flows[5])
+    cots.start()
+    project(3)
+    attend(3)
+
+    def load(j, there):
+        gather.wait_bits(j, me.bits - 1)
+        copy = pltpu.make_async_copy(gather.w_out[j], there, w_sem.at[j])
+        copy.start()
+        return copy
+
+    def swap(t):
+        return remote(part.at[t], theirs.at[t], p_send.at[t], p_recv.at[t], me.across())
+
+    def swap_sums(t):
+        return remote(own_sums.at[t], their_sums.at[t], r_send.at[t], r_recv.at[t], me.across())
+
+    def save(t):
+        slot = t % 2
+        return [
+            pltpu.make_async_copy(mid_v.at[slot], mid_out.at[t], out_sem.at[0, slot]),
+            pltpu.make_async_copy(gate_v.at[slot], gate_out.at[t], out_sem.at[1, slot]),
+            pltpu.make_async_copy(up_v.at[slot], up_out.at[t], out_sem.at[2, slot]),
+        ]
+
+    leave(mix_ref, mix_out)
+    loads = [load(2, wo_v), load(3, wg_v)]
+    loads[0].wait()
+    for t in range(nz):
+        mixed = mix_ref[t * block : (t + 1) * block, :]
+        product = matmul_right_t(mixed, wo_v[...]) if kinds[2].turn else matmul(mixed, wo_v[...])
+        part[t] = product.astype(BF16)
+        swap(t).start()
+
+    ff = hidden.shape[1] // 2
+    wide = up_to(ff, LANES)
+    place = lax.broadcasted_iota(jnp.int32, (1, 2 * wide), 1)
+
+    def row(n):
+        blank = jnp.zeros((1, wide), F32)
+        first = jnp.concatenate([pack[0, n : n + 1, :wide], blank], axis=1)
+        second = jnp.concatenate([pack[1, n : n + 1, :wide], blank], axis=1)
+        return jnp.where(place < ff, first, pltpu.roll(second, ff, 1))[:, : 2 * ff]
+
+    g_bias, u_bias, inner_gain, inner_shift, columns = (row(n) for n in range(2, 7))
+    count = float(FF - PADCOLS)
+
+    def finish_tile(t):
+        slot = t % 2
+        swap_sums(t).wait_recv()
+        total = own_sums[t] + their_sums[t]
+        totals[t] = total
+        mean = total[:, 0:1] / count
+        var = total[:, 1:2] / count - mean * mean
+        nhat = (act_v[slot] - mean) * lax.rsqrt(var + EPS)
+        here = pl.ds(t * block, block)
+        hidden[here, :] = (columns * (nhat * inner_gain + inner_shift)).astype(BF16)
+        leave(hidden.at[here], hidden_out.at[here])
+        leave(normed2.at[here], normed2_out.at[here])
+
+    for t in range(nz):
+        slot = t % 2
+        if t >= 2:
+            for copy in save(t - 2):
+                copy.wait()
+        swap(t).wait_recv()
+        x = tok[t].astype(F32) + (part[t].astype(F32) + theirs[t].astype(F32)) + out_bias[...]
+        mid_v[slot] = x
+        x = x - jnp.sum(x, axis=1, keepdims=True) * (1.0 / width)
+        var = jnp.sum(x * x, axis=1, keepdims=True) * (1.0 / width)
+        x = (x * lax.rsqrt(var + EPS) * gain2_ref[...] + bias2_ref[...]).astype(BF16)
+        normed2[t * block : (t + 1) * block, :] = x
+        if t == 0:
+            loads.append(load(4, wu_v))
+            loads[1].wait()
+        gate = (matmul(x, wg_v[...]) if kinds[3].turn else matmul_right_t(x, wg_v[...])) + g_bias
+        gate_v[slot] = gate
+        if t == 0:
+            loads[2].wait()
+        up = (matmul(x, wu_v[...]) if kinds[4].turn else matmul_right_t(x, wu_v[...])) + u_bias
+        up_v[slot] = up
+        gate = gate_v[slot]
+        act = gate * (1.0 / (1.0 + jnp.exp(-gate))) * up
+        act_v[slot] = act
+        live = act * columns
+        first = jnp.sum(live, axis=1, keepdims=True)
+        second = jnp.sum(live * act, axis=1, keepdims=True)
+        own_sums[t] = jnp.where(lane == 0, first, jnp.where(lane == 1, second, 0.0))
+        swap_sums(t).start()
+        for copy in save(t):
+            copy.start()
+        if t >= 1:
+            finish_tile(t - 1)
+    finish_tile(nz - 1)
     cots.pass_on()
-    for j in range(1, n_w):
-        gather.wait_bits(j, me.bits - 1)
+    for t in range(nz - 2, nz):
+        for copy in save(t):
+            copy.wait()
+    gather.wait_bits(5, me.bits - 1)
+    for copy in leaving:
+        copy.wait()
+    for t in range(nz):
+        swap(t).wait_send()
+        swap_sums(t).wait_send()
     cots.ready()
     for j in range(n_w):
         gather.finish(j)
@@ -795,7 +975,7 @@
     packs.finish()
 
 
-def front(tokens, cotangent, pack, base, weights, kinds, gain, bias, tables, n_head, sizes, cid):
+def front(tokens, cotangent, pack, base, weights, kinds, gain, bias, tables, more, n_head, ff, sizes, cid):
     nz = sizes[1]
     block, width = tokens.shape[1:]
     rows = block * nz
@@ -814,43 +994,71 @@
         shape((rows, width), BF16),
         *[shape((heads, KEYS, lanes), BF16)] * 3,
         shape((rows, heads * HEAD), BF16),
+        shape((nz, block, width), F32),
+        shape((rows, width), BF16),
+        shape((nz, block, 2 * ff), F32),
+        shape((nz, block, 2 * ff), F32),
+        shape((rows, 2 * ff), BF16),
+        shape((nz, block, lanes), F32),
     ]
+    dma = pltpu.SemaphoreType.DMA
     out = pl.pallas_call(
         functools.partial(front_kernel, kinds, sizes),
         out_shape=shapes,
-        in_specs=[hbm] * 9 + [vmem] * 5,
-        out_specs=[vmem, hbm, vmem, vmem, vmem, hbm, hbm, hbm, hbm] + [vmem] * 5,
-        scratch_shapes=Gather.semaphores(len(kinds), sizes)
+        in_specs=[hbm] * 10 + [vmem] * 8,
+        out_specs=[hbm, hbm, vmem, vmem] + [hbm] * 16 + [vmem],
+        scratch_shapes=[
+            pltpu.VMEM((nz, block, width), BF16),
+            pltpu.VMEM(kinds[0].whole, BF16),
+            pltpu.VMEM(kinds[1].whole, BF16),
+            pltpu.VMEM((rows, width), BF16),
+            *[pltpu.VMEM((heads, KEYS, lanes), BF16)] * 3,
+            pltpu.VMEM((rows, heads * HEAD), BF16),
+            pltpu.VMEM((rows, width), BF16),
+            pltpu.VMEM((rows, 2 * ff), BF16),
+            dma((5 + 3 * heads // 2 + 2 * nz,)),
+        ]
+        + [pltpu.VMEM(k.whole, BF16) for k in kinds[2:5]]
+        + [pltpu.VMEM((nz, block, width), BF16)] * 2
+        + [pltpu.VMEM((2, block, width), F32)]
+        + [pltpu.VMEM((2, block, 2 * ff), F32)] * 3
+        + [pltpu.VMEM((nz, block, lanes), F32)] * 2
+        + [dma((nz,)), dma((nz,)), dma((nz,)), dma((nz,)), dma((3, 2)), dma((len(kinds),))]
+        + Gather.semaphores(len(kinds), sizes)
         + Inward.semaphores(sizes)
         + Inward.semaphores(sizes)
         + Packs.semaphores(sizes),
         compiler_params=pltpu.CompilerParams(
-            collective_id=cid, has_side_effects=True, vmem_limit_bytes=48 * 2**20
+            collective_id=cid, has_side_effects=True, vmem_limit_bytes=60 * 2**20
         ),
         name="front",
-    )(tokens, cotangent, pack, base, *weights, gain[None], bias[None], *tables)
-    return out[:4], [k.join(w) for k, w in zip(kinds, out[4:9])], out[9:]
+    )(tokens, cotangent, pack, base, *weights, gain[None], bias[None], *tables, *[v[None] for v in more])
+    return out[:4], [k.join(w) for k, w in zip(kinds, out[4:10])], out[10:]
 
 
 def back_kernel(
-    kinds, sizes, n_late,
-    out_in, g_d, g_g, g_u, g_o, qa_in, ka_in, va_in, do_in, mix_in, normed_in, w_in, x_in, dmid_in,
+    kinds, sizes, n_late, n_before,
+    out_in, g_d, g_g, g_u, g_o, qa_in, ka_in, va_in, do_in, mix_in, normed_in, wa_in, wb_in, x_in, dmid_in,
     cos_ref, up_ref, down_ref, gain_ref, vec_ref,
-    out_rows, in_rows, vec_out, s_d, s_g, s_u, s_o, s_qkv,
     *rest,
 ):
     me = Place(*sizes)
     nz, bits = me.nz, me.bits
+    before = [rest[2 * j : 2 * j + 2] if j < n_before else None for j in range(len(kinds))]
+    rest = rest[2 * n_before :]
+    out_rows, in_rows, vec_out = rest[:3]
+    g_out = rest[3 : 3 + len(kinds)]
+    rest = rest[3 + len(kinds) :]
     n_w = len(kinds)
-    keep = rest[: n_w - 1] + (None,)
-    rest = rest[n_w - 1 :]
+    keep = rest[: n_w - 2] + (None, None)
+    rest = rest[n_w - 2 :]
     got, gotz, stage = (rest[i * n_w : (i + 1) * n_w] for i in range(3))
     rest = rest[3 * n_w :]
     v_sum, v_got, v_all = rest[:3]
-    (qa, ka, va, do, mix, normed, w, x_ref, dmid, d_qkv, g_qkv, part, theirs, da, dq, dk, dv, dgain, dshift) = rest[3:22]
-    sems = rest[22:]
+    (qa, ka, va, do, mix, normed, w, x_ref, dmid, d_qkv, g_a, g_b, part, theirs, da, dq, dk, dv, dgain, dshift) = rest[3:23]
+    sems = rest[23:]
     scatter = Scatter(
-        me, kinds, (g_d, g_g, g_u, g_o, g_qkv), keep, got, gotz, stage, (s_d, s_g, s_u, s_o, s_qkv), sems[:7]
+        me, kinds, (g_d, g_g, g_u, g_o, g_a, g_b), keep, got, gotz, stage, g_out, before, sems[:7]
     )
     sums = Sums(me, v_sum, v_got, v_all, vec_out, sems[7:13])
     outs = Outward(me, out_in, out_rows, sems[13:16])
@@ -865,8 +1073,11 @@
     lane = lax.broadcasted_iota(jnp.int32, (block, lanes), 1)
     low = lane < HEAD
 
-    def loads(g):
-        slot = g % 2
+    turns = [slot * sub + s for s in range(sub) for slot in range(pairs // sub)]
+
+    def loads(n):
+        slot = n % 2
+        g = turns[n]
         heads = pl.ds(2 * g, 2)
         cols = pl.ds(g * lanes, lanes)
         return [
@@ -879,7 +1090,8 @@
 
     late = [
         pltpu.make_async_copy(normed_in, normed, late_sem.at[0]),
-        pltpu.make_async_copy(w_in, w, late_sem.at[1]),
+        pltpu.make_async_copy(wa_in, w.at[:, pl.ds(0, wa_in.shape[1])], late_sem.at[1]),
+        pltpu.make_async_copy(wb_in, w.at[:, pl.ds(wa_in.shape[1], wa_in.shape[1])], late_sem.at[2]),
     ]
 
     def tile_loads(t):
@@ -890,7 +1102,8 @@
         ]
 
     me.barrier()
-    scatter.start(0, 0)
+    for j in range(n_w - 2):
+        scatter.start(j, 0)
     for copy in loads(0):
         copy.start()
     for place in range(nz):
@@ -902,27 +1115,23 @@
             copy.start()
     v_sum[0] = vec_ref[...]
 
-    def on_the_way():
-        for j in range(n_w - 1):
-            for step in range(bits):
-                scatter.add(j, step)
-                if step + 1 < bits:
-                    scatter.start(j, step + 1)
-                else:
-                    scatter.start_z(j)
-                if step == 0 and j + 1 < n_w - 1:
-                    scatter.start(j + 1, 0)
-                yield
-            if j > 0:
-                scatter.end_z(j - 1)
-                yield
-        scatter.end_z(n_w - 2)
-        yield
-
-    events = on_the_way()
-
-    def head(g, h):
-        slot = g % 2
+    def flow(j):
+        for step in range(bits):
+            scatter.add(j, step)
+            if step + 1 < bits:
+                scatter.start(j, step + 1)
+            else:
+                scatter.start_z(j)
+            yield
+
+    flows = [flow(j) for j in range(n_w)]
+
+    def rest_of(j):
+        for _ in flows[j]:
+            pass
+
+    def head(n, h):
+        slot = n % 2
 
         @pl.loop(0, nz)
         def _(t):
@@ -960,7 +1169,7 @@
             dq[h, here, :] = matmul_left_t(ds, ka[slot, h])
 
     def put(g, part_of, row, ref, factor, turn):
-        at = ((g // sub) * (3 * sub) + part_of * sub + g % sub) * lanes
+        at = ((g % sub) * (pairs // sub) * 3 + (g // sub) * 3 + part_of) * lanes
 
         def one(t, total):
             here = pl.ds(pl.multiple_of(t * block, block), block)
@@ -978,87 +1187,119 @@
 
     da[pl.ds(rows, KEYS - rows), :] = jnp.zeros((KEYS - rows, lanes), BF16)
 
-    def weight_gradient(slot):
-        chunk = kinds[-1].two[0]
-        columns = pl.ds(slot * 3 * sub * lanes, 3 * sub * lanes)
-        grad = d_qkv[:, slot * 3 * sub * lanes : (slot + 1) * 3 * sub * lanes]
-        step = max(chunk, lanes)
+    def weight_gradient(s):
+        into = (g_a, g_b)[s]
+        columns = into.shape[1]
+        grad = d_qkv[:, s * columns : (s + 1) * columns]
+        step = max(kinds[-1].two[0], lanes)
         for c in range(width // step):
             left = normed[:, c * step : (c + 1) * step]
-            g_qkv[c * step : (c + 1) * step, columns] = matmul_left_t(left, grad).astype(BF16)
-
-    for g in range(pairs):
+            into[c * step : (c + 1) * step, :] = matmul_left_t(left, grad).astype(BF16)
+
+    def fetch(g):
         for copy in loads(g):
             copy.wait()
         if g + 1 < pairs:
             for copy in loads(g + 1):
                 copy.start()
-        for h in range(2):
-            head(g, h)
-            next(events, None)
+
+    def write(n):
+        g = turns[n]
         base_row = n_late + (g // sub) * (2 * sub) + g % sub
         put(g, 0, base_row, dq, SCALE, True)
         put(g, 1, None, dk, LN2, True)
         put(g, 2, base_row + sub, dv, None, False)
-        if g == 0:
-            for copy in late:
-                copy.wait()
-        if g % sub == sub - 1:
-            weight_gradient(g // sub)
-        next(events, None)
 
     def swap(t):
         return remote(part.at[t], theirs.at[t], p_send.at[t], p_recv.at[t], me.across())
 
-    for t in range(nz):
-        here = slice(t * block, (t + 1) * block)
-        part[t] = matmul_right_t(d_qkv[here, :], w[...]).astype(BF16)
-        swap(t).start()
-    for _ in range(2):
-        next(events, None)
-    dgain[...] = jnp.zeros_like(dgain)
-    dshift[...] = jnp.zeros_like(dshift)
-    for t in range(nz):
-        for copy in tile_loads(t):
-            copy.wait()
-        x = x_ref[t % 2].astype(F32)
-        x = x - jnp.sum(x, axis=1, keepdims=True) * (1.0 / width)
-        var = jnp.sum(x * x, axis=1, keepdims=True) * (1.0 / width)
-        scale = lax.rsqrt(var + EPS)
-        x = x * scale
-        swap(t).wait_recv()
-        dn = part[t].astype(F32) + theirs[t].astype(F32)
-        dgain[...] += jnp.sum(dn * x, axis=0, keepdims=True)
-        dshift[...] += jnp.sum(dn, axis=0, keepdims=True)
-        v = dn * gain_ref[...]
-        mean = jnp.sum(v, axis=1, keepdims=True) * (1.0 / width)
-        along = jnp.sum(v * x, axis=1, keepdims=True) * (1.0 / width)
-        theirs[t] = (dmid[t % 2] + scale * (v - mean - x * along)).astype(BF16)
-        ins.start(t)
-        if t + 2 < nz:
-            for copy in tile_loads(t + 2):
-                copy.start()
-    per = width // lanes
-    for i in range(per):
-        v_sum[0, i : i + 1, :] = dgain[:, i * lanes : (i + 1) * lanes]
-        v_sum[0, per + i : per + i + 1, :] = dshift[:, i * lanes : (i + 1) * lanes]
+    def partial():
+        for t in range(nz):
+            here = slice(t * block, (t + 1) * block)
+            part[t] = matmul_right_t(d_qkv[here, :], w[...]).astype(BF16)
+            swap(t).start()
+
+    def input_gradient():
+        dgain[...] = jnp.zeros_like(dgain)
+        dshift[...] = jnp.zeros_like(dshift)
+        for t in range(nz):
+            for copy in tile_loads(t):
+                copy.wait()
+            x = x_ref[t % 2].astype(F32)
+            x = x - jnp.sum(x, axis=1, keepdims=True) * (1.0 / width)
+            var = jnp.sum(x * x, axis=1, keepdims=True) * (1.0 / width)
+            scale = lax.rsqrt(var + EPS)
+            x = x * scale
+            swap(t).wait_recv()
+            dn = part[t].astype(F32) + theirs[t].astype(F32)
+            dgain[...] += jnp.sum(dn * x, axis=0, keepdims=True)
+            dshift[...] += jnp.sum(dn, axis=0, keepdims=True)
+            v = dn * gain_ref[...]
+            mean = jnp.sum(v, axis=1, keepdims=True) * (1.0 / width)
+            along = jnp.sum(v * x, axis=1, keepdims=True) * (1.0 / width)
+            theirs[t] = (dmid[t % 2] + scale * (v - mean - x * along)).astype(BF16)
+            ins.start(t)
+            if t + 2 < nz:
+                for copy in tile_loads(t + 2):
+                    copy.start()
+        per = width // lanes
+        for i in range(per):
+            v_sum[0, i : i + 1, :] = dgain[:, i * lanes : (i + 1) * lanes]
+            v_sum[0, per + i : per + i + 1, :] = dshift[:, i * lanes : (i + 1) * lanes]
+
+    fetch(0)
+    head(0, 0)
+    head(0, 1)
+    write(0)
+    next(flows[0], None)
+    next(flows[1], None)
+    fetch(1)
+    head(1, 0)
+    head(1, 1)
+    write(1)
+    rest_of(0)
+    rest_of(1)
+    for copy in late:
+        copy.wait()
+    weight_gradient(0)
+    next(flows[2], None)
+    scatter.start(4, 0)
+    scatter.pass_z(0)
+    scatter.pass_z(1)
+    fetch(2)
+    head(2, 0)
+    next(flows[3], None)
+    rest_of(2)
+    scatter.end_z(0)
+    head(2, 1)
+    write(2)
+    next(flows[4], None)
+    scatter.end_z(1)
+    fetch(3)
+    head(3, 0)
+    rest_of(3)
+    scatter.pass_z(2)
+    head(3, 1)
+    write(3)
+    rest_of(4)
+    weight_gradient(1)
+    scatter.start(5, 0)
+    scatter.pass_z(3)
+    partial()
+    next(flows[5], None)
+    scatter.pass_z(4)
+    scatter.end_z(2)
+    input_gradient()
+    rest_of(5)
     small = sums.phases()
     next(small, None)
-    started = False
-    for _ in events:
-        next(small, None)
-    last = n_w - 1
-    scatter.start(last, 0)
-    for step in range(bits):
-        next(small, None)
-        scatter.add(last, step)
-        if step + 1 < bits:
-            scatter.start(last, step + 1)
-        else:
-            scatter.start_z(last)
+    scatter.end_z(3)
+    next(small, None)
+    scatter.pass_z(5)
+    scatter.end_z(4)
     for _ in small:
         pass
-    scatter.end_z(last)
+    scatter.end_z(5)
     for t in range(nz):
         swap(t).wait_send()
     outs.finish()
@@ -1067,7 +1308,7 @@
         scatter.finish(j)
 
 
-def back(out_act, grads, heads, d_mixed, mixed, normed, w, x, dmid, tables, gain, vec, kinds, n_late, sizes, cid):
+def back(out_act, grads, before, heads, d_mixed, mixed, normed, weights, x, dmid, tables, gain, vec, kinds, n_late, sizes, cid):
     n_dp, nz = sizes
     chips = n_dp // 2
     n_w = len(kinds)
@@ -1080,26 +1321,27 @@
     dma = pltpu.SemaphoreType.DMA
     grads = [k.cut(g) for k, g in zip(kinds, grads)]
     out = pl.pallas_call(
-        functools.partial(back_kernel, kinds, sizes, n_late),
+        functools.partial(back_kernel, kinds, sizes, n_late, len(before)),
         out_shape=[shape((nz // 2, block, width), BF16)] * 2
         + [shape((2,) + vec.shape, F32)]
         + [shape(k.shard, F32) for k in kinds],
-        in_specs=[hbm] * 14 + [vmem] * 5,
+        in_specs=[hbm] * 15 + [vmem] * 5 + [hbm] * (2 * len(before)),
         out_specs=[hbm, hbm] + [vmem] * (1 + n_w),
-        scratch_shapes=[pltpu.VMEM((2, chips // 2) + k.two, BF16) for k in kinds[:-1]]
+        scratch_shapes=[pltpu.VMEM((2, chips // 2) + k.two, BF16) for k in kinds[:-2]]
         + [pltpu.VMEM((chips - 1, 2) + k.two, BF16) for k in kinds]
-        + [pltpu.VMEM((nz - 1,) + k.two, BF16) for k in kinds]
+        + [pltpu.VMEM((2,) + k.two, BF16) for k in kinds]
         + [pltpu.VMEM(k.shard, F32) for k in kinds]
         + Sums.scratch(vec.shape, sizes)
         + [pltpu.VMEM((2, 2, KEYS, lanes), BF16)] * 3
         + [pltpu.VMEM((2, rows, lanes), BF16)] * 2
         + [
             pltpu.VMEM((rows, width), BF16),
-            pltpu.VMEM(w.shape, BF16),
+            pltpu.VMEM((width, 2 * weights[0].shape[1]), BF16),
             pltpu.VMEM((2, block, width), BF16),
             pltpu.VMEM((2, block, width), F32),
-            pltpu.VMEM((rows, w.shape[1]), BF16),
-            pltpu.VMEM((width, w.shape[1]), BF16),
+            pltpu.VMEM((rows, 2 * weights[0].shape[1]), BF16),
+            pltpu.VMEM((width, weights[0].shape[1]), BF16),
+            pltpu.VMEM((width, weights[0].shape[1]), BF16),
             pltpu.VMEM((nz, block, width), BF16),
             pltpu.VMEM((nz, block, width), BF16),
             pltpu.VMEM((KEYS, lanes), BF16),
@@ -1110,12 +1352,12 @@
         + Sums.semaphores(sizes)
         + Outward.semaphores(sizes)
         + Outward.semaphores(sizes)
-        + [dma((2, 5)), dma((2,)), dma((2, 2)), dma((nz,)), dma((nz,))],
+        + [dma((2, 5)), dma((3,)), dma((2, 2)), dma((nz,)), dma((nz,))],
         compiler_params=pltpu.CompilerParams(
             collective_id=cid, has_side_effects=True, vmem_limit_bytes=62 * 2**20
         ),
         name="back",
-    )(out_act, *grads, *heads, d_mixed, mixed, normed, w, x, dmid, *tables, gain[None], vec)
+    )(out_act, *grads, *heads, d_mixed, mixed, normed, *weights, x, dmid, *tables, gain[None], vec, *[r for pair in before for r in pair])
     return out[:2], out[2], [k.leave(g) for k, g in zip(kinds, out[3:])]
 
 
@@ -1136,33 +1378,35 @@
     rows = block_pad * n_tensor
     n_head = w_query.shape[1]
     n_ff = w_gate.shape[1]
-    ff = up_to(n_ff, 16)
+    ff = up_to(n_ff, 16 if w_down.shape[1] % LANES == 0 else LANES)
     count_live = float(FF - PADCOLS)
     swap = [(i, (i // n_tensor ^ 1) * n_tensor + i % n_tensor) for i in range(n_dp * n_tensor)]
 
     def other(value):
         return lax.ppermute(value, ("dp", "tensor"), swap)
 
-    shard_qkv = jnp.concatenate([w_query, w_key, w_value], axis=1)
-    kind_qkv = Kind(True, shard_qkv.shape, n_dp)
+    pair = 2 * HEAD
+    shard_a, shard_b = (
+        jnp.concatenate([v[:, s * pair : (s + 1) * pair] for v in (w_query, w_key, w_value)], axis=1) for s in range(2)
+    )
+    kind_p = Kind(True, shard_a.shape, n_dp)
     kind_o = Kind(False, w_out.shape, n_dp)
     kind_f = Kind(False, (ff, w_down.shape[1]), n_dp)
 
-    def pad_ff(vec):
-        return jnp.pad(vec, (0, ff - n_ff))
-
     def turned(weight):
         return jnp.pad(weight.T, ((0, ff - n_ff), (0, 0)))
 
     def pad_rows(value):
         return jnp.pad(value, ((0, 0), (0, block_pad - block), (0, 0)))
 
-    small = jnp.concatenate(
-        [query_bias, value_bias]
-        + [pad_ff(v) for v in (gate_bias, up_bias, inner_gain, inner_shift, column_mask.astype(F32))]
+    wide = up_to(ff, LANES)
+    small = jnp.stack(
+        [
+            jnp.pad(v, (0, wide - v.shape[0]))
+            for v in (query_bias, value_bias, gate_bias, up_bias, inner_gain, inner_shift, column_mask.astype(F32))
+        ]
+        + [jnp.zeros((wide,), F32)]
     )
-    small_rows = up_to(up_to(small.shape[0], LANES) // LANES, 8)
-    small = jnp.pad(small, (0, small_rows * LANES - small.shape[0])).reshape(small_rows, LANES)
     own_image = z % (n_tensor // 2)
     live = lax.dynamic_index_in_dim(key_mask, own_image, 0, False)
     live = jnp.pad(live.reshape(n_tensor, block), ((0, 0), (0, block_pad - block))).reshape(rows)
@@ -1179,46 +1423,36 @@
     ).astype(BF16)
     tables = lane_tables(length, HEAD // 4, block, block_pad)
 
-    (image, cot, packs, base), full, (normed, qa, ka, va, mixed) = front(
+    (image, cot, packs, base), full, kept = front(
         pad_rows(tokens_in),
         pad_rows(cotangent),
         small,
         base,
-        [shard_qkv, w_out, turned(w_gate), turned(w_up), jnp.pad(w_down, ((0, ff - n_ff), (0, 0)))],
-        [kind_qkv, kind_o, kind_f, kind_f, kind_f],
+        [shard_a, shard_b, w_out, turned(w_gate), turned(w_up), jnp.pad(w_down, ((0, ff - n_ff), (0, 0)))],
+        [kind_p, kind_p, kind_o, kind_f, kind_f, kind_f],
         attention_norm_gain,
         attention_norm_bias,
         tables,
+        (out_bias, feedforward_norm_gain, feedforward_norm_bias),
         n_head,
+        ff,
         sizes,
         0,
     )
-    full_qkv, full_o, full_g, full_u, full_d = full
-    packs = packs.reshape(2, -1)
-    cuts = [n_head] * 2 + [ff] * 5
-    parts, at = [], 0
-    for size in cuts:
-        parts.append(packs[:, at : at + size].reshape(-1))
-        at += size
-    _, _, g_bias, u_bias, gain, shift, columns = parts
+    normed, qa, ka, va, mixed, middle, normed2, gate, up, hidden, sums = kept
+    full_a, full_b, full_o, full_g, full_u, full_d = full
+    gain, shift, columns = (packs[:, n, :ff].reshape(-1) for n in range(4, 7))
     flag = base[0, LANES - 1].astype(F32)
-    token_rows = image.reshape(rows, width).astype(F32)
-    xhat1, s1 = norm_pieces(token_rows)
-    part = matmul(mixed, full_o).astype(BF16)
-    middle = token_rows + (part.astype(F32) + other(part).astype(F32)) + out_bias
+    middle = middle.reshape(rows, width)
     xhat2, s2 = norm_pieces(middle)
-    normed2 = (xhat2 * feedforward_norm_gain + feedforward_norm_bias).astype(BF16)
-    gate = matmul_right_t(normed2, full_g) + g_bias
-    up = matmul_right_t(normed2, full_u) + u_bias
+    gate, up = gate.reshape(rows, -1), up.reshape(rows, -1)
     sig = jax.nn.sigmoid(gate)
     act = gate * sig * up
-    sums = jnp.stack([jnp.sum(act * columns, axis=-1), jnp.sum(act * act * columns, axis=-1)])
-    sums = sums + other(sums)
-    mean = sums[0][:, None] / count_live
-    var = sums[1][:, None] / count_live - mean * mean
+    sums = sums.reshape(rows, -1)
+    mean = sums[:, 0:1] / count_live
+    var = sums[:, 1:2] / count_live - mean * mean
     r = lax.rsqrt(var + EPS)
     nhat = (act - mean) * r
-    hidden = (columns * (nhat * gain + shift)).astype(BF16)
     part = matmul(hidden, full_d).astype(BF16)
     output = (middle + (part.astype(F32) + other(part).astype(F32)) + down_bias).astype(BF16)
 
@@ -1261,20 +1495,21 @@
     vec = jnp.concatenate([jnp.zeros(((late_rows + qv_rows) * LANES,), F32), early, tall])
     vec_rows = up_to(up_to(vec.shape[0], LANES) // LANES, 8)
     vec = jnp.pad(vec, (0, vec_rows * LANES - vec.shape[0])).reshape(vec_rows, LANES)
-    (out_rows, in_rows), vec, (s_down, s_gate, s_up, s_out, s_qkv) = back(
+    (out_rows, in_rows), vec, (s_down, s_gate, s_up, s_out, s_a, s_b) = back(
         output.reshape(n_tensor, block_pad, width),
         [g_down, g_gate, g_up, g_out],
+        [send_first(kind_f, g, sizes) for g in (g_down, g_gate)],
         [qa, ka, va],
         d_mixed,
         mixed,
         normed,
-        full_qkv,
+        [full_a, full_b],
         image,
         dmiddle.reshape(n_tensor, block_pad, width),
         tables,
         attention_norm_gain,
         vec,
-        [kind_f, kind_f, kind_f, kind_o, kind_qkv],
+        [kind_f, kind_f, kind_f, kind_o, kind_p, kind_p],
         late_rows,
         sizes,
         1,
@@ -1297,9 +1532,7 @@
         in_rows.astype(F32),
         wide[0],
         wide[1],
-        s_qkv[:, :n_head],
-        s_qkv[:, n_head : 2 * n_head],
-        s_qkv[:, 2 * n_head :],
+        *[jnp.concatenate([v[:, n * pair : (n + 1) * pair] for v in (s_a, s_b)], axis=1) for n in range(3)],
         pieces[0],
         pieces[1],
         s_out,

time: 449 us -> 411 us (0.915)
  the two profiles are of different devices: /device:TPU:27 before, /device:TPU:0 now
where the time goes in v4:
time: 411 us; the launch traced here: 403 us
  Pallas kernels  274 us (67%)
  matrix products  45.9 us (11%)
  other arithmetic  42.7 us (10%)
  local copies, waits for them, and re-layouts  30.8 us (7%)
  starting transfers between devices  5.33 us (1%)
    pallas_call x1, Pallas kernels, front(): pl.pallas_call(functools.partial(front_kernel, kinds, sizes), out_shape=s...  144 us
    pallas_call x1, Pallas kernels, back(): pl.pallas_call(functools.partial(back_kernel, kinds, sizes, n_late, len(b...  130 us
    dot_general x4, matrix products, matmul_left_t(): lax.dot_general(left, right, (((0,), (0,)), ((), ())), preferred_element_...  19.7 us
    dot_general x3, matrix products, matmul(): return jnp.dot(left, right, preferred_element_type=F32)  15.8 us
    unnamed x118, local copies, waits for them, and re-layouts  14.2 us
    reduce_sum x1, other arithmetic, shards(): g_up_bias = jnp.sum(dup, axis=0)  10.9 us
  transfers between devices with their start and end apart: 7, of which 1 were waited for; matrix products, arithmetic and copies ran while one was open for 21% of the time, Pallas kernels for 0%

profile of v4, /device:TPU:0, one launch (start us, length us, event | category | flops | bytes accessed | tf_op | source)
XLA Modules:
  0.0 402.5 jit_solution(10849927621633547682)
XLA Ops:
  0.9 1.6 copy.52
  2.5 1.5 copy.53
  12.3 143.8 %front.1 = (bf16[4,272,1024]{2,1,0:T(8,128)(2,1)}, bf16[4,272,1024]{2,1,0:T(8,128)(2,1)}, f32[2,8,768]{2,1,0:T(8,128)}, bf16[1152,128]{1,0:T(8,128)(2,1)}, bf16[...) custom-call(bf16[2,272,1024]{2,1,0:T(8,128)(2,1)} %pad.52.tok_in, ...), custom_call_target="tpu_custom_call" | custom-call | tf_op jit(solution)/shard_map/front/pallas_call | solution.py:1005
  156.1 7.9 %convolution_convert_fusion.3 = bf16[1088,1024]{1,0:T(8,128)(2,1)} fusion(bf16[1088,1376]{1,0:T(8,128)(2,1)} %get-tuple-element.52, bf16[1376,1024]{1,0:T(8,128)(2,1)} %get-tuple-element.53), kind=kOutput, calls=%fused_computation.39 | convolution fusion | flops 3067150336 | bytes 8040448 | tf_op jit(solution)/shard_map/dot_general | solution.py:77
  170.6 5.7 %fusion.1 = f32[1088,1376]{1,0:T(8,128)S(1)} fusion(f32[4,272,1376]{2,1,0:T(8,128)} %get-tuple-element.59, f32[4,272,1376]{2,1,0:T(8,128)} %get-tuple-element.58, f32[1088]{0:T(1024)S(1)} %get-tuple-element.140, f32[1088]{0:T(1024)S(1)} %get-tuple-element.139), kind=kLoop, calls=%fused_computation.4 | loop fusion | flops 10479616 | bytes 17973760 | tf_op jit(solution)/shard_map/mul | solution.py:1455
  176.4 7.9 %multiply_reduce_fusion = (f32[1376]{0:T(1024)}, f32[1088]{0:T(1024)S(1)}, f32[1088]{0:T(1024)S(1)}, f32[1376]{0:T(1024)}, f32[1088,1376]{1,0:T(8,128)}) fusion(f32[1088,1376]{1,0:T(8,128)S(1)} %fusion.1, f32[1376]{0:T(1024)S(1)} %mul.154, bf16[1088,1024]{1,0:T(8,128)(2,1)S(1)} %bitcast_convert_fusion, bf16[1376,1024]{1,0:T(8,128)(2,1)S(1)} %copy-done.44, ...), kind=kOutput, calls=%fused_computation.16 | convolution fusion | flops 3078008320 | bytes 17053696 | tf_op jit(solution)/shard_map/dot_general | solution.py:1462
  185.1 5.6 %convolution_convert_fusion.2.g_d = bf16[1376,1024]{1,0:T(8,128)(2,1)S(1)} fusion(bf16[1088,1376]{1,0:T(8,128)(2,1)S(1)} %copy-done.41, bf16[1088,1024]{1,0:T(8,128)(2,1)} %copy-done.10), kind=kOutput, calls=%fused_computation.38 | convolution fusion | flops 3067445248 | bytes 8040448 | tf_op jit(solution)/shard_map/dot_general | solution.py:85
  192.1 1.5 collective-permute-start.3
  195.5 3.2 reduce_sum.128
  199.3 2.9 multiply_reduce_fusion.5
  204.7 10.9 %fusion.26 = (f32[1376]{0:T(1024)S(1)}, bf16[1088,1376]{1,0:T(8,128)(2,1)S(1)}, f32[1376]{0:T(1024)S(1)}, bf16[1088,1376]{1,0:T(8,128)(2,1)S(1)}) fusion(f32[4,272,1376]{2,1,0:T(8,128)} %get-tuple-element.58, f32[1088,1376]{1,0:T(8,128)} %copy-done.3, f32[1088]{0:T(1024)S(1)} %get-tuple-element.138, f32[1088]{0:T(1024)S(1)} %get-tuple-element.137, ...), kind=kLoop, calls=%fused_computation.105 | loop fusion | flops 32933184 | bytes 29976832 | tf_op jit(solution)/shard_map/reduce_sum | solution.py:1474
  215.7 3.6 fusion.18
  219.6 4.3 %fusion.14 = bf16[1088,1024]{1,0:T(8,128)(2,1)S(1)} fusion(f32[1088,1024]{1,0:T(8,128)S(1)} %fusion.18, bf16[1376,1024]{1,0:T(8,128)(2,1)S(1)} %copy-done.42, bf16[1088,1376]{1,0:T(8,128)(2,1)S(1)} %get-tuple-element.142), kind=kOutput, calls=%fused_computation.35 | convolution fusion | flops 3068264448 | bytes 12496896 | tf_op jit(solution)/shard_map/dot_general | solution.py:77
  224.3 6.4 %convolution_convert_fusion.1.g_g = bf16[1376,1024]{1,0:T(8,128)(2,1)S(1)} fusion(bf16[1088,1024]{1,0:T(8,128)(2,1)} %get-tuple-element.60, bf16[1088,1376]{1,0:T(8,128)(2,1)} %copy-done.9), kind=kOutput, calls=%fused_computation.37 | convolution fusion | flops 3067445248 | bytes 8040448 | tf_op jit(solution)/shard_map/dot_general | solution.py:85
  234.3 5.3 %convolution_convert_fusion.g_u = bf16[1376,1024]{1,0:T(8,128)(2,1)} fusion(bf16[1088,1024]{1,0:T(8,128)(2,1)S(1)} %copy-done.45, bf16[1088,1376]{1,0:T(8,128)(2,1)S(1)} %copy-done.8), kind=kOutput, calls=%fused_computation.36 | convolution fusion | flops 3067445248 | bytes 8040448 | tf_op jit(solution)/shard_map/dot_general | solution.py:85
  240.7 4.0 fusion.11
  244.7 3.6 multiply_reduce_fusion.3
  248.3 3.3 fusion.30
  251.7 2.4 convolution_convert_fusion.4.do_in
  254.8 2.5 convolution_convert_fusion.5.g_o
  258.1 130.0 %back.1 = (bf16[2,272,1024]{2,1,0:T(8,128)(2,1)}, bf16[2,272,1024]{2,1,0:T(8,128)(2,1)}, f32[2,104,128]{2,1,0:T(8,128)}, f32[688,128]{1,0:T(8,128)}, f32[688,128...) custom-call(bf16[4,272,1024]{2,1,0:T(8,128)(2,1)} %bitcast.121, ...), custom_call_target="tpu_custom_call" | custom-call | tf_op jit(solution)/shard_map/back/pallas_call | solution.py:1323
  388.1 1.4 slice.197
  389.5 2.1 copy.56
  391.9 2.9 copy.57
  (211 shorter events, 35.0 us)
Async XLA Ops:
  0.8 7.1 %copy-start.26 = (bf16[128,256]{1,0:T(8,128)(2,1)S(1)}, bf16[128,256]{1,0:T(8,128)(2,1)}, u32[]{:S(2)}) copy-start(bf16[128,256]{1,0:T(8,128)(2,1)} %param.36) | copy-start | bytes 196612
  0.8 7.1 %copy-start.28 = (bf16[128,256]{1,0:T(8,128)(2,1)S(1)}, bf16[128,256]{1,0:T(8,128)(2,1)}, u32[]{:S(2)}) copy-start(bf16[128,256]{1,0:T(8,128)(2,1)} %param.34) | copy-start | bytes 196612
  0.8 7.1 %copy-start.21 = (bf16[128,684]{0,1:T(8,128)(2,1)S(1)}, bf16[128,684]{0,1:T(8,128)(2,1)}, u32[]{:S(2)}) copy-start(bf16[128,684]{0,1:T(8,128)(2,1)} %param.43) | copy-start | bytes 525316
  0.8 7.8 %copy-start.22 = (bf16[128,684]{0,1:T(8,128)(2,1)S(1)}, bf16[128,684]{0,1:T(8,128)(2,1)}, u32[]{:S(2)}) copy-start(bf16[128,684]{0,1:T(8,128)(2,1)} %param.45) | copy-start | bytes 525316
  0.8 8.5 %copy-start.23 = (bf16[684,128]{1,0:T(8,128)(2,1)S(1)}, bf16[684,128]{1,0:T(8,128)(2,1)}, u32[]{:S(2)}) copy-start(bf16[684,128]{1,0:T(8,128)(2,1)} %param.49) | copy-start | bytes 525316
  156.1 10.2 %copy-start.11 = (bf16[4,272,1024]{2,1,0:T(8,128)(2,1)S(1)}, bf16[4,272,1024]{2,1,0:T(8,128)(2,1)}, u32[]{:S(2)}) copy-start(bf16[4,272,1024]{2,1,0:T(8,128)(2,1)} %get-tuple-element.54) | copy-start | bytes 6684676
  164.0 75.6 %collective-permute-start = (bf16[1088,1024]{1,0:T(8,128)(2,1)}, bf16[1088,1024]{1,0:T(8,128)(2,1)}, u32[]{:S(2)}, u32[]{:S(2)}) collective-permute-start(bf16[1088,1024]{1,0:T(8,128)(2,1)} %convolution_convert_fusion.3), channel_id=1, source_target_pairs={{0,4},{1,5},{2,6},{3,7},{4,0},{5,1},{6,2},{7,3},{8,12},{9,13},{10,... | collective-permute-start | bytes 6684680 | tf_op jit(solution)/shard_map/ppermute | solution.py:1386
  167.4 9.0 %copy-start.10 = (bf16[1088,1024]{1,0:T(8,128)(2,1)}, bf16[1088,1024]{1,0:T(8,128)(2,1)S(1)}, u32[]{:S(2)}) copy-start(bf16[1088,1024]{1,0:T(8,128)(2,1)S(1)} %bitcast_convert_fusion) | copy-start | bytes 6684676
  176.4 8.0 %copy-start.3 = (f32[1088,1376]{1,0:T(8,128)}, f32[1088,1376]{1,0:T(8,128)S(1)}, u32[]{:S(2)}) copy-start(f32[1088,1376]{1,0:T(8,128)S(1)} %fusion.1) | copy-start | bytes 17965060
  176.4 8.6 %copy-start.41 = (bf16[1088,1376]{1,0:T(8,128)(2,1)S(1)}, bf16[1088,1376]{1,0:T(8,128)(2,1)}, u32[]{:S(2)}) copy-start(bf16[1088,1376]{1,0:T(8,128)(2,1)} %get-tuple-element.52) | copy-start | bytes 8982532
  185.0 18.9 %collective-permute-start.1 = (f32[2,1088]{1,0:T(2,128)}, f32[2,1088]{1,0:T(2,128)}, u32[]{:S(2)}, u32[]{:S(2)}) collective-permute-start(f32[2,1088]{1,0:T(2,128)} %pad_maximum_fusion.9), channel_id=1, source_target_pairs={{0,4},{1,5},{2,6},{3,7},{4,0},{5,1},{6,2},{7,3},{8,12},{9,13},{10,... | collective-permute-start | bytes 26120 | tf_op jit(solution)/shard_map/ppermute | solution.py:1386
  190.6 8.0 %copy-start.5 = (bf16[1376,1024]{1,0:T(8,128)(2,1)}, bf16[1376,1024]{1,0:T(8,128)(2,1)S(1)}, u32[]{:S(2)}) copy-start(bf16[1376,1024]{1,0:T(8,128)(2,1)S(1)} %convolution_convert_fusion.2.g_d) | copy-start | bytes 8454148
  192.1 65.2 %collective-permute-start.3 = (bf16[2,688,256]{2,1,0:T(8,128)(2,1)}, bf16[2,688,256]{2,1,0:T(8,128)(2,1)S(1)}, u32[]{:S(2)}, u32[]{:S(2)}) collective-permute-start(bf16[2,688,256]{2,1,0:T(8,128)(2,1)} %pad_maximum_fusion), channel_id=1, source_target_pairs={{0,16},{1,17},{2,18},{3,19},{4,20},{5,21},{6,22},{7,23},{8,24},{9,... | collective-permute-start | bytes 2113544 | tf_op jit(solution)/shard_map/ppermute | solution.py:685
  194.5 62.8 %collective-permute-start.4 = (bf16[2,688,256]{2,1,0:T(8,128)(2,1)}, bf16[2,688,256]{2,1,0:T(8,128)(2,1)}, u32[]{:S(2)}, u32[]{:S(2)}) collective-permute-start(bf16[2,688,256]{2,1,0:T(8,128)(2,1)} %pad_maximum_fusion.1), channel_id=1, source_target_pairs={{0,8},{1,9},{2,10},{3,11},{4,12},{5,13},{6,14},{7,15},{8,0},{9,1},... | collective-permute-start | bytes 2113544 | tf_op jit(solution)/shard_map/ppermute | solution.py:685
  204.7 11.0 %copy-start.43 = (bf16[1376,1024]{1,0:T(8,128)(2,1)S(1)}, bf16[1376,1024]{1,0:T(8,128)(2,1)}, u32[]{:S(2)}) copy-start(bf16[1376,1024]{1,0:T(8,128)(2,1)} %get-tuple-element.62) | copy-start | bytes 8454148
  223.9 20.9 %collective-permute-start.2 = (bf16[1088,1024]{1,0:T(8,128)(2,1)S(1)}, bf16[1088,1024]{1,0:T(8,128)(2,1)}, u32[]{:S(2)}, u32[]{:S(2)}) collective-permute-start(bf16[1088,1024]{1,0:T(8,128)(2,1)S(1)} %fusion.14), channel_id=1, source_target_pairs={{0,4},{1,5},{2,6},{3,7},{4,0},{5,1},{6,2},{7,3},{8,12},{9,13},{10,... | collective-permute-start | bytes 6684680 | tf_op jit(solution)/shard_map/ppermute | solution.py:1386
  232.3 8.4 %slice-start = ((s8[4456448]{0:T(1024)(128)(4,1)}), s8[4194304]{0:T(1024)(128)(4,1)S(1)}, s32[]{:S(2)}) async-start(s8[4456448]{0:T(1024)(128)(4,1)} %bitcast.116), calls=%async_computation | async-start | bytes 8388608
  232.4 24.9 %collective-permute-start.5 = (bf16[2,688,256]{2,1,0:T(8,128)(2,1)S(1)}, bf16[2,688,256]{2,1,0:T(8,128)(2,1)}, u32[]{:S(2)}, u32[]{:S(2)}) collective-permute-start(bf16[2,688,256]{2,1,0:T(8,128)(2,1)S(1)} %pad_maximum_fusion.2), channel_id=1, source_target_pairs={{0,16},{1,17},{2,18},{3,19},{4,20},{5,21},{6,22},{7,23},{8,24},{9,... | collective-permute-start | bytes 2113544 | tf_op jit(solution)/shard_map/ppermute | solution.py:685
  234.3 14.0 %slice-start.2 = ((s8[4456448]{0:T(1024)(128)(4,1)}), s8[4194304]{0:T(1024)(128)(4,1)S(1)}, s32[]{:S(2)}) async-start(s8[4456448]{0:T(1024)(128)(4,1)} %bitcast.118), calls=%async_computation.2 | async-start | bytes 8388608
  239.6 8.7 %slice-start.3 = ((s8[4456448]{0:T(1024)(128)(4,1)}), s8[262144]{0:T(1024)(128)(4,1)S(1)}, s32[]{:S(2)}) async-start(s8[4456448]{0:T(1024)(128)(4,1)} %bitcast.118), calls=%async_computation.3 | async-start | bytes 524288
  239.6 18.4 %collective-permute-start.6 = (bf16[2,688,256]{2,1,0:T(8,128)(2,1)S(1)}, bf16[2,688,256]{2,1,0:T(8,128)(2,1)}, u32[]{:S(2)}, u32[]{:S(2)}) collective-permute-start(bf16[2,688,256]{2,1,0:T(8,128)(2,1)S(1)} %pad_maximum_fusion.3), channel_id=1, source_target_pairs={{0,8},{1,9},{2,10},{3,11},{4,12},{5,13},{6,14},{7,15},{8,0},{9,1},... | collective-permute-start | bytes 2113544 | tf_op jit(solution)/shard_map/ppermute | solution.py:685
  391.6 10.5 %copy-start.1 = (s32[2,1028]{1,0:T(2,128)S(1)}, s32[2,1028]{1,0:T(2,128)}, u32[]{:S(2)}) copy-start(s32[2,1028]{1,0:T(2,128)} %param.30) | copy-start | bytes 24676
  391.9 8.8 %copy-start.24 = (f32[256,128]{1,0:T(8,128)S(1)}, f32[256,128]{1,0:T(8,128)}, u32[]{:S(2)}) copy-start(f32[256,128]{1,0:T(8,128)} %get-tuple-element.221) | copy-start | bytes 393220
  391.9 9.5 %copy-start.16 = (f32[688,128]{1,0:T(8,128)S(1)}, f32[688,128]{1,0:T(8,128)}, u32[]{:S(2)}) copy-start(f32[688,128]{1,0:T(8,128)} %get-tuple-element.80) | copy-start | bytes 1056772
  (35 other events, 162.4 us)

commit v5 on v4

--- a/solution.py
+++ b/solution.py
@@ -55,13 +55,6 @@
 
     zero = np.zeros_like(sinv)
     return [jnp.asarray(t, F32) for t in (lay(cosv, cosv), lay(-sinv, zero), lay(zero, sinv))]
-
-
-def norm_pieces(values):
-    row_mean = jnp.mean(values, axis=-1, keepdims=True)
-    var = jnp.mean(jnp.square(values - row_mean), axis=-1, keepdims=True)
-    inverse_scale = lax.rsqrt(var + EPS)
-    return ((values - row_mean) * inverse_scale, inverse_scale)
 
 
 def norm_backward(incoming_gradient, centered_normalized, inverse_scale, norm_gain):
@@ -687,7 +680,7 @@
 
 
 KEYS = 1152
-TILE = 272
+STRIP = 272
 COLS = 384
 
 
@@ -705,9 +698,9 @@
     tok_in, cot_in, pack_in, base_in, a_in, b_in, o_in, g_in, u_in, d_in,
     gain_ref, bias_ref, cos_ref, up_ref, down_ref, out_bias, gain2_ref, bias2_ref,
     tok_out, cot, pack, base, a_out, b_out, w_o, w_g, w_u, w_d, normed_out, qa_out, ka_out, va_out, mix_out,
-    mid_out, normed2_out, gate_out, up_out, hidden_out, totals,
+    mid_out, hat_out, normed2_out, gate_out, up_out, hidden_out, totals,
     tok, w_a, w_b, normed, qa_ref, ka_ref, va_ref, mix_ref, normed2, hidden, done_sem,
-    wo_v, wg_v, wu_v, part, theirs, mid_v, gate_v, up_v, act_v, own_sums, their_sums, p_send, p_recv, r_send, r_recv, out_sem, w_sem,
+    wo_v, wg_v, wu_v, part, theirs, mid_v, hat_v, gate_v, up_v, act_v, own_sums, their_sums, p_send, p_recv, r_send, r_recv, out_sem, w_sem,
     *sems,
 ):
     me = Place(*sizes)
@@ -886,6 +879,7 @@
             pltpu.make_async_copy(mid_v.at[slot], mid_out.at[t], out_sem.at[0, slot]),
             pltpu.make_async_copy(gate_v.at[slot], gate_out.at[t], out_sem.at[1, slot]),
             pltpu.make_async_copy(up_v.at[slot], up_out.at[t], out_sem.at[2, slot]),
+            pltpu.make_async_copy(hat_v.at[slot], hat_out.at[t], out_sem.at[3, slot]),
         ]
 
     leave(mix_ref, mix_out)
@@ -914,7 +908,7 @@
         slot = t % 2
         swap_sums(t).wait_recv()
         total = own_sums[t] + their_sums[t]
-        totals[t] = total
+        totals[t] = jnp.where(lane < 2, total, totals[t])
         mean = total[:, 0:1] / count
         var = total[:, 1:2] / count - mean * mean
         nhat = (act_v[slot] - mean) * lax.rsqrt(var + EPS)
@@ -933,7 +927,11 @@
         mid_v[slot] = x
         x = x - jnp.sum(x, axis=1, keepdims=True) * (1.0 / width)
         var = jnp.sum(x * x, axis=1, keepdims=True) * (1.0 / width)
-        x = (x * lax.rsqrt(var + EPS) * gain2_ref[...] + bias2_ref[...]).astype(BF16)
+        scale = lax.rsqrt(var + EPS)
+        totals[t] = jnp.broadcast_to(scale, (block, lanes))
+        x = x * scale
+        hat_v[slot] = x
+        x = (x * gain2_ref[...] + bias2_ref[...]).astype(BF16)
         normed2[t * block : (t + 1) * block, :] = x
         if t == 0:
             loads.append(load(4, wu_v))
@@ -995,6 +993,7 @@
         *[shape((heads, KEYS, lanes), BF16)] * 3,
         shape((rows, heads * HEAD), BF16),
         shape((nz, block, width), F32),
+        shape((nz, block, width), F32),
         shape((rows, width), BF16),
         shape((nz, block, 2 * ff), F32),
         shape((nz, block, 2 * ff), F32),
@@ -1006,7 +1005,7 @@
         functools.partial(front_kernel, kinds, sizes),
         out_shape=shapes,
         in_specs=[hbm] * 10 + [vmem] * 8,
-        out_specs=[hbm, hbm, vmem, vmem] + [hbm] * 16 + [vmem],
+        out_specs=[hbm, hbm, vmem, vmem] + [hbm] * 17 + [vmem],
         scratch_shapes=[
             pltpu.VMEM((nz, block, width), BF16),
             pltpu.VMEM(kinds[0].whole, BF16),
@@ -1020,10 +1019,10 @@
         ]
         + [pltpu.VMEM(k.whole, BF16) for k in kinds[2:5]]
         + [pltpu.VMEM((nz, block, width), BF16)] * 2
-        + [pltpu.VMEM((2, block, width), F32)]
+        + [pltpu.VMEM((2, block, width), F32)] * 2
         + [pltpu.VMEM((2, block, 2 * ff), F32)] * 3
         + [pltpu.VMEM((nz, block, lanes), F32)] * 2
-        + [dma((nz,)), dma((nz,)), dma((nz,)), dma((nz,)), dma((3, 2)), dma((len(kinds),))]
+        + [dma((nz,)), dma((nz,)), dma((nz,)), dma((nz,)), dma((4, 2)), dma((len(kinds),))]
         + Gather.semaphores(len(kinds), sizes)
         + Inward.semaphores(sizes)
         + Inward.semaphores(sizes)
@@ -1157,9 +1156,7 @@
         dk[h] = jnp.zeros((KEYS, lanes), F32)
         dv[h] = jnp.zeros((KEYS, lanes), F32)
 
-        @pl.loop(0, KEYS // COLS)
-        def _(t):
-            here = pl.ds(pl.multiple_of(t * COLS, COLS), COLS)
+        def some(here):
             q = qa[slot, h, here, :]
             d = da[here, :]
             p = jnp.exp2(matmul_right_t(ka[slot, h], q))
@@ -1167,6 +1164,13 @@
             dv[h] += matmul(p.astype(BF16), d)
             dk[h] += matmul(ds, q)
             dq[h, here, :] = matmul_left_t(ds, ka[slot, h])
+
+        @pl.loop(0, KEYS // COLS)
+        def _(t):
+            some(pl.ds(pl.multiple_of(t * COLS, COLS), COLS))
+
+        if KEYS % COLS:
+            some(pl.ds(KEYS - KEYS % COLS, KEYS % COLS))
 
     def put(g, part_of, row, ref, factor, turn):
         at = ((g % sub) * (pairs // sub) * 3 + (g // sub) * 3 + part_of) * lanes
@@ -1225,27 +1229,34 @@
         for t in range(nz):
             for copy in tile_loads(t):
                 copy.wait()
-            x = x_ref[t % 2].astype(F32)
-            x = x - jnp.sum(x, axis=1, keepdims=True) * (1.0 / width)
-            var = jnp.sum(x * x, axis=1, keepdims=True) * (1.0 / width)
-            scale = lax.rsqrt(var + EPS)
-            x = x * scale
             swap(t).wait_recv()
-            dn = part[t].astype(F32) + theirs[t].astype(F32)
-            dgain[...] += jnp.sum(dn * x, axis=0, keepdims=True)
-            dshift[...] += jnp.sum(dn, axis=0, keepdims=True)
-            v = dn * gain_ref[...]
-            mean = jnp.sum(v, axis=1, keepdims=True) * (1.0 / width)
-            along = jnp.sum(v * x, axis=1, keepdims=True) * (1.0 / width)
-            theirs[t] = (dmid[t % 2] + scale * (v - mean - x * along)).astype(BF16)
+
+            @pl.loop(0, block // STRIP)
+            def _(i, t=t):
+                here = pl.ds(pl.multiple_of(i * STRIP, STRIP), STRIP)
+                x = x_ref[t % 2, here, :].astype(F32)
+                x = x - jnp.sum(x, axis=1, keepdims=True) * (1.0 / width)
+                var = jnp.sum(x * x, axis=1, keepdims=True) * (1.0 / width)
+                scale = lax.rsqrt(var + EPS)
+                x = x * scale
+                dn = part[t, here, :].astype(F32) + theirs[t, here, :].astype(F32)
+                dgain[...] += dn * x
+                dshift[...] += dn
+                v = dn * gain_ref[...]
+                mean = jnp.sum(v, axis=1, keepdims=True) * (1.0 / width)
+                along = jnp.sum(v * x, axis=1, keepdims=True) * (1.0 / width)
+                theirs[t, here, :] = (dmid[t % 2, here, :] + scale * (v - mean - x * along)).astype(BF16)
+
             ins.start(t)
             if t + 2 < nz:
                 for copy in tile_loads(t + 2):
                     copy.start()
         per = width // lanes
+        whole_gain = jnp.sum(dgain[...], axis=0, keepdims=True)
+        whole_shift = jnp.sum(dshift[...], axis=0, keepdims=True)
         for i in range(per):
-            v_sum[0, i : i + 1, :] = dgain[:, i * lanes : (i + 1) * lanes]
-            v_sum[0, per + i : per + i + 1, :] = dshift[:, i * lanes : (i + 1) * lanes]
+            v_sum[0, i : i + 1, :] = whole_gain[:, i * lanes : (i + 1) * lanes]
+            v_sum[0, per + i : per + i + 1, :] = whole_shift[:, i * lanes : (i + 1) * lanes]
 
     fetch(0)
     head(0, 0)
@@ -1347,7 +1358,7 @@
             pltpu.VMEM((KEYS, lanes), BF16),
         ]
         + [pltpu.VMEM((2, KEYS, lanes), F32)] * 3
-        + [pltpu.VMEM((1, width), F32)] * 2
+        + [pltpu.VMEM((STRIP, width), F32)] * 2
         + Scatter.semaphores(n_w, sizes)
         + Sums.semaphores(sizes)
         + Outward.semaphores(sizes)
@@ -1439,16 +1450,17 @@
         sizes,
         0,
     )
-    normed, qa, ka, va, mixed, middle, normed2, gate, up, hidden, sums = kept
+    normed, qa, ka, va, mixed, middle, xhat2, normed2, gate, up, hidden, sums = kept
     full_a, full_b, full_o, full_g, full_u, full_d = full
     gain, shift, columns = (packs[:, n, :ff].reshape(-1) for n in range(4, 7))
     flag = base[0, LANES - 1].astype(F32)
     middle = middle.reshape(rows, width)
-    xhat2, s2 = norm_pieces(middle)
+    xhat2 = xhat2.reshape(rows, width)
     gate, up = gate.reshape(rows, -1), up.reshape(rows, -1)
     sig = jax.nn.sigmoid(gate)
     act = gate * sig * up
     sums = sums.reshape(rows, -1)
+    s2 = sums[:, 2:3]
     mean = sums[:, 0:1] / count_live
     var = sums[:, 1:2] / count_live - mean * mean
     r = lax.rsqrt(var + EPS)

time: 411 us -> 407 us (level)
  other arithmetic: 42.7 us -> 37.8 us
    reduce_sum x3 -> x1, other arithmetic: 9.58 us -> 3.71 us  [shards(): g_mlp_shift = jnp.sum(dnormed2, axis=0)]
    convert_element_type x0 -> x1, other arithmetic: none -> 5.67 us  [shards(): (middle + (part.astype(F32) + other(part).astype(F32)) + down_bias).astyp...]
    unnamed x118 -> x126, local copies, waits for them, and re-layouts: 14.2 us -> 13.6 us
  transfers between devices with their start and end apart: 7 -> 7, of which waited for: 1 -> 0; matrix products, arithmetic and copies ran while one was open for 21% -> 20% of each run, Pallas kernels for 0% -> 0%
where the time goes in v5:
time: 407 us; the launch traced here: 400 us
  Pallas kernels  275 us (68%)
  matrix products  44.7 us (11%)
  other arithmetic  37.8 us (9%)
  local copies, waits for them, and re-layouts  33.7 us (8%)
  starting transfers between devices  5.24 us (1%)
    pallas_call x1, Pallas kernels, front(): pl.pallas_call(functools.partial(front_kernel, kinds, sizes), out_shape=s...  144 us
    pallas_call x1, Pallas kernels, back(): pl.pallas_call(functools.partial(back_kernel, kinds, sizes, n_late, len(b...  131 us
    dot_general x4, matrix products, matmul_left_t(): lax.dot_general(left, right, (((0,), (0,)), ((), ())), preferred_element_...  19 us
    dot_general x3, matrix products, matmul(): return jnp.dot(left, right, preferred_element_type=F32)  15.4 us
    unnamed x126, local copies, waits for them, and re-layouts  13.6 us
    reduce_sum x1, other arithmetic, shards(): g_up_bias = jnp.sum(dup, axis=0)  10.9 us
  transfers between devices with their start and end apart: 7, of which 0 were waited for; matrix products, arithmetic and copies ran while one was open for 20% of the time, Pallas kernels for 0%

profile of v5, /device:TPU:0, one launch (start us, length us, event | category | flops | bytes accessed | tf_op | source)
XLA Modules:
  0.0 399.7 jit_solution(7893270570130883669)
XLA Ops:
  0.7 1.5 copy.52
  2.4 1.6 copy.53
  12.3 143.7 %front.1 = (bf16[4,272,1024]{2,1,0:T(8,128)(2,1)}, bf16[4,272,1024]{2,1,0:T(8,128)(2,1)}, f32[2,8,768]{2,1,0:T(8,128)}, bf16[1152,128]{1,0:T(8,128)(2,1)}, bf16[...) custom-call(bf16[2,272,1024]{2,1,0:T(8,128)(2,1)} %pad.52.tok_in, ...), custom_call_target="tpu_custom_call" | custom-call | tf_op jit(solution)/shard_map/front/pallas_call | solution.py:1004
  156.0 7.9 %convolution_convert_fusion.3 = bf16[1088,1024]{1,0:T(8,128)(2,1)} fusion(bf16[1088,1376]{1,0:T(8,128)(2,1)} %get-tuple-element.53, bf16[1376,1024]{1,0:T(8,128)(2,1)} %get-tuple-element.54), kind=kOutput, calls=%fused_computation.36 | convolution fusion | flops 3067150336 | bytes 8040448 | tf_op jit(solution)/shard_map/dot_general | solution.py:70
  167.2 1.8 copy-done.2
  172.0 5.7 %fusion.1 = f32[1088,1376]{1,0:T(8,128)S(1)} fusion(f32[4,272,1376]{2,1,0:T(8,128)} %get-tuple-element.60, f32[4,272,1376]{2,1,0:T(8,128)} %get-tuple-element.59, f32[1088]{0:T(1024)S(1)} %get-tuple-element.144, f32[1088]{0:T(1024)S(1)} %get-tuple-element.143), kind=kLoop, calls=%fused_computation.4 | loop fusion | flops 10479616 | bytes 17973760 | tf_op jit(solution)/shard_map/mul | solution.py:1467
  177.8 7.8 %multiply_reduce_fusion = (f32[1376]{0:T(1024)}, f32[1088]{0:T(1024)S(1)}, f32[1088]{0:T(1024)S(1)}, f32[1376]{0:T(1024)}, f32[1088,1376]{1,0:T(8,128)}) fusion(f32[1088,1376]{1,0:T(8,128)S(1)} %fusion.1, f32[1376]{0:T(1024)S(1)} %mul.150, bf16[1088,1024]{1,0:T(8,128)(2,1)S(1)} %bitcast_convert_fusion, bf16[1376,1024]{1,0:T(8,128)(2,1)S(1)} %copy-done.45, ...), kind=kOutput, calls=%fused_computation.16 | convolution fusion | flops 3078008320 | bytes 17053696 | tf_op jit(solution)/shard_map/dot_general | solution.py:1474
  186.3 5.6 %convolution_convert_fusion.2.g_d = bf16[1376,1024]{1,0:T(8,128)(2,1)S(1)} fusion(bf16[1088,1376]{1,0:T(8,128)(2,1)S(1)} %copy-done.42, bf16[1088,1024]{1,0:T(8,128)(2,1)} %copy-done.9), kind=kOutput, calls=%fused_computation.35 | convolution fusion | flops 3067445248 | bytes 8040448 | tf_op jit(solution)/shard_map/dot_general | solution.py:78
  193.2 1.5 collective-permute-start.3
  200.7 10.9 %fusion.25 = (f32[1376]{0:T(1024)S(1)}, bf16[1088,1376]{1,0:T(8,128)(2,1)S(1)}, f32[1376]{0:T(1024)S(1)}, bf16[1088,1376]{1,0:T(8,128)(2,1)S(1)}) fusion(f32[4,272,1376]{2,1,0:T(8,128)} %get-tuple-element.59, f32[1088,1376]{1,0:T(8,128)} %copy-done.3, f32[1088]{0:T(1024)S(1)} %get-tuple-element.142, f32[1088]{0:T(1024)S(1)} %get-tuple-element.141, ...), kind=kLoop, calls=%fused_computation.101 | loop fusion | flops 32933184 | bytes 29976832 | tf_op jit(solution)/shard_map/reduce_sum | solution.py:1486
  211.7 3.6 fusion.17
  215.4 3.9 fusion.13
  219.4 5.3 %convolution_convert_fusion.1.g_g = bf16[1376,1024]{1,0:T(8,128)(2,1)} fusion(bf16[1088,1024]{1,0:T(8,128)(2,1)S(1)} %copy-done.46, bf16[1088,1376]{1,0:T(8,128)(2,1)S(1)} %get-tuple-element.152), kind=kOutput, calls=%fused_computation.34 | convolution fusion | flops 3067445248 | bytes 8040448 | tf_op jit(solution)/shard_map/dot_general | solution.py:78
  225.1 1.6 dynamic-slice_bitcast_fusion.1
  228.1 5.6 %convolution_convert_fusion.g_u = bf16[1376,1024]{1,0:T(8,128)(2,1)} fusion(bf16[1088,1024]{1,0:T(8,128)(2,1)S(1)} %copy-done.47, bf16[1088,1376]{1,0:T(8,128)(2,1)S(1)} %copy-done.8), kind=kOutput, calls=%fused_computation.33 | convolution fusion | flops 3067445248 | bytes 8040448 | tf_op jit(solution)/shard_map/dot_general | solution.py:78
  234.8 5.7 %fusion.10 = bf16[1088,1024]{1,0:T(8,128)(2,1)} fusion(f32[4,272,1024]{2,1,0:T(8,128)S(1)} %bitcast.126, bf16[1088,1024]{1,0:T(8,128)(2,1)} %collective-permute-done, bf16[1088,1024]{1,0:T(8,128)(2,1)} %convolution_convert_fusion.3, f32[1024]{0:T(1024)S(1)} %copy-done.34), kind=kLoop, calls=%fused_computation.25 | loop fusion | flops 6684672 | bytes 11145216 | tf_op jit(solution)/shard_map/convert_element_type | solution.py:1469
  240.6 3.7 fusion.11
  244.3 3.3 fusion.29
  247.7 2.4 convolution_convert_fusion.4.do_in
  250.8 2.5 convolution_convert_fusion.5.g_o
  254.2 131.1 %back.1 = (bf16[2,272,1024]{2,1,0:T(8,128)(2,1)}, bf16[2,272,1024]{2,1,0:T(8,128)(2,1)}, f32[2,104,128]{2,1,0:T(8,128)}, f32[688,128]{1,0:T(8,128)}, f32[688,128...) custom-call(bf16[4,272,1024]{2,1,0:T(8,128)(2,1)} %bitcast.123, ...), custom_call_target="tpu_custom_call" | custom-call | tf_op jit(solution)/shard_map/back/pallas_call | solution.py:1334
  385.3 1.4 slice.201
  386.7 2.1 copy.57
  389.1 2.9 copy.58
  (214 shorter events, 33.0 us)
Async XLA Ops:
  0.7 7.0 %copy-start = (s32[2,1028]{1,0:T(2,128)S(1)}, s32[2,1028]{1,0:T(2,128)}, u32[]{:S(2)}) copy-start(s32[2,1028]{1,0:T(2,128)} %param.30) | copy-start | bytes 24676
  156.0 10.3 %copy-start.10 = (bf16[4,272,1024]{2,1,0:T(8,128)(2,1)S(1)}, bf16[4,272,1024]{2,1,0:T(8,128)(2,1)}, u32[]{:S(2)}) copy-start(bf16[4,272,1024]{2,1,0:T(8,128)(2,1)} %get-tuple-element.55) | copy-start | bytes 6684676
  163.9 69.8 %collective-permute-start = (bf16[1088,1024]{1,0:T(8,128)(2,1)}, bf16[1088,1024]{1,0:T(8,128)(2,1)}, u32[]{:S(2)}, u32[]{:S(2)}) collective-permute-start(bf16[1088,1024]{1,0:T(8,128)(2,1)} %convolution_convert_fusion.3), channel_id=1, source_target_pairs={{0,4},{1,5},{2,6},{3,7},{4,0},{5,1},{6,2},{7,3},{8,12},{9,13},{10,... | collective-permute-start | bytes 6684680 | tf_op jit(solution)/shard_map/ppermute | solution.py:1397
  169.1 8.6 %copy-start.9 = (bf16[1088,1024]{1,0:T(8,128)(2,1)}, bf16[1088,1024]{1,0:T(8,128)(2,1)S(1)}, u32[]{:S(2)}) copy-start(bf16[1088,1024]{1,0:T(8,128)(2,1)S(1)} %bitcast_convert_fusion) | copy-start | bytes 6684676
  171.8 5.9 %copy-start.30 = (f32[1376]{0:T(1024)}, f32[1376]{0:T(1024)S(1)}, u32[]{:S(2)}) copy-start(f32[1376]{0:T(1024)S(1)} %mul.150) | copy-start | bytes 16516
  171.9 5.8 %copy-start.31 = (f32[1376]{0:T(1024)}, f32[1376]{0:T(1024)S(1)}, u32[]{:S(2)}) copy-start(f32[1376]{0:T(1024)S(1)} %mul.147) | copy-start | bytes 16516
  172.0 5.8 %copy-start.45 = (bf16[1376,1024]{1,0:T(8,128)(2,1)S(1)}, bf16[1376,1024]{1,0:T(8,128)(2,1)}, u32[]{:S(2)}) copy-start(bf16[1376,1024]{1,0:T(8,128)(2,1)} %get-tuple-element.54) | copy-start | bytes 8454148
  177.7 7.9 %copy-start.3 = (f32[1088,1376]{1,0:T(8,128)}, f32[1088,1376]{1,0:T(8,128)S(1)}, u32[]{:S(2)}) copy-start(f32[1088,1376]{1,0:T(8,128)S(1)} %fusion.1) | copy-start | bytes 17965060
  177.8 8.5 %copy-start.42 = (bf16[1088,1376]{1,0:T(8,128)(2,1)S(1)}, bf16[1088,1376]{1,0:T(8,128)(2,1)}, u32[]{:S(2)}) copy-start(bf16[1088,1376]{1,0:T(8,128)(2,1)} %get-tuple-element.53) | copy-start | bytes 8982532
  186.2 13.7 %collective-permute-start.1 = (f32[2,1088]{1,0:T(2,128)}, f32[2,1088]{1,0:T(2,128)}, u32[]{:S(2)}, u32[]{:S(2)}) collective-permute-start(f32[2,1088]{1,0:T(2,128)} %pad_maximum_fusion.9), channel_id=1, source_target_pairs={{0,4},{1,5},{2,6},{3,7},{4,0},{5,1},{6,2},{7,3},{8,12},{9,13},{10,... | collective-permute-start | bytes 26120 | tf_op jit(solution)/shard_map/ppermute | solution.py:1397
  191.8 19.8 %copy-start.5 = (bf16[1376,1024]{1,0:T(8,128)(2,1)}, bf16[1376,1024]{1,0:T(8,128)(2,1)S(1)}, u32[]{:S(2)}) copy-start(bf16[1376,1024]{1,0:T(8,128)(2,1)S(1)} %convolution_convert_fusion.2.g_d) | copy-start | bytes 8454148
  193.2 60.1 %collective-permute-start.3 = (bf16[2,688,256]{2,1,0:T(8,128)(2,1)}, bf16[2,688,256]{2,1,0:T(8,128)(2,1)S(1)}, u32[]{:S(2)}, u32[]{:S(2)}) collective-permute-start(bf16[2,688,256]{2,1,0:T(8,128)(2,1)} %pad_maximum_fusion), channel_id=1, source_target_pairs={{0,16},{1,17},{2,18},{3,19},{4,20},{5,21},{6,22},{7,23},{8,24},{9,... | collective-permute-start | bytes 2113544 | tf_op jit(solution)/shard_map/ppermute | solution.py:678
  195.7 57.7 %collective-permute-start.4 = (bf16[2,688,256]{2,1,0:T(8,128)(2,1)}, bf16[2,688,256]{2,1,0:T(8,128)(2,1)}, u32[]{:S(2)}, u32[]{:S(2)}) collective-permute-start(bf16[2,688,256]{2,1,0:T(8,128)(2,1)} %pad_maximum_fusion.1), channel_id=1, source_target_pairs={{0,8},{1,9},{2,10},{3,11},{4,12},{5,13},{6,14},{7,15},{8,0},{9,1},... | collective-permute-start | bytes 2113544 | tf_op jit(solution)/shard_map/ppermute | solution.py:678
  200.7 11.0 %copy-start.44 = (bf16[1376,1024]{1,0:T(8,128)(2,1)S(1)}, bf16[1376,1024]{1,0:T(8,128)(2,1)}, u32[]{:S(2)}) copy-start(bf16[1376,1024]{1,0:T(8,128)(2,1)} %get-tuple-element.63) | copy-start | bytes 8454148
  219.3 21.2 %collective-permute-start.2 = (bf16[1088,1024]{1,0:T(8,128)(2,1)S(1)}, bf16[1088,1024]{1,0:T(8,128)(2,1)}, u32[]{:S(2)}, u32[]{:S(2)}) collective-permute-start(bf16[1088,1024]{1,0:T(8,128)(2,1)S(1)} %fusion.13), channel_id=1, source_target_pairs={{0,4},{1,5},{2,6},{3,7},{4,0},{5,1},{6,2},{7,3},{8,12},{9,13},{10,... | collective-permute-start | bytes 6684680 | tf_op jit(solution)/shard_map/ppermute | solution.py:1397
  226.7 26.6 %collective-permute-start.5 = (bf16[2,688,256]{2,1,0:T(8,128)(2,1)S(1)}, bf16[2,688,256]{2,1,0:T(8,128)(2,1)}, u32[]{:S(2)}, u32[]{:S(2)}) collective-permute-start(bf16[2,688,256]{2,1,0:T(8,128)(2,1)S(1)} %pad_maximum_fusion.2), channel_id=1, source_target_pairs={{0,16},{1,17},{2,18},{3,19},{4,20},{5,21},{6,22},{7,23},{8,24},{9,... | collective-permute-start | bytes 2113544 | tf_op jit(solution)/shard_map/ppermute | solution.py:678
  227.8 7.0 %slice-start.4 = ((s8[4456448]{0:T(1024)(128)(4,1)}), s8[4194304]{0:T(1024)(128)(4,1)S(1)}, s32[]{:S(2)}) async-start(s8[4456448]{0:T(1024)(128)(4,1)} %bitcast.125), calls=%async_computation.4 | async-start | bytes 8388608
  228.1 6.7 %slice-start.5 = ((s8[4456448]{0:T(1024)(128)(4,1)}), s8[262144]{0:T(1024)(128)(4,1)S(1)}, s32[]{:S(2)}) async-start(s8[4456448]{0:T(1024)(128)(4,1)} %bitcast.125), calls=%async_computation.5 | async-start | bytes 524288
  228.1 6.7 %copy-start.34 = (f32[1024]{0:T(1024)S(1)}, f32[1024]{0:T(1024)}, u32[]{:S(2)}) copy-start(f32[1024]{0:T(1024)} %param.50) | copy-start | bytes 12292
  233.7 19.6 %collective-permute-start.6 = (bf16[2,688,256]{2,1,0:T(8,128)(2,1)S(1)}, bf16[2,688,256]{2,1,0:T(8,128)(2,1)}, u32[]{:S(2)}, u32[]{:S(2)}) collective-permute-start(bf16[2,688,256]{2,1,0:T(8,128)(2,1)S(1)} %pad_maximum_fusion.3), channel_id=1, source_target_pairs={{0,8},{1,9},{2,10},{3,11},{4,12},{5,13},{6,14},{7,15},{8,0},{9,1},... | collective-permute-start | bytes 2113544 | tf_op jit(solution)/shard_map/ppermute | solution.py:678
  234.8 5.7 %slice-start = ((s8[4456448]{0:T(1024)(128)(4,1)}), s8[4194304]{0:T(1024)(128)(4,1)S(1)}, s32[]{:S(2)}) async-start(s8[4456448]{0:T(1024)(128)(4,1)} %bitcast.117), calls=%async_computation | async-start | bytes 8388608
  389.1 8.8 %copy-start.22 = (f32[256,128]{1,0:T(8,128)S(1)}, f32[256,128]{1,0:T(8,128)}, u32[]{:S(2)}) copy-start(f32[256,128]{1,0:T(8,128)} %get-tuple-element.224) | copy-start | bytes 393220
  389.1 9.5 %copy-start.14 = (f32[688,128]{1,0:T(8,128)S(1)}, f32[688,128]{1,0:T(8,128)}, u32[]{:S(2)}) copy-start(f32[688,128]{1,0:T(8,128)} %get-tuple-element.82) | copy-start | bytes 1056772
  389.1 10.2 %copy-start.1 = (s32[2,1028]{1,0:T(2,128)S(1)}, s32[2,1028]{1,0:T(2,128)}, u32[]{:S(2)}) copy-start(s32[2,1028]{1,0:T(2,128)} %param.30) | copy-start | bytes 24676
  (39 other events, 154.0 us)

commit v6 on v5

--- a/solution.py
+++ b/solution.py
@@ -1101,8 +1101,9 @@
         ]
 
     me.barrier()
-    for j in range(n_w - 2):
-        scatter.start(j, 0)
+    scatter.start(0, 0)
+    scatter.start(1, 0)
+    scatter.start(2, 0)
     for copy in loads(0):
         copy.start()
     for place in range(nz):
@@ -1248,6 +1249,8 @@
                 theirs[t, here, :] = (dmid[t % 2, here, :] + scale * (v - mean - x * along)).astype(BF16)
 
             ins.start(t)
+            if t == 1:
+                rest_of(5)
             if t + 2 < nz:
                 for copy in tile_loads(t + 2):
                     copy.start()
@@ -1258,38 +1261,39 @@
             v_sum[0, i : i + 1, :] = whole_gain[:, i * lanes : (i + 1) * lanes]
             v_sum[0, per + i : per + i + 1, :] = whole_shift[:, i * lanes : (i + 1) * lanes]
 
+    next(flows[0], None)
+    next(flows[1], None)
+    scatter.start(3, 0)
     fetch(0)
     head(0, 0)
     head(0, 1)
     write(0)
-    next(flows[0], None)
-    next(flows[1], None)
+    next(flows[2], None)
     fetch(1)
     head(1, 0)
+    rest_of(0)
     head(1, 1)
     write(1)
-    rest_of(0)
     rest_of(1)
     for copy in late:
         copy.wait()
     weight_gradient(0)
-    next(flows[2], None)
     scatter.start(4, 0)
+    next(flows[3], None)
     scatter.pass_z(0)
-    scatter.pass_z(1)
     fetch(2)
     head(2, 0)
-    next(flows[3], None)
     rest_of(2)
-    scatter.end_z(0)
+    scatter.pass_z(1)
     head(2, 1)
     write(2)
     next(flows[4], None)
-    scatter.end_z(1)
+    scatter.end_z(0)
     fetch(3)
     head(3, 0)
     rest_of(3)
     scatter.pass_z(2)
+    scatter.end_z(1)
     head(3, 1)
     write(3)
     rest_of(4)
@@ -1301,12 +1305,12 @@
     scatter.pass_z(4)
     scatter.end_z(2)
     input_gradient()
-    rest_of(5)
     small = sums.phases()
+    next(small, None)
+    scatter.pass_z(5)
     next(small, None)
     scatter.end_z(3)
     next(small, None)
-    scatter.pass_z(5)
     scatter.end_z(4)
     for _ in small:
         pass

time: 407 us -> 404 us (level)
  the two profiles are of different devices: /device:TPU:0 before, /device:TPU:25 now
where the time goes in v6:
time: 404 us; the launch traced here: 396 us
  Pallas kernels  269 us (67%)
  matrix products  44.7 us (11%)
  other arithmetic  37.8 us (9%)
  local copies, waits for them, and re-layouts  34.7 us (9%)
  starting transfers between devices  6.62 us (2%)
    pallas_call x1, Pallas kernels, front(): pl.pallas_call(functools.partial(front_kernel, kinds, sizes), out_shape=s...  140 us
    pallas_call x1, Pallas kernels, back(): pl.pallas_call(functools.partial(back_kernel, kinds, sizes, n_late, len(b...  129 us
    dot_general x4, matrix products, matmul_left_t(): lax.dot_general(left, right, (((0,), (0,)), ((), ())), preferred_element_...  19 us
    dot_general x3, matrix products, matmul(): return jnp.dot(left, right, preferred_element_type=F32)  15.4 us
    unnamed x126, local copies, waits for them, and re-layouts  14.7 us
    reduce_sum x1, other arithmetic, shards(): g_up_bias = jnp.sum(dup, axis=0)  10.9 us
  transfers between devices with their start and end apart: 7, of which 0 were waited for; matrix products, arithmetic and copies ran while one was open for 20% of the time, Pallas kernels for 0%

profile of v6, /device:TPU:25, one launch (start us, length us, event | category | flops | bytes accessed | tf_op | source)
XLA Modules:
  0.0 396.1 jit_solution(6242183973578561699)
XLA Ops:
  0.7 1.5 copy.52
  2.4 1.6 copy.53
  12.3 139.7 %front.1 = (bf16[4,272,1024]{2,1,0:T(8,128)(2,1)}, bf16[4,272,1024]{2,1,0:T(8,128)(2,1)}, f32[2,8,768]{2,1,0:T(8,128)}, bf16[1152,128]{1,0:T(8,128)(2,1)}, bf16[...) custom-call(bf16[2,272,1024]{2,1,0:T(8,128)(2,1)} %pad.52.tok_in, ...), custom_call_target="tpu_custom_call" | custom-call | tf_op jit(solution)/shard_map/front/pallas_call | solution.py:1004
  152.0 7.9 %convolution_convert_fusion.3 = bf16[1088,1024]{1,0:T(8,128)(2,1)} fusion(bf16[1088,1376]{1,0:T(8,128)(2,1)} %get-tuple-element.53, bf16[1376,1024]{1,0:T(8,128)(2,1)} %get-tuple-element.54), kind=kOutput, calls=%fused_computation.36 | convolution fusion | flops 3067150336 | bytes 8040448 | tf_op jit(solution)/shard_map/dot_general | solution.py:70
  163.3 1.8 copy-done.2
  168.0 5.7 %fusion.1 = f32[1088,1376]{1,0:T(8,128)S(1)} fusion(f32[4,272,1376]{2,1,0:T(8,128)} %get-tuple-element.60, f32[4,272,1376]{2,1,0:T(8,128)} %get-tuple-element.59, f32[1088]{0:T(1024)S(1)} %get-tuple-element.144, f32[1088]{0:T(1024)S(1)} %get-tuple-element.143), kind=kLoop, calls=%fused_computation.4 | loop fusion | flops 10479616 | bytes 17973760 | tf_op jit(solution)/shard_map/mul | solution.py:1471
  173.8 7.8 %multiply_reduce_fusion = (f32[1376]{0:T(1024)}, f32[1088]{0:T(1024)S(1)}, f32[1088]{0:T(1024)S(1)}, f32[1376]{0:T(1024)}, f32[1088,1376]{1,0:T(8,128)}) fusion(f32[1088,1376]{1,0:T(8,128)S(1)} %fusion.1, f32[1376]{0:T(1024)S(1)} %mul.150, bf16[1088,1024]{1,0:T(8,128)(2,1)S(1)} %bitcast_convert_fusion, bf16[1376,1024]{1,0:T(8,128)(2,1)S(1)} %copy-done.45, ...), kind=kOutput, calls=%fused_computation.16 | convolution fusion | flops 3078008320 | bytes 17053696 | tf_op jit(solution)/shard_map/dot_general | solution.py:1478
  182.3 5.6 %convolution_convert_fusion.2.g_d = bf16[1376,1024]{1,0:T(8,128)(2,1)S(1)} fusion(bf16[1088,1376]{1,0:T(8,128)(2,1)S(1)} %copy-done.42, bf16[1088,1024]{1,0:T(8,128)(2,1)} %copy-done.9), kind=kOutput, calls=%fused_computation.35 | convolution fusion | flops 3067445248 | bytes 8040448 | tf_op jit(solution)/shard_map/dot_general | solution.py:78
  191.3 3.8 collective-permute-start.4
  199.3 10.9 %fusion.25 = (f32[1376]{0:T(1024)S(1)}, bf16[1088,1376]{1,0:T(8,128)(2,1)S(1)}, f32[1376]{0:T(1024)S(1)}, bf16[1088,1376]{1,0:T(8,128)(2,1)S(1)}) fusion(f32[4,272,1376]{2,1,0:T(8,128)} %get-tuple-element.59, f32[1088,1376]{1,0:T(8,128)} %copy-done.3, f32[1088]{0:T(1024)S(1)} %get-tuple-element.142, f32[1088]{0:T(1024)S(1)} %get-tuple-element.141, ...), kind=kLoop, calls=%fused_computation.101 | loop fusion | flops 32933184 | bytes 29976832 | tf_op jit(solution)/shard_map/reduce_sum | solution.py:1490
  210.3 3.6 fusion.17
  213.9 3.9 fusion.13
  218.9 5.3 %convolution_convert_fusion.1.g_g = bf16[1376,1024]{1,0:T(8,128)(2,1)} fusion(bf16[1088,1024]{1,0:T(8,128)(2,1)S(1)} %copy-done.46, bf16[1088,1376]{1,0:T(8,128)(2,1)S(1)} %get-tuple-element.152), kind=kOutput, calls=%fused_computation.34 | convolution fusion | flops 3067445248 | bytes 8040448 | tf_op jit(solution)/shard_map/dot_general | solution.py:78
  224.6 1.6 dynamic-slice_bitcast_fusion.1
  227.6 5.6 %convolution_convert_fusion.g_u = bf16[1376,1024]{1,0:T(8,128)(2,1)} fusion(bf16[1088,1024]{1,0:T(8,128)(2,1)S(1)} %copy-done.47, bf16[1088,1376]{1,0:T(8,128)(2,1)S(1)} %copy-done.8), kind=kOutput, calls=%fused_computation.33 | convolution fusion | flops 3067445248 | bytes 8040448 | tf_op jit(solution)/shard_map/dot_general | solution.py:78
  233.3 5.7 %fusion.10 = bf16[1088,1024]{1,0:T(8,128)(2,1)} fusion(f32[4,272,1024]{2,1,0:T(8,128)S(1)} %bitcast.126, bf16[1088,1024]{1,0:T(8,128)(2,1)} %collective-permute-done, bf16[1088,1024]{1,0:T(8,128)(2,1)} %convolution_convert_fusion.3, f32[1024]{0:T(1024)S(1)} %copy-done.34), kind=kLoop, calls=%fused_computation.25 | loop fusion | flops 6684672 | bytes 11145216 | tf_op jit(solution)/shard_map/convert_element_type | solution.py:1473
  239.0 3.7 fusion.11
  242.8 3.3 fusion.29
  246.2 2.4 convolution_convert_fusion.4.do_in
  249.3 2.5 convolution_convert_fusion.5.g_o
  252.6 129.0 %back.1 = (bf16[2,272,1024]{2,1,0:T(8,128)(2,1)}, bf16[2,272,1024]{2,1,0:T(8,128)(2,1)}, f32[2,104,128]{2,1,0:T(8,128)}, f32[688,128]{1,0:T(8,128)}, f32[688,128...) custom-call(bf16[4,272,1024]{2,1,0:T(8,128)(2,1)} %bitcast.123, ...), custom_call_target="tpu_custom_call" | custom-call | tf_op jit(solution)/shard_map/back/pallas_call | solution.py:1338
  381.7 1.4 slice.201
  383.1 2.1 copy.57
  385.5 2.9 copy.58
  (214 shorter events, 33.1 us)
Async XLA Ops:
  0.7 7.0 %copy-start = (s32[2,1028]{1,0:T(2,128)S(1)}, s32[2,1028]{1,0:T(2,128)}, u32[]{:S(2)}) copy-start(s32[2,1028]{1,0:T(2,128)} %param.30) | copy-start | bytes 24676
  152.0 10.3 %copy-start.10 = (bf16[4,272,1024]{2,1,0:T(8,128)(2,1)S(1)}, bf16[4,272,1024]{2,1,0:T(8,128)(2,1)}, u32[]{:S(2)}) copy-start(bf16[4,272,1024]{2,1,0:T(8,128)(2,1)} %get-tuple-element.55) | copy-start | bytes 6684676
  159.9 73.3 %collective-permute-start = (bf16[1088,1024]{1,0:T(8,128)(2,1)}, bf16[1088,1024]{1,0:T(8,128)(2,1)}, u32[]{:S(2)}, u32[]{:S(2)}) collective-permute-start(bf16[1088,1024]{1,0:T(8,128)(2,1)} %convolution_convert_fusion.3), channel_id=1, source_target_pairs={{0,4},{1,5},{2,6},{3,7},{4,0},{5,1},{6,2},{7,3},{8,12},{9,13},{10,... | collective-permute-start | bytes 6684680 | tf_op jit(solution)/shard_map/ppermute | solution.py:1401
  165.1 8.6 %copy-start.9 = (bf16[1088,1024]{1,0:T(8,128)(2,1)}, bf16[1088,1024]{1,0:T(8,128)(2,1)S(1)}, u32[]{:S(2)}) copy-start(bf16[1088,1024]{1,0:T(8,128)(2,1)S(1)} %bitcast_convert_fusion) | copy-start | bytes 6684676
  167.9 5.9 %copy-start.30 = (f32[1376]{0:T(1024)}, f32[1376]{0:T(1024)S(1)}, u32[]{:S(2)}) copy-start(f32[1376]{0:T(1024)S(1)} %mul.150) | copy-start | bytes 16516
  168.0 5.8 %copy-start.31 = (f32[1376]{0:T(1024)}, f32[1376]{0:T(1024)S(1)}, u32[]{:S(2)}) copy-start(f32[1376]{0:T(1024)S(1)} %mul.147) | copy-start | bytes 16516
  168.0 5.8 %copy-start.45 = (bf16[1376,1024]{1,0:T(8,128)(2,1)S(1)}, bf16[1376,1024]{1,0:T(8,128)(2,1)}, u32[]{:S(2)}) copy-start(bf16[1376,1024]{1,0:T(8,128)(2,1)} %get-tuple-element.54) | copy-start | bytes 8454148
  173.8 7.9 %copy-start.3 = (f32[1088,1376]{1,0:T(8,128)}, f32[1088,1376]{1,0:T(8,128)S(1)}, u32[]{:S(2)}) copy-start(f32[1088,1376]{1,0:T(8,128)S(1)} %fusion.1) | copy-start | bytes 17965060
  173.8 8.5 %copy-start.42 = (bf16[1088,1376]{1,0:T(8,128)(2,1)S(1)}, bf16[1088,1376]{1,0:T(8,128)(2,1)}, u32[]{:S(2)}) copy-start(bf16[1088,1376]{1,0:T(8,128)(2,1)} %get-tuple-element.53) | copy-start | bytes 8982532
  182.3 16.2 %collective-permute-start.1 = (f32[2,1088]{1,0:T(2,128)}, f32[2,1088]{1,0:T(2,128)}, u32[]{:S(2)}, u32[]{:S(2)}) collective-permute-start(f32[2,1088]{1,0:T(2,128)} %pad_maximum_fusion.9), channel_id=1, source_target_pairs={{0,4},{1,5},{2,6},{3,7},{4,0},{5,1},{6,2},{7,3},{8,12},{9,13},{10,... | collective-permute-start | bytes 26120 | tf_op jit(solution)/shard_map/ppermute | solution.py:1401
  187.9 22.3 %copy-start.5 = (bf16[1376,1024]{1,0:T(8,128)(2,1)}, bf16[1376,1024]{1,0:T(8,128)(2,1)S(1)}, u32[]{:S(2)}) copy-start(bf16[1376,1024]{1,0:T(8,128)(2,1)S(1)} %convolution_convert_fusion.2.g_d) | copy-start | bytes 8454148
  189.3 62.5 %collective-permute-start.3 = (bf16[2,688,256]{2,1,0:T(8,128)(2,1)}, bf16[2,688,256]{2,1,0:T(8,128)(2,1)S(1)}, u32[]{:S(2)}, u32[]{:S(2)}) collective-permute-start(bf16[2,688,256]{2,1,0:T(8,128)(2,1)} %pad_maximum_fusion), channel_id=1, source_target_pairs={{0,16},{1,17},{2,18},{3,19},{4,20},{5,21},{6,22},{7,23},{8,24},{9,... | collective-permute-start | bytes 2113544 | tf_op jit(solution)/shard_map/ppermute | solution.py:678
  191.3 60.5 %collective-permute-start.4 = (bf16[2,688,256]{2,1,0:T(8,128)(2,1)}, bf16[2,688,256]{2,1,0:T(8,128)(2,1)}, u32[]{:S(2)}, u32[]{:S(2)}) collective-permute-start(bf16[2,688,256]{2,1,0:T(8,128)(2,1)} %pad_maximum_fusion.1), channel_id=1, source_target_pairs={{0,8},{1,9},{2,10},{3,11},{4,12},{5,13},{6,14},{7,15},{8,0},{9,1},... | collective-permute-start | bytes 2113544 | tf_op jit(solution)/shard_map/ppermute | solution.py:678
  199.3 11.0 %copy-start.44 = (bf16[1376,1024]{1,0:T(8,128)(2,1)S(1)}, bf16[1376,1024]{1,0:T(8,128)(2,1)}, u32[]{:S(2)}) copy-start(bf16[1376,1024]{1,0:T(8,128)(2,1)} %get-tuple-element.63) | copy-start | bytes 8454148
  217.8 21.1 %collective-permute-start.2 = (bf16[1088,1024]{1,0:T(8,128)(2,1)S(1)}, bf16[1088,1024]{1,0:T(8,128)(2,1)}, u32[]{:S(2)}, u32[]{:S(2)}) collective-permute-start(bf16[1088,1024]{1,0:T(8,128)(2,1)S(1)} %fusion.13), channel_id=1, source_target_pairs={{0,4},{1,5},{2,6},{3,7},{4,0},{5,1},{6,2},{7,3},{8,12},{9,13},{10,... | collective-permute-start | bytes 6684680 | tf_op jit(solution)/shard_map/ppermute | solution.py:1401
  226.2 25.6 %collective-permute-start.5 = (bf16[2,688,256]{2,1,0:T(8,128)(2,1)S(1)}, bf16[2,688,256]{2,1,0:T(8,128)(2,1)}, u32[]{:S(2)}, u32[]{:S(2)}) collective-permute-start(bf16[2,688,256]{2,1,0:T(8,128)(2,1)S(1)} %pad_maximum_fusion.2), channel_id=1, source_target_pairs={{0,16},{1,17},{2,18},{3,19},{4,20},{5,21},{6,22},{7,23},{8,24},{9,... | collective-permute-start | bytes 2113544 | tf_op jit(solution)/shard_map/ppermute | solution.py:678
  226.3 6.9 %slice-start.4 = ((s8[4456448]{0:T(1024)(128)(4,1)}), s8[4194304]{0:T(1024)(128)(4,1)S(1)}, s32[]{:S(2)}) async-start(s8[4456448]{0:T(1024)(128)(4,1)} %bitcast.125), calls=%async_computation.4 | async-start | bytes 8388608
  233.2 18.6 %collective-permute-start.6 = (bf16[2,688,256]{2,1,0:T(8,128)(2,1)S(1)}, bf16[2,688,256]{2,1,0:T(8,128)(2,1)}, u32[]{:S(2)}, u32[]{:S(2)}) collective-permute-start(bf16[2,688,256]{2,1,0:T(8,128)(2,1)S(1)} %pad_maximum_fusion.3), channel_id=1, source_target_pairs={{0,8},{1,9},{2,10},{3,11},{4,12},{5,13},{6,14},{7,15},{8,0},{9,1},... | collective-permute-start | bytes 2113544 | tf_op jit(solution)/shard_map/ppermute | solution.py:678
  233.2 5.7 %slice-start = ((s8[4456448]{0:T(1024)(128)(4,1)}), s8[4194304]{0:T(1024)(128)(4,1)S(1)}, s32[]{:S(2)}) async-start(s8[4456448]{0:T(1024)(128)(4,1)} %bitcast.117), calls=%async_computation | async-start | bytes 8388608
  233.3 5.7 %slice-start.1 = ((s8[4456448]{0:T(1024)(128)(4,1)}), s8[262144]{0:T(1024)(128)(4,1)S(1)}, s32[]{:S(2)}) async-start(s8[4456448]{0:T(1024)(128)(4,1)} %bitcast.117), calls=%async_computation.1 | async-start | bytes 524288
  233.3 5.7 %copy-start.28 = (f32[1024]{0:T(1024)S(1)}, f32[1024]{0:T(1024)}, u32[]{:S(2)}) copy-start(f32[1024]{0:T(1024)} %param.41) | copy-start | bytes 12292
  385.4 8.8 %copy-start.22 = (f32[256,128]{1,0:T(8,128)S(1)}, f32[256,128]{1,0:T(8,128)}, u32[]{:S(2)}) copy-start(f32[256,128]{1,0:T(8,128)} %get-tuple-element.224) | copy-start | bytes 393220
  385.5 9.5 %copy-start.14 = (f32[688,128]{1,0:T(8,128)S(1)}, f32[688,128]{1,0:T(8,128)}, u32[]{:S(2)}) copy-start(f32[688,128]{1,0:T(8,128)} %get-tuple-element.82) | copy-start | bytes 1056772
  385.5 10.2 %copy-start.1 = (s32[2,1028]{1,0:T(2,128)S(1)}, s32[2,1028]{1,0:T(2,128)}, u32[]{:S(2)}) copy-start(s32[2,1028]{1,0:T(2,128)} %param.30) | copy-start | bytes 24676
  (39 other events, 154.3 us)
